TPU v7x, 32 devices: a whole 2x2x4 slice. The times are simulated.
32 devices in a mesh: dp: 2 (over x), ep: 16 (over z, y, core).
Axes of the slice: x: 2, y: 2, z: 4, core: 2. Of those that a mesh axis runs over, the one named last changes fastest.
Arguments:
- layer_input: bfloat16 [4096, 2048], P(('dp', 'ep')), may hold values from -6 to 6
- lengths: int32 [32], P(('dp', 'ep')), may hold values from 32 to 128, as said below
- routes: int32 [4096, 4], P(('dp', 'ep')), may hold values from 0 to 7, all different within a row; in each aligned block of 128 rows (0 to 127, 128 to 255, ...) at most 128 rows name the same one
- route_weight: bfloat16 [4096, 4], P(('dp', 'ep')), may hold values from 0.19921875 to 0.796875
- cotangent: bfloat16 [4096, 2048], P(('dp', 'ep')), may hold values from -6 to 6
- norm_gain: bfloat16 [2048], P(('dp', 'ep')), may hold values from 0.5 to 1.5
- w_qkv: bfloat16 [2048, 6144], P(('dp', 'ep')), may hold values from -0.125 to 0.125
- b_qkv: bfloat16 [6144], P(('dp', 'ep')), may hold values from -3 to 3
- w_out: bfloat16 [2048, 2048], P(('dp', 'ep')), may hold values from -0.5 to 0.5
- post_gain: bfloat16 [2048], P(('dp', 'ep')), may hold values from 0.5 to 1.5
- w_gate: bfloat16 [16, 2048, 704], P('ep'), may hold values from -0.125 to 0.125
- w_up: bfloat16 [16, 2048, 704], P('ep'), may hold values from -0.125 to 0.125
- w_down: bfloat16 [16, 704, 2048], P('ep'), may hold values from -0.3125 to 0.3125
- shared_gate: bfloat16 [2048, 5632], P(None, 'ep'), may hold values from -0.125 to 0.125
- shared_up: bfloat16 [2048, 5632], P(None, 'ep'), may hold values from -0.125 to 0.125
- shared_down: bfloat16 [5632, 2048], P('ep'), may hold values from -0.078125 to 0.078125
- shared_vector: bfloat16 [2048], P(('dp', 'ep')), may hold values from -0.125 to 0.125
Outputs:
- layer_output: bfloat16 [4096, 2048], P(('dp', 'ep'))
- input_grad: bfloat16 [4096, 2048], P(('dp', 'ep'))
- norm_gain_grad: float32 [2048], P(('dp', 'ep'))
- w_qkv_grad: float32 [2048, 6144], P(('dp', 'ep'))
- b_qkv_grad: float32 [6144], P(('dp', 'ep'))
- w_out_grad: float32 [2048, 2048], P(('dp', 'ep'))
- post_gain_grad: float32 [2048], P(('dp', 'ep'))
- w_gate_grad: float32 [16, 2048, 704], P('ep')
- w_up_grad: float32 [16, 2048, 704], P('ep')
- w_down_grad: float32 [16, 704, 2048], P('ep')
- shared_gate_grad: float32 [2048, 5632], P(None, 'ep')
- shared_up_grad: float32 [2048, 5632], P(None, 'ep')
- shared_down_grad: float32 [5632, 2048], P('ep')
- shared_vector_grad: float32 [2048], P(('dp', 'ep'))
Inputs may be any that keep to these rules, and one draw needn't show every extreme that they name: `routes`: each row names 4 different experts. In the rows of one device no expert is named by more than 128 rows, a bound that some block reaches. `lengths`: some sequence uses all 128 slots.
All inputs are finite; a program needn't handle non-finite values.
Results may differ from a plain program's by a relative error of at most 0.018.
Values may be sent and summed in bfloat16 or wider, within the bound.
No kernel may reach another device: no remote copies, remote signals or barrier semaphores. Data moves between devices by JAX's collectives and lax.ppermute only.
A program may use at most 448 MiB of HBM per device.

v0:
```python
import math

import jax
import jax.numpy as jnp
from jax import lax
from jax.sharding import PartitionSpec as P

HEADS = 16
HEAD_DIM = 128
TOP = 4
HALVES = 2


epsilon = 1e-06
rope_base = 1000000.0


def norm_forward(values, gain_row):
    factor = lax.rsqrt(jnp.mean(values * values, axis=-1, keepdims=True) + epsilon)
    unit_rows = values * factor
    return (unit_rows * gain_row, unit_rows, factor)


def norm_backward(incoming, unit_rows, factor, gain_row):
    scaled = incoming * gain_row
    gain_grad = jnp.sum(incoming * unit_rows, axis=0)
    inner_mean = jnp.mean(scaled * unit_rows, axis=-1, keepdims=True)
    return (factor * (scaled - unit_rows * inner_mean), gain_grad)


def rope_tables(row_count, head_size):
    inverse = rope_base ** (-jnp.arange(0, head_size, 2, dtype=jnp.float32) / head_size)
    angles = jnp.arange(row_count, dtype=jnp.float32)[:, None] * inverse[None, :]
    angles = jnp.concatenate([angles, angles], axis=-1)
    return (jnp.cos(angles)[:, None, :], jnp.sin(angles)[:, None, :])


def turn_half(values):
    middle_index = values.shape[-1] // 2
    return jnp.concatenate([-values[..., middle_index:], values[..., :middle_index]], axis=-1)


def rotate(values, cosine_table, sine_table):
    return values * cosine_table + turn_half(values) * sine_table


def rotate_back(incoming, cosine_table, sine_table):
    return incoming * cosine_table - turn_half(incoming * sine_table)


def expert_forward(rows_in, gate_weight, up_weight, down_weight):
    gate_pre = jnp.dot(rows_in, gate_weight, preferred_element_type=jnp.float32)
    up_pre = jnp.dot(rows_in, up_weight, preferred_element_type=jnp.float32)
    middle = (jax.nn.silu(gate_pre) * up_pre).astype(jnp.bfloat16)
    result = jnp.dot(middle, down_weight, preferred_element_type=jnp.float32)
    return (result, gate_pre, up_pre, middle)


def expert_backward(
    rows_in, gate_pre, up_pre, middle, grad_out, gate_weight, up_weight, down_weight
):
    grad_mid = jnp.einsum("rd,fd->rf", grad_out, down_weight, preferred_element_type=jnp.float32)
    down_grad = jnp.einsum("rf,rd->fd", middle, grad_out, preferred_element_type=jnp.float32)
    sigmoid_gate = jax.nn.sigmoid(gate_pre)
    grad_gate = (grad_mid * up_pre * sigmoid_gate * (1.0 + gate_pre * (1.0 - sigmoid_gate))).astype(
        jnp.bfloat16
    )
    grad_up = (grad_mid * gate_pre * sigmoid_gate).astype(jnp.bfloat16)
    grad_rows = jnp.einsum("rf,df->rd", grad_gate, gate_weight, preferred_element_type=jnp.float32)
    grad_rows = grad_rows + jnp.einsum(
        "rf,df->rd", grad_up, up_weight, preferred_element_type=jnp.float32
    )
    gate_grad = jnp.einsum("rd,rf->df", rows_in, grad_gate, preferred_element_type=jnp.float32)
    up_grad = jnp.einsum("rd,rf->df", rows_in, grad_up, preferred_element_type=jnp.float32)
    return (grad_rows, gate_grad, up_grad, down_grad)


def slot_table(matched, weights, capacity):
    running = jnp.cumsum(matched, axis=1) - 1
    places = jnp.arange(capacity, dtype=jnp.int32)
    slot_hit = (running[:, None, :] == places[None, :, None]) & (matched[:, None, :] > 0)
    positions = jnp.arange(matched.shape[1], dtype=jnp.int32)
    token_index = jnp.sum(jnp.where(slot_hit, positions[None, None, :], 0), axis=2)
    slot_weight = jnp.sum(jnp.where(slot_hit, weights[:, None, :], 0.0), axis=2)
    return (token_index, slot_weight)


def local(
    layer_input,
    lengths,
    routes,
    route_weight,
    cotangent,
    norm_gain,
    w_qkv,
    b_qkv,
    w_out,
    post_gain,
    w_gate,
    w_up,
    w_down,
    shared_gate,
    shared_up,
    shared_down,
    shared_vector,
):
    row_count, feature_count = layer_input.shape
    owners = lax.axis_size("ep")
    expert_count = owners // HALVES
    capacity = min(row_count, 2 * row_count * TOP // expert_count)
    gains_in, qkv_weight, qkv_bias, out_weight, gains_post, gate_vector = (
        lax.all_gather(norm_gain, ("dp", "ep"), axis=0, tiled=True),
        lax.all_gather(w_qkv, ("dp", "ep"), axis=0, tiled=True),
        lax.all_gather(b_qkv, ("dp", "ep"), axis=0, tiled=True),
        lax.all_gather(w_out, ("dp", "ep"), axis=0, tiled=True),
        lax.all_gather(post_gain, ("dp", "ep"), axis=0, tiled=True),
        lax.all_gather(shared_vector, ("dp", "ep"), axis=0, tiled=True),
    )
    inputs = layer_input.astype(jnp.float32)
    positions = jnp.arange(row_count, dtype=jnp.int32)
    valid_rows = positions < lengths[0]
    cosine_table, sine_table = rope_tables(row_count, HEAD_DIM)
    head_shape = (row_count, HEADS, HEAD_DIM)
    normed_first, unit_first, factor_first = norm_forward(inputs, gains_in.astype(jnp.float32))
    normed_first = normed_first.astype(jnp.bfloat16)
    projected = jnp.dot(
        normed_first, qkv_weight, preferred_element_type=jnp.float32
    ) + qkv_bias.astype(jnp.float32)
    query_low = rotate(
        projected[:, :feature_count].reshape(head_shape), cosine_table, sine_table
    ).astype(jnp.bfloat16)
    key_low = rotate(
        projected[:, feature_count : 2 * feature_count].reshape(head_shape),
        cosine_table,
        sine_table,
    ).astype(jnp.bfloat16)
    value_low = projected[:, 2 * feature_count :].reshape(head_shape).astype(jnp.bfloat16)
    allowed = (positions[None, :] <= positions[:, None]) & valid_rows[None, :]
    root_size = math.sqrt(HEAD_DIM)

    def attention_scores():
        scores = (
            jnp.einsum("qhd,khd->hqk", query_low, key_low, preferred_element_type=jnp.float32)
            / root_size
        )
        return jnp.where(allowed[None], scores, -1e30)

    scores = attention_scores()
    top_score = jnp.max(scores, axis=-1, keepdims=True)
    exponent = jnp.exp(scores - top_score)
    denominator = jnp.sum(exponent, axis=-1, keepdims=True)
    log_total = top_score + jnp.log(denominator)
    probs_low = (exponent / denominator).astype(jnp.bfloat16)
    context = jnp.einsum("hqk,khd->qhd", probs_low, value_low, preferred_element_type=jnp.float32)
    context = context.reshape(row_count, feature_count).astype(jnp.bfloat16)
    attended = jnp.dot(context, out_weight, preferred_element_type=jnp.float32)
    residual = inputs + attended
    normed_second, unit_second, factor_second = norm_forward(
        residual, gains_post.astype(jnp.float32)
    )
    normed_second = normed_second.astype(jnp.bfloat16)
    gathered = lax.all_gather(normed_second, "ep", axis=0, tiled=True)
    experts_all = jnp.arange(expert_count, dtype=jnp.int32)
    route_hits = routes[None, :, :] == experts_all[:, None, None]
    matched = jnp.any(route_hits, axis=2).astype(jnp.int32)
    weights_here = jnp.sum(
        jnp.where(route_hits, route_weight.astype(jnp.float32)[None], 0.0), axis=2
    )
    token_index, slot_weight = slot_table(matched, weights_here, capacity)
    flat_index = token_index.reshape(-1)
    slot_weight = slot_weight.reshape(-1)
    outgoing = jnp.take(normed_second, flat_index, axis=0).reshape(
        expert_count, capacity, feature_count
    )
    outgoing = jnp.repeat(outgoing, HALVES, axis=0)
    received = lax.all_to_all(outgoing, "ep", split_axis=0, concat_axis=0, tiled=True)
    item_count = received.shape[1]
    flat_rows = received.reshape(-1, feature_count)
    result, gate_pre, up_pre, middle = expert_forward(flat_rows, w_gate[0], w_up[0], w_down[0])
    sent_back = result.astype(jnp.bfloat16).reshape(owners, item_count, feature_count)
    expert_gate_pre = gate_pre.reshape(owners, item_count, -1)
    expert_up_pre = up_pre.reshape(owners, item_count, -1)
    expert_mid = middle.reshape(owners, item_count, -1)
    returned = lax.all_to_all(sent_back, "ep", split_axis=0, concat_axis=0, tiled=True)
    both_parts = jnp.sum(
        returned.reshape(expert_count, HALVES, capacity, feature_count).astype(jnp.float32), axis=1
    )
    routed_here = (
        jnp.zeros((row_count, feature_count), jnp.float32)
        .at[flat_index]
        .add(slot_weight[:, None] * both_parts.reshape(-1, feature_count))
    )
    routed_terms = 0.0
    shared_out, shared_gate_pre, shared_up_pre, shared_mid = expert_forward(
        gathered, shared_gate, shared_up, shared_down
    )
    group_sigmoid = jax.nn.sigmoid(
        jnp.dot(gathered, gate_vector, preferred_element_type=jnp.float32)
    )
    mixed = lax.psum_scatter(
        routed_terms + group_sigmoid[:, None] * shared_out, "ep", scatter_dimension=0, tiled=True
    )
    own_sigmoid = jax.nn.sigmoid(
        jnp.dot(normed_second, gate_vector, preferred_element_type=jnp.float32)
    )
    combined = residual + routed_here + mixed
    output = jnp.where(valid_rows[:, None], combined, 0.0).astype(jnp.bfloat16)
    grad_rows_out = jnp.where(valid_rows[:, None], cotangent, jnp.zeros_like(cotangent))
    grad_float = grad_rows_out.astype(jnp.float32)
    group_grad = lax.all_gather(grad_rows_out, "ep", axis=0, tiled=True)
    group_float = group_grad.astype(jnp.float32)
    shared_in_grad = (group_sigmoid[:, None] * group_float).astype(jnp.bfloat16)
    sigmoid_dots = jnp.sum(group_float * shared_out, axis=1)
    group_terms, shared_gate_grad, shared_up_grad, shared_down_grad = expert_backward(
        gathered,
        shared_gate_pre,
        shared_up_pre,
        shared_mid,
        shared_in_grad,
        shared_gate,
        shared_up,
        shared_down,
    )
    outgoing_grad = (slot_weight[:, None] * jnp.take(grad_float, flat_index, axis=0)).astype(
        jnp.bfloat16
    )
    outgoing_grad = jnp.repeat(
        outgoing_grad.reshape(expert_count, capacity, feature_count), HALVES, axis=0
    )
    incoming_grad = lax.all_to_all(outgoing_grad, "ep", split_axis=0, concat_axis=0, tiled=True)
    expert_terms, expert_gate_grad, expert_up_grad, expert_down_grad = expert_backward(
        received.reshape(-1, feature_count),
        expert_gate_pre.reshape(-1, expert_gate_pre.shape[-1]),
        expert_up_pre.reshape(-1, expert_up_pre.shape[-1]),
        expert_mid.reshape(-1, expert_mid.shape[-1]),
        incoming_grad.reshape(-1, feature_count),
        w_gate[0],
        w_up[0],
        w_down[0],
    )
    back_terms = lax.all_to_all(
        expert_terms.reshape(owners, capacity, feature_count),
        "ep",
        split_axis=0,
        concat_axis=0,
        tiled=True,
    )
    back_sum = jnp.sum(back_terms.reshape(expert_count, HALVES, capacity, feature_count), axis=1)
    routed_grad = (
        jnp.zeros((row_count, feature_count), jnp.float32)
        .at[flat_index]
        .add(back_sum.reshape(-1, feature_count))
    )
    own_terms, own_dots = (
        lax.psum_scatter(group_terms, "ep", scatter_dimension=0, tiled=True),
        lax.psum_scatter(sigmoid_dots, "ep", scatter_dimension=0, tiled=True),
    )
    logit_grad = own_dots * own_sigmoid * (1.0 - own_sigmoid)
    vector_grad = jnp.einsum("t,td->d", logit_grad, normed_second.astype(jnp.float32))
    second_grad = own_terms + routed_grad + logit_grad[:, None] * gate_vector.astype(jnp.float32)
    residual_part, post_gain_grad = norm_backward(
        second_grad, unit_second, factor_second, gains_post.astype(jnp.float32)
    )
    residual_grad = grad_float + residual_part
    attended_grad = residual_grad.astype(jnp.bfloat16)
    out_weight_grad = jnp.einsum(
        "td,te->de", context, attended_grad, preferred_element_type=jnp.float32
    )
    context_grad = jnp.einsum(
        "te,de->td", attended_grad, out_weight, preferred_element_type=jnp.float32
    )
    context_grad = context_grad.astype(jnp.bfloat16).reshape(head_shape)
    probs_grad = jnp.einsum(
        "qhd,khd->hqk", context_grad, value_low, preferred_element_type=jnp.float32
    )
    value_grad = jnp.einsum(
        "hqk,qhd->khd", probs_low, context_grad, preferred_element_type=jnp.float32
    )
    probabilities = jnp.exp(attention_scores() - log_total)
    score_grad = probabilities * (
        probs_grad - jnp.sum(probabilities * probs_grad, axis=-1, keepdims=True)
    )
    score_grad = score_grad.astype(jnp.bfloat16)
    query_grad = (
        jnp.einsum("hqk,khd->qhd", score_grad, key_low, preferred_element_type=jnp.float32)
        / root_size
    )
    key_grad = (
        jnp.einsum("hqk,qhd->khd", score_grad, query_low, preferred_element_type=jnp.float32)
        / root_size
    )
    projected_grad = jnp.concatenate(
        [
            rotate_back(query_grad, cosine_table, sine_table).reshape(row_count, feature_count),
            rotate_back(key_grad, cosine_table, sine_table).reshape(row_count, feature_count),
            value_grad.reshape(row_count, feature_count),
        ],
        axis=1,
    ).astype(jnp.bfloat16)
    qkv_weight_grad = jnp.einsum(
        "td,te->de", normed_first, projected_grad, preferred_element_type=jnp.float32
    )
    qkv_bias_grad = jnp.sum(projected_grad.astype(jnp.float32), axis=0)
    first_grad = jnp.einsum(
        "te,de->td", projected_grad, qkv_weight, preferred_element_type=jnp.float32
    )
    input_part, norm_gain_grad = norm_backward(
        first_grad, unit_first, factor_first, gains_in.astype(jnp.float32)
    )
    layer_grad = (residual_grad + input_part).astype(jnp.bfloat16)
    dense = (
        lax.psum_scatter(norm_gain_grad, ("dp", "ep"), scatter_dimension=0, tiled=True),
        lax.psum_scatter(qkv_weight_grad, ("dp", "ep"), scatter_dimension=0, tiled=True),
        lax.psum_scatter(qkv_bias_grad, ("dp", "ep"), scatter_dimension=0, tiled=True),
        lax.psum_scatter(out_weight_grad, ("dp", "ep"), scatter_dimension=0, tiled=True),
        lax.psum_scatter(post_gain_grad, ("dp", "ep"), scatter_dimension=0, tiled=True),
        lax.psum_scatter(vector_grad, ("dp", "ep"), scatter_dimension=0, tiled=True),
    )
    summed = lax.psum(
        (
            expert_gate_grad,
            expert_up_grad,
            expert_down_grad,
            shared_gate_grad,
            shared_up_grad,
            shared_down_grad,
        ),
        "dp",
    )
    return (
        output,
        layer_grad,
        dense[0],
        dense[1],
        dense[2],
        dense[3],
        dense[4],
        summed[0][None],
        summed[1][None],
        summed[2][None],
        summed[3],
        summed[4],
        summed[5],
        dense[5],
    )


def solution(mesh):
    return jax.shard_map(
        local,
        mesh=mesh,
        in_specs=(
            P(("dp", "ep"), None),
            P(("dp", "ep")),
            P(("dp", "ep"), None),
            P(("dp", "ep"), None),
            P(("dp", "ep"), None),
            P(("dp", "ep")),
            P(("dp", "ep"), None),
            P(("dp", "ep")),
            P(("dp", "ep"), None),
            P(("dp", "ep")),
            P("ep", None, None),
            P("ep", None, None),
            P("ep", None, None),
            P(None, "ep"),
            P(None, "ep"),
            P("ep", None),
            P(("dp", "ep")),
        ),
        out_specs=(
            P(("dp", "ep"), None),
            P(("dp", "ep"), None),
            P(("dp", "ep")),
            P(("dp", "ep"), None),
            P(("dp", "ep")),
            P(("dp", "ep"), None),
            P(("dp", "ep")),
            P("ep", None, None),
            P("ep", None, None),
            P("ep", None, None),
            P(None, "ep"),
            P(None, "ep"),
            P("ep", None),
            P(("dp", "ep")),
        ),
        check_vma=False,
    )
```

profile of v0, /device:TPU:0, one launch (start us, length us, event | category | flops | bytes accessed | tf_op | source)
XLA Modules:
  0.0 2404.6 jit_solution(10963253739894868231)
XLA Ops:
  12.8 43.6 %all-reduce.11 = (bf16[6144]{0:T(1024)(128)(2,1)S(1)}, bf16[2048]{0:T(1024)(128)(2,1)S(1)}, bf16[2048]{0:T(1024)(128)(2,1)S(1)}, bf16[2048]{0:T(1024)(128)(2,1)S(1)}) all-reduce(bf16[6144]{0:T(1024)(128)(2,1)S(1)} %dynamic-update-slice.1, bf16[2048]{0:T(1024)(128)(2,1)S(1)} %dynamic-update-slice, ...), channel_id=1, replica_groups=mesh['dp'=2,'ep'=16] {'dp','ep'}, use_global_device_ids=true, to_apply=%add.1 | all-reduce | flops 12288 | bytes 49152
  58.8 111.2 %all-gather.5.cloned.1.call-done = bf16[2048,6144]{1,0:T(8,128)(2,1)} async-done(((bf16[64,6144]{1,0:T(8,128)(2,1)}), bf16[2048,6144]{1,0:T(8,128)(2,1)}) %all-gather.5.cloned.1.call-update) | async-done | bytes 25165840 | tf_op jit(solution)/shard_map/all_gather | solution.py:113
  196.3 52.4 %all-gather.7.cloned.1.call-done = bf16[2048,2048]{1,0:T(8,128)(2,1)} async-done(((bf16[64,2048]{1,0:T(8,128)(2,1)}), bf16[2048,2048]{1,0:T(8,128)(2,1)}) %all-gather.7.cloned.1.call-update) | async-done | bytes 8388624 | tf_op jit(solution)/shard_map/all_gather | solution.py:115
  258.2 70.9 %all-gather.9.cloned.1.call-done = bf16[2048,2048]{1,0:T(8,128)(2,1)} async-done(((bf16[128,2048]{1,0:T(8,128)(2,1)}), bf16[2048,2048]{1,0:T(8,128)(2,1)}) %all-gather.9.cloned.1.call-update) | async-done | bytes 8388624 | tf_op jit(solution)/shard_map/all_gather | solution.py:162
  344.8 60.1 %all-gather.11.cloned.1.call-done = bf16[2048,2048]{1,0:T(8,128)(2,1)} async-done(((bf16[128,2048]{1,0:T(8,128)(2,1)}), bf16[2048,2048]{1,0:T(8,128)(2,1)}) %all-gather.11.cloned.1.call-update) | async-done | bytes 8388624 | tf_op jit(solution)/shard_map/all_gather | solution.py:210
  422.9 11.5 convolution_add_fusion
  477.8 201.9 %all-to-all-done = bf16[16,128,2048]{2,1,0:T(8,128)(2,1)} async-done(((bf16[16,128,2048]{2,1,0:T(8,128)(2,1)}), bf16[16,128,2048]{2,1,0:T(8,128)(2,1)}, u32[]{:S(2)}, u32[]{:S(2)}) %all-to-all-start) | async-done | bytes 8388640 | tf_op jit(solution)/shard_map/all_to_all | solution.py:176
  686.5 37.2 %all-to-all-start.2 = ((bf16[16,128,2048]{2,1,0:T(8,128)(2,1)}), bf16[16,128,2048]{2,1,0:T(8,128)(2,1)}, u32[]{:S(2)}, u32[]{:S(2)}) async-start(bf16[16,128,2048]{2,1,0:T(8,128)(2,1)} %bitcast.148), calls=%async_computation.4 | async-start | bytes 16777216 | tf_op jit(solution)/shard_map/all_to_all | solution.py:230
  723.9 16.1 fusion.1
  740.0 11.3 fusion.10
  761.5 188.8 %all-to-all-done.2 = bf16[16,128,2048]{2,1,0:T(8,128)(2,1)} async-done(((bf16[16,128,2048]{2,1,0:T(8,128)(2,1)}), bf16[16,128,2048]{2,1,0:T(8,128)(2,1)}, u32[]{:S(2)}, u32[]{:S(2)}) %all-to-all-start.2) | async-done | bytes 8388640 | tf_op jit(solution)/shard_map/all_to_all | solution.py:230
  950.3 14.8 multiply_convert_fusion.1
  975.6 13.7 convolution_add_fusion.2
  989.3 48.4 %all-to-all-start.3 = ((f32[16,128,2048]{2,1,0:T(8,128)}), f32[16,128,2048]{2,1,0:T(8,128)}, u32[]{:S(2)}, u32[]{:S(2)}) async-start(f32[16,128,2048]{2,1,0:T(8,128)} %bitcast.151), calls=%async_computation.5 | async-start | bytes 33554432 | tf_op jit(solution)/shard_map/all_to_all | solution.py:241
  1092.8 297.0 %all-reduce.4 = f32[2048]{0:T(1024)S(1)} all-reduce(f32[2048]{0:T(1024)S(1)} %copy-done.50), channel_id=4, replica_groups=mesh['dp'=2,'ep'=16] {'ep'}, use_global_device_ids=true, to_apply=%region_14.15.clone | all-reduce | flops 2048 | bytes 16384
  1403.4 17.1 scatter_fusion.1
  1452.6 22.8 fusion.50
  1486.3 53.3 %all-to-all-start.1 = ((bf16[16,128,2048]{2,1,0:T(8,128)(2,1)}), bf16[16,128,2048]{2,1,0:T(8,128)(2,1)}, u32[]{:S(2)}, u32[]{:S(2)}) async-start(bf16[16,128,2048]{2,1,0:T(8,128)(2,1)} %bitcast.158), calls=%async_computation.2 | async-start | bytes 16777216 | tf_op jit(solution)/shard_map/all_to_all | solution.py:184
  1539.8 150.5 %all-to-all-done.1 = bf16[16,128,2048]{2,1,0:T(8,128)(2,1)} async-done(((bf16[16,128,2048]{2,1,0:T(8,128)(2,1)}), bf16[16,128,2048]{2,1,0:T(8,128)(2,1)}, u32[]{:S(2)}, u32[]{:S(2)}) %all-to-all-start.1) | async-done | bytes 8388640 | tf_op jit(solution)/shard_map/all_to_all | solution.py:184
  1708.1 14.7 fusion.31
  1722.8 80.6 %all-reduce.9 = (f32[2048]{0:T(1024)S(1)}, f32[6144]{0:T(1024)S(1)}, f32[2048]{0:T(1024)S(1)}, f32[2048]{0:T(1024)S(1)}) all-reduce(f32[2048]{0:T(1024)S(1)} %get-tuple-element.16, f32[6144]{0:T(1024)S(1)} %convert_reduce_fusion.1, f32[2048]{0:T(1024)S(1)} %get-tuple-element.14, ...), channel_id=5, replica_groups=mesh['dp'=2,'ep'=16] {'dp','ep'}, use_global_device_ids=true, to_apply=%region_21.22.clone | all-reduce | flops 12288 | bytes 98304
  1805.1 16.9 scatter_fusion
  1827.5 109.0 %reduce-scatter.11.cloned.1.call-done = f32[64,2048]{1,0:T(8,128)} async-done(((f32[2048,2048]{1,0:T(8,128)}), f32[64,2048]{1,0:T(8,128)}) %reduce-scatter.11.cloned.1.call-update) | async-done | bytes 524304 | tf_op jit(solution)/shard_map/reduce_scatter | solution.py:315
  1936.5 440.2 %reduce-scatter.9.cloned.1.call-done = f32[64,6144]{1,0:T(8,128)} async-done(((f32[2048,6144]{1,0:T(8,128)}), f32[64,6144]{1,0:T(8,128)}) %reduce-scatter.9.cloned.1.call-update) | async-done | bytes 1572880 | tf_op jit(solution)/shard_map/reduce_scatter | solution.py:313
  (274 shorter events, 304.7 us)
Async XLA Ops:
  7.2 943.1 %copy-start = (bf16[1,704,2048]{2,1,0:T(8,128)(2,1)S(1)}, bf16[1,704,2048]{2,1,0:T(8,128)(2,1)}, u32[]{:S(2)}) copy-start(bf16[1,704,2048]{2,1,0:T(8,128)(2,1)} %param.29) | copy-start | bytes 8650756
  7.2 162.8 %all-gather.5.cloned.1.call-start = ((), (), s32[]{:S(2)}) async-start(), calls=%async_computation.8 | async-start | bytes 25952256 | tf_op jit(solution)/shard_map/all_gather | solution.py:113
  7.9 240.7 %all-gather.7.cloned.1.call-start = ((), (), s32[]{:S(2)}) async-start(), calls=%async_computation.9 | async-start | bytes 8650752 | tf_op jit(solution)/shard_map/all_gather | solution.py:115
  8.7 320.5 %all-gather.9.cloned.1.call-start = ((), (), s32[]{:S(2)}) async-start(), calls=%async_computation.10 | async-start | bytes 8912896 | tf_op jit(solution)/shard_map/all_gather | solution.py:162
  56.4 201.8 %copy-start.53 = (bf16[2048]{0:T(1024)(128)(2,1)}, bf16[2048]{0:T(1024)(128)(2,1)S(1)}, u32[]{:S(2)}) copy-start(bf16[2048]{0:T(1024)(128)(2,1)S(1)} %get-tuple-element.31) | copy-start | bytes 12292
  56.4 123.8 %copy-start.34 = (f32[2048]{0:T(1024)}, f32[2048]{0:T(1024)S(1)}, u32[]{:S(2)}) copy-start(f32[2048]{0:T(1024)S(1)} %convert_element_type.120) | copy-start | bytes 24580
  56.4 197.2 %copy-start.38 = (f32[2048]{0:T(1024)}, f32[2048]{0:T(1024)S(1)}, u32[]{:S(2)}) copy-start(f32[2048]{0:T(1024)S(1)} %convert_element_type.130) | copy-start | bytes 24580
  56.5 199.1 %copy-start.56 = (pred[128]{0:T(512)(128)(4,1)}, pred[128]{0:T(512)(128)(4,1)S(1)}, u32[]{:S(2)}) copy-start(pred[128]{0:T(512)(128)(4,1)S(1)} %iota_compare_fusion.3) | copy-start | bytes 388
  58.7 121.5 %copy-start.51 = (f32[128]{0:T(128)}, f32[128]{0:T(128)S(1)}, u32[]{:S(2)}) copy-start(f32[128]{0:T(128)S(1)} %add_rsqrt_fusion.1) | copy-start | bytes 1540
  192.3 56.3 %copy-start.7 = (bf16[128,2048]{1,0:T(8,128)(2,1)S(1)}, bf16[128,2048]{1,0:T(8,128)(2,1)}, u32[]{:S(2)}) copy-start(bf16[128,2048]{1,0:T(8,128)(2,1)} %param.17) | copy-start | bytes 1572868
  255.5 149.4 %all-gather.11.cloned.1.call-start = ((), (), s32[]{:S(2)}) async-start(), calls=%async_computation.12 | async-start | bytes 8912896 | tf_op jit(solution)/shard_map/all_gather | solution.py:210
  258.0 1132.1 %reduce-scatter.7.cloned.1.call-start = ((), (), s32[]{:S(2)}) async-start(), calls=%async_computation.13 | async-start | bytes 17825792 | tf_op jit(solution)/shard_map/reduce_scatter | solution.py:255
  258.2 76.7 %copy-start.42 = (bf16[2048,1]{0,1:T(2,128)(2,1)}, bf16[2048,1]{0,1:T(2,128)(2,1)S(1)}, u32[]{:S(2)}) copy-start(bf16[2048,1]{0,1:T(2,128)(2,1)S(1)} %reshape.333) | copy-start | bytes 12292
  456.7 223.0 %all-to-all-start = ((bf16[16,128,2048]{2,1,0:T(8,128)(2,1)}), bf16[16,128,2048]{2,1,0:T(8,128)(2,1)}, u32[]{:S(2)}, u32[]{:S(2)}) async-start(bf16[16,128,2048]{2,1,0:T(8,128)(2,1)} %bitcast.149), calls=%async_computation.1 | async-start | bytes 16777216 | tf_op jit(solution)/shard_map/all_to_all | solution.py:176
  686.5 263.8 %all-to-all-start.2 = ((bf16[16,128,2048]{2,1,0:T(8,128)(2,1)}), bf16[16,128,2048]{2,1,0:T(8,128)(2,1)}, u32[]{:S(2)}, u32[]{:S(2)}) async-start(bf16[16,128,2048]{2,1,0:T(8,128)(2,1)} %bitcast.148), calls=%async_computation.4 | async-start | bytes 16777216 | tf_op jit(solution)/shard_map/all_to_all | solution.py:230
  723.7 698.8 %reduce-scatter.5.cloned.1.call-start = ((), (), s32[]{:S(2)}) async-start(), calls=%async_computation.11 | async-start | bytes 17825792 | tf_op jit(solution)/shard_map/reduce_scatter | solution.py:200
  989.3 403.2 %all-to-all-start.3 = ((f32[16,128,2048]{2,1,0:T(8,128)}), f32[16,128,2048]{2,1,0:T(8,128)}, u32[]{:S(2)}, u32[]{:S(2)}) async-start(f32[16,128,2048]{2,1,0:T(8,128)} %bitcast.151), calls=%async_computation.5 | async-start | bytes 33554432 | tf_op jit(solution)/shard_map/all_to_all | solution.py:241
  1037.7 789.8 %all-reduce.14.cloned.1.call-start = ((), (), s32[]{:S(2)}) async-start(), calls=%async_computation.16 | async-start | bytes 51904512 | tf_op jit(solution)/shard_map/psum | solution.py:319
  1090.9 298.9 %copy-start.2 = (bf16[128,2048]{1,0:T(8,128)(2,1)S(1)}, bf16[128,2048]{1,0:T(8,128)(2,1)}, u32[]{:S(2)}) copy-start(bf16[128,2048]{1,0:T(8,128)(2,1)} %multiply_convert_fusion.8) | copy-start | bytes 1572868
  1090.9 298.9 %copy-start.43 = (bf16[2048,1]{0,1:T(2,128)(2,1)S(1)}, bf16[2048,1]{0,1:T(2,128)(2,1)}, u32[]{:S(2)}) copy-start(bf16[2048,1]{0,1:T(2,128)(2,1)} %copy-done.42) | copy-start | bytes 12292
  1091.0 845.6 %reduce-scatter.11.cloned.1.call-start = ((), (), s32[]{:S(2)}) async-start(), calls=%async_computation.15 | async-start | bytes 17301504 | tf_op jit(solution)/shard_map/reduce_scatter | solution.py:315
  1434.9 941.8 %reduce-scatter.9.cloned.1.call-start = ((), (), s32[]{:S(2)}) async-start(), calls=%async_computation.14 | async-start | bytes 51904512 | tf_op jit(solution)/shard_map/reduce_scatter | solution.py:313
  1486.3 204.0 %all-to-all-start.1 = ((bf16[16,128,2048]{2,1,0:T(8,128)(2,1)}), bf16[16,128,2048]{2,1,0:T(8,128)(2,1)}, u32[]{:S(2)}, u32[]{:S(2)}) async-start(bf16[16,128,2048]{2,1,0:T(8,128)(2,1)} %bitcast.158), calls=%async_computation.2 | async-start | bytes 16777216 | tf_op jit(solution)/shard_map/all_to_all | solution.py:184
  1539.8 160.3 %copy-start.47 = (f32[8,128]{1,0:T(8,128)S(1)}, f32[8,128]{1,0:T(8,128)}, u32[]{:S(2)}) copy-start(f32[8,128]{1,0:T(8,128)} %copy-done.46) | copy-start | bytes 12292
  (63 other events, 342.1 us)
Sparse Core Ops, SparseCore 0:
  10.9 158.9 all-gather.4
  172.8 75.7 all-gather.6
  255.6 73.4 all-gather.8
  331.7 73.1 all-gather.10
  434.6 369.8 reduce-scatter.6
  808.4 355.8 reduce-scatter.4
  1168.3 578.0 all-reduce.13
  1749.3 187.1 reduce-scatter.10
  1943.5 433.1 reduce-scatter.8
where the time goes:
time: 2410 us; the launch traced here: 2400 us
  waiting for transfers between devices  1390 us (58%)
  blocking collectives  421 us (17%)
  matrix products  261 us (11%)
  starting transfers between devices  145 us (6%)
  other arithmetic  96.7 us (4%)
  local copies, waits for them, and re-layouts  78.1 us (3%)
    reduce_scatter x1, waiting for transfers between devices, local(): lax.psum_scatter(qkv_weight_grad, ('dp', 'ep'), scatter_dimension=0, tile...  440 us
    unnamed x3, blocking collectives  421 us
    all_to_all x1, waiting for transfers between devices, local(): lax.all_to_all(outgoing, 'ep', split_axis=0, concat_axis=0, tiled=True)  202 us
    all_to_all x1, waiting for transfers between devices, local(): lax.all_to_all(outgoing_grad, 'ep', split_axis=0, concat_axis=0, tiled=True)  189 us
    all_to_all x1, waiting for transfers between devices, local(): lax.all_to_all(sent_back, 'ep', split_axis=0, concat_axis=0, tiled=True)  150 us
    all_gather x1, waiting for transfers between devices, local(): lax.all_gather(w_qkv, ('dp', 'ep'), axis=0, tiled=True)  111 us
    reduce_scatter x1, waiting for transfers between devices, local(): lax.psum_scatter(out_weight_grad, ('dp', 'ep'), scatter_dimension=0, tile...  109 us
    all_gather x1, waiting for transfers between devices, local(): gathered = lax.all_gather(normed_second, 'ep', axis=0, tiled=True)  70.9 us
  transfers between devices with their start and end apart: 13, of which 9 were waited for; matrix products, arithmetic and copies ran while one was open for 15% of the time, Pallas kernels for 0%

commit v1 on v0

v1 whole, which is shorter than its diff:
```python
import math

import jax
import jax.numpy as jnp
from jax import lax
from jax.sharding import PartitionSpec as P

HEADS = 16
HEAD_DIM = 128
TOP = 4
HALVES = 2
CORES = 2
LINE = 4


epsilon = 1e-06
rope_base = 1000000.0
bf16 = jnp.bfloat16
f32 = jnp.float32


def unit_norm(values):
    factor = lax.rsqrt(jnp.mean(values * values, axis=-1, keepdims=True) + epsilon)
    return (values * factor, factor)


def norm_backward(incoming, unit_rows, factor, gain_row):
    scaled = incoming * gain_row
    inner_mean = jnp.mean(scaled * unit_rows, axis=-1, keepdims=True)
    return factor * (scaled - unit_rows * inner_mean)


def rope_tables(row_count, head_size):
    inverse = rope_base ** (-jnp.arange(0, head_size, 2, dtype=f32) / head_size)
    angles = jnp.arange(row_count, dtype=f32)[:, None] * inverse[None, :]
    angles = jnp.concatenate([angles, angles], axis=-1)
    return (jnp.cos(angles)[:, None, :], jnp.sin(angles)[:, None, :])


def turn_half(values):
    middle_index = values.shape[-1] // 2
    return jnp.concatenate([-values[..., middle_index:], values[..., :middle_index]], axis=-1)


def rotate(values, cosine_table, sine_table):
    return values * cosine_table + turn_half(values) * sine_table


def rotate_back(incoming, cosine_table, sine_table):
    return incoming * cosine_table - turn_half(incoming * sine_table)


def dot(left, right, dims):
    return lax.dot_general(left, right, (dims, ((), ())), preferred_element_type=f32)


class Grid:
    def __init__(self):
        self.groups = lax.axis_size("dp")
        self.owners = lax.axis_size("ep")
        self.chips = self.owners // CORES
        self.na = math.gcd(LINE, self.chips)
        self.nb = self.chips // self.na
        self.group = lax.axis_index("dp")
        me = lax.axis_index("ep")
        self.chip = me // CORES
        self.core = me % CORES
        self.a = self.chip // self.nb
        self.b = self.chip % self.nb

    def place(self, a, b, c):
        return ((a % self.na) * self.nb + b % self.nb) * CORES + c % CORES

    def hop(self, values, da=0, db=0, dc=0):
        pairs = [
            (self.place(a, b, c), self.place(a + da, b + db, c + dc))
            for a in range(self.na)
            for b in range(self.nb)
            for c in range(CORES)
        ]
        return lax.ppermute(values, "ep", pairs)

    def cross(self, values, shift):
        pairs = [(g, (g + shift) % self.groups) for g in range(self.groups)]
        return lax.ppermute(values, "dp", pairs)

    def plane(self, block):
        slots = []
        for da in range(self.na):
            along = self.hop(block, da=-da) if da else block
            rows = [along]
            for db in range(1, self.nb):
                rows.append(self.hop(along, db=-db))
            slots.append(jnp.concatenate(rows, axis=0))
        return slots

    def both(self, slots):
        return [jnp.concatenate([rows, self.hop(rows, dc=1)], axis=0) for rows in slots]

    def plane_sum(self, slots):
        total = None
        for da in list(range(1, self.na)) + [0]:
            terms = slots[da]
            here = terms[0].astype(f32)
            for db in range(1, self.nb):
                here = here + self.hop(terms[db], db=db).astype(f32)
            if da:
                here = self.hop(here.astype(bf16), da=da).astype(f32)
            total = here if total is None else total + here
        return total

    def pair_sum(self, terms):
        return (terms[0].astype(f32) + self.hop(terms[1], dc=1).astype(f32)).astype(bf16)

    def absolute(self, relative):
        turned = jnp.roll(relative, self.a, axis=0)
        return jnp.roll(turned, self.b, axis=1)

    def relative(self, by_place):
        turned = jnp.roll(by_place, -self.a, axis=0)
        return jnp.roll(turned, -self.b, axis=1)

    def same_core(self):
        return [[k * CORES + c for k in range(self.chips)] for c in range(CORES)]

    def swap(self, blocks):
        return lax.all_to_all(
            blocks,
            "ep",
            split_axis=0,
            concat_axis=0,
            tiled=True,
            axis_index_groups=self.same_core(),
        )

    def scatter_core(self, terms, axis):
        mine = lax.dynamic_index_in_dim(terms, self.core, axis, keepdims=False)
        other = lax.dynamic_index_in_dim(terms, 1 - self.core, axis, keepdims=False)
        return mine.astype(f32) + self.hop(other, dc=1).astype(f32)

    def scatter_groups(self, terms):
        total = lax.dynamic_index_in_dim(terms, self.group, 0, keepdims=False).astype(f32)
        for shift in range(1, self.groups):
            there = (self.group + shift) % self.groups
            piece = lax.dynamic_index_in_dim(terms, there, 0, keepdims=False)
            total = total + self.cross(piece, shift).astype(f32)
        return total

    def scatter_rows(self, terms):
        total = lax.dynamic_index_in_dim(terms, self.b, 1, keepdims=False).astype(f32)
        for db in range(1, self.nb):
            there = (self.b + db) % self.nb
            piece = lax.dynamic_index_in_dim(terms, there, 1, keepdims=False)
            total = total + self.hop(piece, db=db).astype(f32)
        terms = total.astype(terms.dtype)
        total = lax.dynamic_index_in_dim(terms, self.a, 0, keepdims=False).astype(f32)
        for da in range(1, self.na):
            there = (self.a + da) % self.na
            piece = lax.dynamic_index_in_dim(terms, there, 0, keepdims=False)
            total = total + self.hop(piece, da=da).astype(f32)
        return total

    def everywhere(self, small):
        parts = [small] + [self.cross(small, -shift) for shift in range(1, self.groups)]
        level = jnp.stack(parts)
        parts = [level] + [self.hop(level, db=-db) for db in range(1, self.nb)]
        level = jnp.stack(parts, axis=1)
        parts = [level] + [self.hop(level, da=-da) for da in range(1, self.na)]
        level = jnp.stack(parts, axis=1)
        return jnp.stack([level, self.hop(level, dc=1)], axis=3)


def expert_rows(rows, grads, scale_routed, scale_shared, into, out_weights, routed_units):
    units = into.shape[1] // 2
    pre = dot(rows, into, ((1,), (0,)))
    gate_pre, up_pre = pre[:, :units], pre[:, units:]
    back = dot(grads, out_weights, ((1,), (1,)))
    is_routed = lax.broadcasted_iota(jnp.int32, (1, units), 1) < routed_units
    scale = jnp.where(is_routed, scale_routed[:, None], scale_shared[:, None])
    gate_sigmoid = jax.nn.sigmoid(gate_pre)
    silu = gate_pre * gate_sigmoid
    middle = silu * up_pre
    inner = jnp.sum(jnp.where(is_routed, 0.0, middle * back), axis=1)
    scaled_middle = (scale * middle).astype(bf16)
    back = scale * back
    grad_gate = (back * up_pre * gate_sigmoid * (1.0 + gate_pre * (1.0 - gate_sigmoid))).astype(
        bf16
    )
    grad_up = (back * silu).astype(bf16)
    return scaled_middle, jnp.concatenate([grad_gate, grad_up], axis=1), inner


def local(
    layer_input,
    lengths,
    routes,
    route_weight,
    cotangent,
    norm_gain,
    w_qkv,
    b_qkv,
    w_out,
    post_gain,
    w_gate,
    w_up,
    w_down,
    shared_gate,
    shared_up,
    shared_down,
    shared_vector,
):
    grid = Grid()
    row_count, feature_count = layer_input.shape
    groups, owners, chips, na, nb = grid.groups, grid.owners, grid.chips, grid.na, grid.nb
    devices = groups * owners
    heads_here = HEADS // chips
    width = heads_here * HEAD_DIM
    routed_units = w_gate.shape[2]
    shared_units = shared_gate.shape[1]
    units = routed_units + shared_units
    positions = jnp.arange(row_count, dtype=jnp.int32)

    x_slots = grid.plane(layer_input)
    small = jnp.concatenate([norm_gain, post_gain, shared_vector, b_qkv]).astype(f32)
    small_count = small.shape[0]
    small = jnp.pad(small, (0, -small_count % row_count))
    meta = jnp.concatenate(
        [
            routes.T.astype(f32),
            route_weight.T.astype(f32),
            jnp.broadcast_to(lengths.astype(f32)[:, None], (1, row_count)),
            small.reshape(-1, row_count),
        ],
        axis=0,
    )
    meta_all = grid.everywhere(meta)
    flat_meta = meta_all.reshape(devices, *meta.shape)
    index = jnp.arange(devices, dtype=jnp.int32)
    ig, ia, ib, ic = (
        index // owners,
        index // (nb * CORES) % na,
        index // CORES % nb,
        index % CORES,
    )
    from_here = (
        ((ig - grid.group) % groups * na + (ia - grid.a) % na) * nb + (ib - grid.b) % nb
    ) * CORES + (ic - grid.core) % CORES
    small_all = jnp.take(flat_meta[:, 2 * TOP + 1 :], from_here, axis=0).reshape(devices, -1)
    own_features = norm_gain.shape[0]
    gains_in = small_all[:, :own_features].reshape(-1)
    gains_post = small_all[:, own_features : 2 * own_features].reshape(-1)
    gate_vector = small_all[:, 2 * own_features : 3 * own_features].reshape(-1)
    qkv_bias = small_all[:, 3 * own_features : small_count].reshape(3, chips, width)
    bias_here = lax.dynamic_index_in_dim(qkv_bias, grid.chip, 1, keepdims=False).reshape(-1)

    own_rows = w_qkv.shape[0]
    sliced = jnp.transpose(w_qkv.reshape(own_rows, 3, chips, width), (2, 0, 1, 3))
    by_chip = grid.swap(sliced.reshape(chips, own_rows, 3 * width))
    by_core = jnp.zeros((chips, CORES, own_rows, 3 * width), bf16)
    by_core = lax.dynamic_update_slice(by_core, by_chip[:, None], (0, grid.core, 0, 0))
    by_core = lax.dynamic_update_slice(
        by_core, grid.hop(by_chip, dc=1)[:, None], (0, 1 - grid.core, 0, 0)
    )
    by_core = by_core.reshape(-1, 3 * width)
    heads_weight = jnp.zeros((groups, *by_core.shape), bf16)
    for shift in range(groups):
        piece = grid.cross(by_core, shift) if shift else by_core
        heads_weight = lax.dynamic_update_slice(
            heads_weight, piece[None], ((grid.group - shift) % groups, 0, 0)
        )
    heads_weight = heads_weight.reshape(feature_count, 3 * width)
    out_weight = lax.all_gather(w_out, ("dp", "ep"), axis=0, tiled=True)

    valid_rows = positions < lengths[0]
    grad_rows = jnp.where(valid_rows[:, None], cotangent, jnp.zeros_like(cotangent))
    grad_plane = grid.plane(grad_rows)
    grad_slots = grid.both(grad_plane)

    inputs = layer_input.astype(f32)
    plane_rows = jnp.concatenate(x_slots, axis=0).astype(f32)
    plane_unit, _ = unit_norm(plane_rows)
    normed_first = (plane_unit * gains_in).astype(bf16)
    projected = dot(normed_first, heads_weight, ((1,), (0,))) + bias_here
    cosine_table, sine_table = rope_tables(row_count, HEAD_DIM)
    head_shape = (chips, row_count, heads_here, HEAD_DIM)
    query_low = rotate(
        projected[:, :width].reshape(head_shape), cosine_table, sine_table
    ).astype(bf16)
    key_low = rotate(
        projected[:, width : 2 * width].reshape(head_shape), cosine_table, sine_table
    ).astype(bf16)
    value_low = projected[:, 2 * width :].reshape(head_shape).astype(bf16)
    plane_lengths = meta_all[0, :, :, 0, 2 * TOP, 0].reshape(chips, 1)
    plane_valid = positions[None, :] < plane_lengths.astype(jnp.int32)
    allowed = (positions[None, None, :] <= positions[None, :, None]) & plane_valid[:, None, :]
    root_size = math.sqrt(HEAD_DIM)
    scores = (
        jnp.einsum("nqhd,nkhd->nhqk", query_low, key_low, preferred_element_type=f32) / root_size
    )
    scores = jnp.where(allowed[:, None], scores, -1e30)
    probabilities = jax.nn.softmax(scores, axis=-1)
    probs_low = probabilities.astype(bf16)
    context_here = jnp.einsum("nhqk,nkhd->nqhd", probs_low, value_low, preferred_element_type=f32)
    context_here = context_here.astype(bf16).reshape(na, nb, row_count, width)
    sent = grid.absolute(context_here).reshape(chips, row_count, width)
    context = jnp.transpose(grid.swap(sent), (1, 0, 2)).reshape(row_count, feature_count)
    residual = inputs + dot(context, out_weight, ((1,), (0,)))
    unit_second, factor_second = unit_norm(residual)
    normed_second = (unit_second * gains_post).astype(bf16)

    expert = lax.axis_index("ep") // HALVES
    into = jnp.concatenate([w_gate[0], shared_gate, w_up[0], shared_up], axis=1)
    out_of = jnp.concatenate([w_down[0], shared_down], axis=0)
    hits = meta_all[..., :TOP, :] == expert.astype(f32)
    route_scale = jnp.sum(jnp.where(hits, meta_all[..., TOP : 2 * TOP, :], 0.0), axis=-2)
    route_scale = jnp.transpose(route_scale, (0, 1, 3, 2, 4)).reshape(groups, na, -1)

    def slot_work(rows, grads, scale):
        gate_logit = dot(rows, gate_vector.astype(bf16), ((1,), (0,)))
        group_sigmoid = jax.nn.sigmoid(gate_logit)
        middle, grad_pre, inner = expert_rows(
            rows, grads, scale, group_sigmoid, into, out_of, routed_units
        )
        return middle, grad_pre, inner * group_sigmoid * (1.0 - group_sigmoid)

    second_plane = grid.plane(normed_second)
    second_slots = grid.both(second_plane)
    slot_shape = (CORES, nb, row_count, feature_count)
    worked = [
        slot_work(second_slots[s], grad_slots[s], route_scale[0, s]) for s in range(na)
    ]
    back_terms, out_terms = [], []
    for middle, grad_pre, logit_grad in worked:
        term = dot(grad_pre, into, ((1,), (1,))) + logit_grad[:, None] * gate_vector
        back_terms.append(grid.pair_sum(term.astype(bf16).reshape(slot_shape)))
        out_term = dot(middle, out_of, ((1,), (0,)))
        out_terms.append(grid.pair_sum(out_term.astype(bf16).reshape(slot_shape)))
    second_grad = grid.plane_sum(back_terms)
    mixed = grid.plane_sum(out_terms)
    combined = residual + mixed
    output = jnp.where(valid_rows[:, None], combined, 0.0).astype(bf16)

    def weight_grads(rows, grads, middles, grad_pres):
        rows, grads = jnp.concatenate(rows), jnp.concatenate(grads)
        middles, grad_pres = jnp.concatenate(middles), jnp.concatenate(grad_pres)
        columns = (0, routed_units, units, units + routed_units, 2 * units)
        into_grads = [
            dot(rows, grad_pres[:, lo:hi], ((0,), (0,))) for lo, hi in zip(columns, columns[1:])
        ]
        out_grads = [
            dot(middles[:, lo:hi], grads, ((0,), (0,)))
            for lo, hi in ((0, routed_units), (routed_units, units))
        ]
        return into_grads + out_grads

    logit_all = jnp.concatenate([w[2] for w in worked])
    vector_grad = dot(logit_all[None], jnp.concatenate(second_slots).astype(f32), ((1,), (0,)))[0]
    totals = weight_grads(
        second_slots, grad_slots, [w[0] for w in worked], [w[1] for w in worked]
    )
    for shift in range(1, groups):
        if groups > 2:
            totals, second_plane, grad_plane = lax.optimization_barrier(
                (totals, second_plane, grad_plane)
            )
        far_rows = grid.both([grid.cross(rows, -shift) for rows in second_plane])
        far_grads = grid.both([grid.cross(rows, -shift) for rows in grad_plane])
        far = [slot_work(far_rows[s], far_grads[s], route_scale[shift, s]) for s in range(na)]
        more = weight_grads(far_rows, far_grads, [w[0] for w in far], [w[1] for w in far])
        totals = [total + extra for total, extra in zip(totals, more)]

    grad_float = grad_rows.astype(f32)
    post_gain_grad = jnp.sum(second_grad * unit_second, axis=0)
    residual_grad = grad_float + norm_backward(
        second_grad, unit_second, factor_second, gains_post
    )
    attended_grad = residual_grad.astype(bf16)
    context_grad = dot(attended_grad, out_weight, ((1,), (1,))).astype(bf16)
    sent = jnp.transpose(context_grad.reshape(row_count, chips, width), (1, 0, 2))
    arrived = grid.relative(grid.swap(sent).reshape(na, nb, row_count, width))
    context_grad = arrived.reshape(head_shape)
    probs_grad = jnp.einsum("nqhd,nkhd->nhqk", context_grad, value_low, preferred_element_type=f32)
    value_grad = jnp.einsum("nhqk,nqhd->nkhd", probs_low, context_grad, preferred_element_type=f32)
    score_grad = probabilities * (
        probs_grad - jnp.sum(probabilities * probs_grad, axis=-1, keepdims=True)
    )
    score_grad = score_grad.astype(bf16)
    query_grad = (
        jnp.einsum("nhqk,nkhd->nqhd", score_grad, key_low, preferred_element_type=f32) / root_size
    )
    key_grad = (
        jnp.einsum("nhqk,nqhd->nkhd", score_grad, query_low, preferred_element_type=f32)
        / root_size
    )
    plane_count = chips * row_count
    projected_grad = jnp.concatenate(
        [
            rotate_back(query_grad, cosine_table, sine_table).reshape(plane_count, width),
            rotate_back(key_grad, cosine_table, sine_table).reshape(plane_count, width),
            value_grad.reshape(plane_count, width),
        ],
        axis=1,
    ).astype(bf16)
    first_terms = dot(projected_grad, heads_weight, ((1,), (1,))).astype(bf16)
    slot_first = first_terms.reshape(na, nb, row_count, feature_count)
    first_grad = grid.plane_sum([slot_first[s] for s in range(na)])
    unit_first, factor_first = unit_norm(inputs)
    input_part = norm_backward(first_grad, unit_first, factor_first, gains_in)
    layer_grad = (residual_grad + input_part).astype(bf16)

    out_weight_grad = dot(context, attended_grad, ((0,), (0,))).astype(bf16)
    out_weight_grad = grid.scatter_core(
        out_weight_grad.reshape(groups, na, nb, CORES, own_rows, feature_count), 3
    )
    out_weight_grad = grid.scatter_groups(out_weight_grad.astype(bf16))
    out_weight_grad = grid.scatter_rows(out_weight_grad.astype(bf16))

    qkv_grad = dot(normed_first, projected_grad, ((0,), (0,))).astype(bf16)
    qkv_grad = grid.scatter_core(qkv_grad.reshape(groups, chips, CORES, own_rows, 3 * width), 2)
    qkv_grad = grid.scatter_groups(qkv_grad.astype(bf16)).astype(bf16)
    qkv_grad = grid.swap(qkv_grad).reshape(chips, own_rows, 3, width)
    qkv_weight_grad = jnp.transpose(qkv_grad, (1, 2, 0, 3)).reshape(own_rows, -1).astype(f32)

    gain_grad = jnp.sum(first_terms.astype(f32) * plane_unit, axis=0)
    bias_grad = jnp.zeros((3, chips, width), f32)
    bias_grad = lax.dynamic_update_slice(
        bias_grad,
        jnp.sum(projected_grad.astype(f32), axis=0).reshape(3, 1, width),
        (0, grid.chip, 0),
    )
    vectors = jnp.concatenate(
        [
            gain_grad.reshape(devices, -1),
            post_gain_grad.reshape(devices, -1),
            vector_grad.reshape(devices, -1),
            bias_grad.reshape(devices, -1),
        ],
        axis=1,
    ).reshape(groups, na, nb, CORES, -1)
    vectors = grid.scatter_core(vectors, 3)
    vectors = grid.scatter_groups(vectors)
    vectors = grid.scatter_rows(vectors)
    return (
        output,
        layer_grad,
        vectors[:own_features],
        qkv_weight_grad,
        vectors[3 * own_features :],
        out_weight_grad,
        vectors[own_features : 2 * own_features],
        totals[0][None],
        totals[2][None],
        totals[4][None],
        totals[1],
        totals[3],
        totals[5],
        vectors[2 * own_features : 3 * own_features],
    )


def solution(mesh):
    rows = P(("dp", "ep"), None)
    split = P(("dp", "ep"))
    parts = P("ep", None, None)
    return jax.shard_map(
        local,
        mesh=mesh,
        in_specs=(
            rows,
            split,
            rows,
            rows,
            rows,
            split,
            rows,
            split,
            rows,
            split,
            parts,
            parts,
            parts,
            P(None, "ep"),
            P(None, "ep"),
            P("ep", None),
            split,
        ),
        out_specs=(
            rows,
            rows,
            split,
            rows,
            split,
            rows,
            split,
            parts,
            parts,
            parts,
            P(None, "ep"),
            P(None, "ep"),
            P("ep", None),
            split,
        ),
        check_vma=False,
    )
```

time: 2410 us -> 1170 us (0.49)
  waiting for transfers between devices: 1390 us -> 389 us
  blocking collectives: 421 us -> 0 us
  other arithmetic: 96.7 us -> 173 us
  local copies, waits for them, and re-layouts: 78.1 us -> 142 us
  matrix products: 261 us -> 301 us
    reduce_scatter x4 -> x0, waiting for transfers between devices: 549 us -> none  [the longest x1 440 us: local(): lax.psum_scatter(qkv_weight_grad, ('dp', 'ep'), scatter_dimension=0, tile...]
    all_to_all x4, waiting for transfers between devices: 541 us -> 13.4 us  [swap(): lax.all_to_all(blocks, 'ep', split_axis=0, concat_axis=0, tiled=True, axi...]
    unnamed x3 -> x0, blocking collectives: 421 us -> none
    ppermute x0 -> x96, waiting for transfers between devices: none -> 375 us  [the longest x83 305 us: hop(): return lax.ppermute(values, 'ep', pairs)]
    all_gather x4 -> x1, waiting for transfers between devices: 295 us -> 0.01 us  [local(): out_weight = lax.all_gather(w_out, ('dp', 'ep'), axis=0, tiled=True)]
    all_to_all x4, starting transfers between devices: 144 us -> 16 us  [swap(): lax.all_to_all(blocks, 'ep', split_axis=0, concat_axis=0, tiled=True, axi...]
    concatenate x0 -> x13, other arithmetic: none -> 127 us  [the longest x4 118 us: weight_grads(): middles, grad_pres = (jnp.concatenate(middles), jnp.concatenate(grad_pres))]
    ppermute x0 -> x96, starting transfers between devices: none -> 125 us  [the longest x83 109 us: hop(): return lax.ppermute(values, 'ep', pairs)]
  transfers between devices with their start and end apart: 13 -> 101, of which waited for: 9 -> 30; matrix products, arithmetic and copies ran while one was open for 15% -> 51% of each run, Pallas kernels for 0% -> 0%
where the time goes in v1:
time: 1170 us; the launch traced here: 1160 us
  waiting for transfers between devices  389 us (33%)
  matrix products  301 us (26%)
  other arithmetic  173 us (15%)
  local copies, waits for them, and re-layouts  142 us (12%)
  starting transfers between devices  141 us (12%)
  between operations  17.9 us (2%)
    ppermute x83, waiting for transfers between devices, hop(): return lax.ppermute(values, 'ep', pairs)  305 us
    dot_general x51, matrix products, dot(): lax.dot_general(left, right, (dims, ((), ())), preferred_element_type=f32)  296 us
    concatenate x4, other arithmetic, weight_grads(): middles, grad_pres = (jnp.concatenate(middles), jnp.concatenate(grad_pres))  118 us
    ppermute x83, starting transfers between devices, hop(): return lax.ppermute(values, 'ep', pairs)  109 us
    ppermute x13, waiting for transfers between devices, cross(): return lax.ppermute(values, 'dp', pairs)  69.8 us
    unnamed x365, local copies, waits for them, and re-layouts  68.3 us
  transfers between devices with their start and end apart: 101, of which 30 were waited for; matrix products, arithmetic and copies ran while one was open for 51% of the time, Pallas kernels for 0%

profile of v1, /device:TPU:0, one launch (start us, length us, event | category | flops | bytes accessed | tf_op | source)
XLA Modules:
  0.0 1164.2 jit_solution(4128098100196865703)
XLA Ops:
  58.8 13.3 %collective-permute-done.55 = bf16[128,2048]{1,0:T(8,128)(2,1)S(1)} collective-permute-done((bf16[128,2048]{1,0:T(8,128)(2,1)S(1)}, bf16[128,2048]{1,0:T(8,128)(2,1)S(1)}, u32[]{:S(2)}, u32[]{:S(2)}) %collective-permute-start.55) | collective-permute-done | bytes 524320 | tf_op jit(solution)/shard_map/ppermute | solution.py:81
  77.3 22.6 %collective-permute-done.3 = bf16[128,2048]{1,0:T(8,128)(2,1)S(1)} collective-permute-done((bf16[128,2048]{1,0:T(8,128)(2,1)S(1)}, bf16[128,2048]{1,0:T(8,128)(2,1)S(1)}, u32[]{:S(2)}, u32[]{:S(2)}) %collective-permute-start.3) | collective-permute-done | bytes 524320 | tf_op jit(solution)/shard_map/ppermute | solution.py:81
  106.0 30.1 %collective-permute-start.49 = (bf16[128,2048]{1,0:T(8,128)(2,1)S(1)}, bf16[128,2048]{1,0:T(8,128)(2,1)}, u32[]{:S(2)}, u32[]{:S(2)}) collective-permute-start(bf16[128,2048]{1,0:T(8,128)(2,1)S(1)} %get-tuple-element.27), channel_id=1, source_target_pairs={{0,4},{1,5},{2,6},{3,7},{4,8},{5,9},{6,10},{7,11},{8,12},{9,13},{1... | collective-permute-start | bytes 1572872 | tf_op jit(solution)/shard_map/ppermute | solution.py:81
  141.2 25.1 %collective-permute-done.43 = bf16[128,2048]{1,0:T(8,128)(2,1)} collective-permute-done((bf16[128,2048]{1,0:T(8,128)(2,1)S(1)}, bf16[128,2048]{1,0:T(8,128)(2,1)}, u32[]{:S(2)}, u32[]{:S(2)}) %collective-permute-start.43) | collective-permute-done | bytes 524320 | tf_op jit(solution)/shard_map/ppermute | solution.py:81
  200.2 10.5 collective-permute-done.90
  218.2 26.1 %collective-permute-done.14 = bf16[1024,768]{1,0:T(8,128)(2,1)S(1)} collective-permute-done((bf16[1024,768]{1,0:T(8,128)(2,1)S(1)}, bf16[1024,768]{1,0:T(8,128)(2,1)S(1)}, u32[]{:S(2)}, u32[]{:S(2)}) %collective-permute-start.14) | collective-permute-done | bytes 1572896 | tf_op jit(solution)/shard_map/ppermute | solution.py:85
  320.0 31.7 %collective-permute-done.21 = bf16[128,2048]{1,0:T(8,128)(2,1)S(1)} collective-permute-done((bf16[128,2048]{1,0:T(8,128)(2,1)S(1)}, bf16[128,2048]{1,0:T(8,128)(2,1)S(1)}, u32[]{:S(2)}, u32[]{:S(2)}) %collective-permute-start.21) | collective-permute-done | bytes 524320 | tf_op jit(solution)/shard_map/ppermute | solution.py:81
  435.4 13.5 %multiply_convert_fusion.15 = (bf16[512,1056]{0,1:T(8,128)(2,1)}, bf16[512,1056]{0,1:T(8,128)(2,1)}, f32[512]{0:T(512)S(1)}, f32[512]{0:T(512)S(1)}, f32[512]{0:T(512)S(1)}, /*index=5*/f32[512]{0:T(512)S(1)}) fusion(f32[512,2112]{0,1:T(8,128)} %fusion.304, f32[512]{0:T(512)S(1)} %add_divide_fusion.15, f32[512]{0:T(512)S(1)} %bitcast.409, ...), kind=kOutput, calls=%fused_computation.115 | convolution fusion | flops 2252781568 | bytes 32388128 | tf_op jit(solution)/shard_map/dot_general | solution.py:54
  461.6 57.0 %maximum_maximum_fusion = bf16[2048,2112]{0,1:T(8,128)(2,1)S(1)} fusion(bf16[512,1056]{0,1:T(8,128)(2,1)S(1)} %get-tuple-element.38, bf16[512,1056]{0,1:T(8,128)(2,1)S(1)} %get-tuple-element.37, bf16[512,1056]{0,1:T(8,128)(2,1)S(1)} %get-tuple-element.36, bf16[512,1056]{0,1:T(8,128)(2,1)S(1)} %get-tuple-element.35, bf16[512,1056]{0,1:T(8,128)(2,1)} %get-tuple-element.34, ...), kind=kLoop, calls=%fused_computation.7 | loop fusion | flops 69206016 | bytes 17301504 | tf_op jit(solution)/shard_map/concatenate | solution.py:345
  594.5 12.4 %copy.131 = bf16[2048,2048]{1,0:T(8,128)(2,1)} copy(bf16[2048,2048]{0,1:T(8,128)(2,1)} %bitcast.344) | data formatting | bytes 16777216 | tf_op jit(solution)/shard_map/dot_general | solution.py:54
  627.9 10.5 fusion.10
  673.5 57.9 %maximum_maximum_fusion.1 = bf16[2048,2112]{0,1:T(8,128)(2,1)S(1)} fusion(bf16[512,1056]{0,1:T(8,128)(2,1)S(1)} %get-tuple-element.52, bf16[512,1056]{0,1:T(8,128)(2,1)S(1)} %get-tuple-element.51, bf16[512,1056]{0,1:T(8,128)(2,1)S(1)} %get-tuple-element.50, bf16[512,1056]{0,1:T(8,128)(2,1)S(1)} %get-tuple-element.49, bf16[512,1056]{0,1:T(8,128)(2,1)S(1)} %copy-done.64, ...), kind=kLoop, calls=%fused_computation.8 | loop fusion | flops 69206016 | bytes 17301504 | tf_op jit(solution)/shard_map/concatenate | solution.py:345
  731.4 12.2 %add_bitcast_fusion.2 = f32[1,2048,704]{1,2,0:T(8,128)} fusion(f32[2048,704]{0,1:T(8,128)} %fusion.16, bf16[2048,2048]{1,0:T(8,128)(2,1)} %get-tuple-element.98, bf16[2048,2112]{0,1:T(8,128)(2,1)S(1)} %maximum_maximum_fusion.1), kind=kOutput, calls=%fused_computation.17 | convolution fusion | flops 5907021824 | bytes 22806528 | tf_op jit(solution)/shard_map/dot_general | solution.py:54
  743.7 12.3 %add_bitcast_fusion.1 = f32[1,2048,704]{1,2,0:T(8,128)} fusion(f32[2048,704]{0,1:T(8,128)} %fusion.13, bf16[2048,2048]{1,0:T(8,128)(2,1)} %get-tuple-element.98, bf16[2048,2112]{0,1:T(8,128)(2,1)S(1)} %maximum_maximum_fusion.1), kind=kOutput, calls=%fused_computation.16 | convolution fusion | flops 5907021824 | bytes 22806528 | tf_op jit(solution)/shard_map/dot_general | solution.py:54
  756.8 12.4 %add_bitcast_fusion = f32[1,704,2048]{2,1,0:T(8,128)} fusion(f32[704,2048]{1,0:T(8,128)} %fusion.10, bf16[2048,2048]{1,0:T(8,128)(2,1)} %constant_dynamic-update-slice_fusion.69, bf16[2048,1056]{0,1:T(8,128)(2,1)S(1)} %pad_maximum_fusion.3), kind=kOutput, calls=%fused_computation.15 | convolution fusion | flops 5907021824 | bytes 22806528 | tf_op jit(solution)/shard_map/dot_general | solution.py:54
  824.1 11.1 collective-permute-done.31
  846.6 10.6 collective-permute-done.19
  859.7 13.0 %collective-permute-done.48 = bf16[128,2048]{1,0:T(8,128)(2,1)S(1)} collective-permute-done((bf16[128,2048]{1,0:T(8,128)(2,1)S(1)}, bf16[128,2048]{1,0:T(8,128)(2,1)S(1)}, u32[]{:S(2)}, u32[]{:S(2)}) %collective-permute-start.48) | collective-permute-done | bytes 524320 | tf_op jit(solution)/shard_map/ppermute | solution.py:81
  882.5 33.7 %collective-permute-done.26 = bf16[128,2048]{1,0:T(8,128)(2,1)S(1)} collective-permute-done((bf16[128,2048]{1,0:T(8,128)(2,1)S(1)}, bf16[128,2048]{1,0:T(8,128)(2,1)S(1)}, u32[]{:S(2)}, u32[]{:S(2)}) %collective-permute-start.26) | collective-permute-done | bytes 524320 | tf_op jit(solution)/shard_map/ppermute | solution.py:81
  984.5 25.0 %collective-permute-done.68 = f32[4,384]{1,0:T(4,128)S(1)} collective-permute-done((f32[4,384]{1,0:T(4,128)S(1)}, f32[4,384]{1,0:T(4,128)S(1)}, u32[]{:S(2)}, u32[]{:S(2)}) %collective-permute-start.68) | collective-permute-done | bytes 6176 | tf_op jit(solution)/shard_map/ppermute | solution.py:81
  1029.1 27.9 %collective-permute-done.75 = bf16[4,2,64,2048]{3,2,0,1:T(8,128)(2,1)S(1)} collective-permute-done((bf16[4,2,64,2048]{3,2,0,1:T(8,128)(2,1)S(1)}, bf16[4,2,64,2048]{3,2,0,1:T(8,128)(2,1)S(1)}, u32[]{:S(2)}, u32[]{:S(2)}) %collective-permute-start.75) | collective-permute-done | bytes 2097184 | tf_op jit(solution)/shard_map/ppermute | solution.py:85
  1073.0 31.7 %collective-permute-done.62 = bf16[128,2048]{1,0:T(8,128)(2,1)S(1)} collective-permute-done((bf16[128,2048]{1,0:T(8,128)(2,1)S(1)}, bf16[128,2048]{1,0:T(8,128)(2,1)S(1)}, u32[]{:S(2)}, u32[]{:S(2)}) %collective-permute-start.62) | collective-permute-done | bytes 524320 | tf_op jit(solution)/shard_map/ppermute | solution.py:81
  1122.6 11.3 all-to-all-done.3
  1139.1 16.1 %collective-permute-done.78 = bf16[64,2048]{1,0:T(8,128)(2,1)} collective-permute-done((bf16[64,2048]{1,0:T(8,128)(2,1)}, bf16[64,2048]{1,0:T(8,128)(2,1)}, u32[]{:S(2)}, u32[]{:S(2)}) %collective-permute-start.78) | collective-permute-done | bytes 262176 | tf_op jit(solution)/shard_map/ppermute | solution.py:81
  (786 shorter events, 618.3 us)
Async XLA Ops:
  7.2 69.4 %collective-permute-start = (bf16[128,2048]{1,0:T(8,128)(2,1)}, bf16[128,2048]{1,0:T(8,128)(2,1)}, u32[]{:S(2)}, u32[]{:S(2)}) collective-permute-start(bf16[128,2048]{1,0:T(8,128)(2,1)} %param.21), channel_id=1, source_target_pairs={{0,2},{1,3},{2,0},{3,1},{4,6},{5,7},{6,4},{7,5},{8,10},{9,11},{10,... | collective-permute-start | bytes 1572872 | tf_op jit(solution)/shard_map/ppermute | solution.py:81
  10.2 66.4 %collective-permute-start.1 = (bf16[128,2048]{1,0:T(8,128)(2,1)}, bf16[128,2048]{1,0:T(8,128)(2,1)}, u32[]{:S(2)}, u32[]{:S(2)}) collective-permute-start(bf16[128,2048]{1,0:T(8,128)(2,1)} %param.21), channel_id=1, source_target_pairs={{0,12},{1,13},{2,14},{3,15},{4,0},{5,1},{6,2},{7,3},{8,4},{9,5},{1... | collective-permute-start | bytes 1572872 | tf_op jit(solution)/shard_map/ppermute | solution.py:81
  17.3 152.4 %all-to-all-start = ((bf16[8,64,768]{2,1,0:T(8,128)(2,1)}), bf16[8,64,768]{2,1,0:T(8,128)(2,1)S(1)}, u32[]{:S(2)}, u32[]{:S(2)}) async-start(bf16[8,64,768]{2,1,0:T(8,128)(2,1)} %reshape.738), calls=%async_computation | async-start | bytes 1572864 | tf_op jit(solution)/shard_map/all_to_all | solution.py:127
  21.0 259.1 %all-gather.2.cloned.1.call-start = ((), (), s32[]{:S(2)}) async-start(), calls=%async_computation.4 | async-start | bytes 8650752 | tf_op jit(solution)/shard_map/all_gather | solution.py:272
  45.5 54.4 %collective-permute-start.3 = (bf16[128,2048]{1,0:T(8,128)(2,1)S(1)}, bf16[128,2048]{1,0:T(8,128)(2,1)S(1)}, u32[]{:S(2)}, u32[]{:S(2)}) collective-permute-start(bf16[128,2048]{1,0:T(8,128)(2,1)S(1)} %copy-done.3), channel_id=1, source_target_pairs={{0,8},{1,9},{2,10},{3,11},{4,12},{5,13},{6,14},{7,15},{8,0},{9,1},... | collective-permute-start | bytes 1572872 | tf_op jit(solution)/shard_map/ppermute | solution.py:81
  53.0 53.0 %collective-permute-start.5 = (bf16[128,2048]{1,0:T(8,128)(2,1)S(1)}, bf16[128,2048]{1,0:T(8,128)(2,1)}, u32[]{:S(2)}, u32[]{:S(2)}) collective-permute-start(bf16[128,2048]{1,0:T(8,128)(2,1)S(1)} %copy-done.3), channel_id=1, source_target_pairs={{0,4},{1,5},{2,6},{3,7},{4,8},{5,9},{6,10},{7,11},{8,12},{9,13},{1... | collective-permute-start | bytes 1572872 | tf_op jit(solution)/shard_map/ppermute | solution.py:81
  72.2 67.6 %collective-permute-start.37 = (bf16[128,2048]{1,0:T(8,128)(2,1)S(1)}, bf16[128,2048]{1,0:T(8,128)(2,1)}, u32[]{:S(2)}, u32[]{:S(2)}) collective-permute-start(bf16[128,2048]{1,0:T(8,128)(2,1)S(1)} %get-tuple-element.27), channel_id=1, source_target_pairs={{0,12},{1,13},{2,14},{3,15},{4,0},{5,1},{6,2},{7,3},{8,4},{9,5},{1... | collective-permute-start | bytes 1572872 | tf_op jit(solution)/shard_map/ppermute | solution.py:81
  76.6 89.7 %collective-permute-start.43 = (bf16[128,2048]{1,0:T(8,128)(2,1)S(1)}, bf16[128,2048]{1,0:T(8,128)(2,1)}, u32[]{:S(2)}, u32[]{:S(2)}) collective-permute-start(bf16[128,2048]{1,0:T(8,128)(2,1)S(1)} %get-tuple-element.27), channel_id=1, source_target_pairs={{0,8},{1,9},{2,10},{3,11},{4,12},{5,13},{6,14},{7,15},{8,0},{9,1},... | collective-permute-start | bytes 1572872 | tf_op jit(solution)/shard_map/ppermute | solution.py:81
  105.2 64.5 %collective-permute-start.56 = (bf16[256,2048]{1,0:T(8,128)(2,1)}, bf16[256,2048]{1,0:T(8,128)(2,1)}, u32[]{:S(2)}, u32[]{:S(2)}) collective-permute-start(bf16[256,2048]{1,0:T(8,128)(2,1)} %pad_maximum_fusion.6), channel_id=1, source_target_pairs={{0,1},{1,0},{2,3},{3,2},{4,5},{5,4},{6,7},{7,6},{8,9},{9,8},{10,11... | collective-permute-start | bytes 3145736 | tf_op jit(solution)/shard_map/ppermute | solution.py:81
  106.0 60.8 %collective-permute-start.49 = (bf16[128,2048]{1,0:T(8,128)(2,1)S(1)}, bf16[128,2048]{1,0:T(8,128)(2,1)}, u32[]{:S(2)}, u32[]{:S(2)}) collective-permute-start(bf16[128,2048]{1,0:T(8,128)(2,1)S(1)} %get-tuple-element.27), channel_id=1, source_target_pairs={{0,4},{1,5},{2,6},{3,7},{4,8},{5,9},{6,10},{7,11},{8,12},{9,13},{1... | collective-permute-start | bytes 1572872 | tf_op jit(solution)/shard_map/ppermute | solution.py:81
  168.4 97.5 %collective-permute-start.50 = (bf16[128,2048]{1,0:T(8,128)(2,1)}, bf16[128,2048]{1,0:T(8,128)(2,1)}, u32[]{:S(2)}, u32[]{:S(2)}) collective-permute-start(bf16[128,2048]{1,0:T(8,128)(2,1)} %collective-permute-done.49), channel_id=1, source_target_pairs={{0,2},{1,3},{2,0},{3,1},{4,6},{5,7},{6,4},{7,5},{8,10},{9,11},{10,... | collective-permute-start | bytes 1572872 | tf_op jit(solution)/shard_map/ppermute | solution.py:81
  186.6 57.7 %collective-permute-start.14 = (bf16[1024,768]{1,0:T(8,128)(2,1)S(1)}, bf16[1024,768]{1,0:T(8,128)(2,1)S(1)}, u32[]{:S(2)}, u32[]{:S(2)}) collective-permute-start(bf16[1024,768]{1,0:T(8,128)(2,1)S(1)} %bitcast.353), channel_id=1, source_target_pairs={{0,16},{16,0},{1,17},{17,1},{2,18},{18,2},{3,19},{19,3},{4,20},{20... | collective-permute-start | bytes 4718600 | tf_op jit(solution)/shard_map/ppermute | solution.py:85
  210.7 59.0 %collective-permute-start.92 = (bf16[256,2048]{1,0:T(8,128)(2,1)}, bf16[256,2048]{1,0:T(8,128)(2,1)}, u32[]{:S(2)}, u32[]{:S(2)}) collective-permute-start(bf16[256,2048]{1,0:T(8,128)(2,1)} %get-tuple-element.125), channel_id=1, source_target_pairs={{0,16},{16,0},{1,17},{17,1},{2,18},{18,2},{3,19},{19,3},{4,20},{20... | collective-permute-start | bytes 3145736 | tf_op jit(solution)/shard_map/ppermute | solution.py:85
  212.2 57.7 %collective-permute-start.91 = (bf16[256,2048]{1,0:T(8,128)(2,1)}, bf16[256,2048]{1,0:T(8,128)(2,1)}, u32[]{:S(2)}, u32[]{:S(2)}) collective-permute-start(bf16[256,2048]{1,0:T(8,128)(2,1)} %collective-permute-done.90), channel_id=1, source_target_pairs={{0,1},{1,0},{2,3},{3,2},{4,5},{5,4},{6,7},{7,6},{8,9},{9,8},{10,11... | collective-permute-start | bytes 3145736 | tf_op jit(solution)/shard_map/ppermute | solution.py:81
  299.8 54.0 %collective-permute-start.34 = (bf16[256,2048]{1,0:T(8,128)(2,1)S(1)}, bf16[256,2048]{1,0:T(8,128)(2,1)S(1)}, u32[]{:S(2)}, u32[]{:S(2)}) collective-permute-start(bf16[256,2048]{1,0:T(8,128)(2,1)S(1)} %pad_maximum_fusion.5), channel_id=1, source_target_pairs={{0,1},{1,0},{2,3},{3,2},{4,5},{5,4},{6,7},{7,6},{8,9},{9,8},{10,11... | collective-permute-start | bytes 3145736 | tf_op jit(solution)/shard_map/ppermute | solution.py:81
  399.4 249.2 %collective-permute-start.86 = (bf16[256,2048]{1,0:T(8,128)(2,1)}, bf16[256,2048]{1,0:T(8,128)(2,1)}, u32[]{:S(2)}, u32[]{:S(2)}) collective-permute-start(bf16[256,2048]{1,0:T(8,128)(2,1)} %get-tuple-element.134), channel_id=1, source_target_pairs={{0,16},{16,0},{1,17},{17,1},{2,18},{18,2},{3,19},{19,3},{4,20},{20... | collective-permute-start | bytes 3145736 | tf_op jit(solution)/shard_map/ppermute | solution.py:85
  416.3 199.4 %collective-permute-start.85 = (bf16[256,2048]{1,0:T(8,128)(2,1)}, bf16[256,2048]{1,0:T(8,128)(2,1)}, u32[]{:S(2)}, u32[]{:S(2)}) collective-permute-start(bf16[256,2048]{1,0:T(8,128)(2,1)} %collective-permute-done.84), channel_id=1, source_target_pairs={{0,1},{1,0},{2,3},{3,2},{4,5},{5,4},{6,7},{7,6},{8,9},{9,8},{10,11... | collective-permute-start | bytes 3145736 | tf_op jit(solution)/shard_map/ppermute | solution.py:81
  564.2 205.0 %collective-permute-start.57 = (bf16[2,128,2048]{2,1,0:T(8,128)(2,1)}, bf16[2,128,2048]{2,1,0:T(8,128)(2,1)}, u32[]{:S(2)}, u32[]{:S(2)}) collective-permute-start(bf16[2,128,2048]{2,1,0:T(8,128)(2,1)} %bitcast.73), channel_id=1, source_target_pairs={{0,1},{1,0},{2,3},{3,2},{4,5},{5,4},{6,7},{7,6},{8,9},{9,8},{10,11... | collective-permute-start | bytes 3145736 | tf_op jit(solution)/shard_map/ppermute | solution.py:81
  572.1 199.1 %collective-permute-start.52 = (bf16[2,128,2048]{2,1,0:T(8,128)(2,1)}, bf16[2,128,2048]{2,1,0:T(8,128)(2,1)}, u32[]{:S(2)}, u32[]{:S(2)}) collective-permute-start(bf16[2,128,2048]{2,1,0:T(8,128)(2,1)} %bitcast.69), channel_id=1, source_target_pairs={{0,1},{1,0},{2,3},{3,2},{4,5},{5,4},{6,7},{7,6},{8,9},{9,8},{10,11... | collective-permute-start | bytes 3145736 | tf_op jit(solution)/shard_map/ppermute | solution.py:81
  579.1 194.5 %collective-permute-start.46 = (bf16[2,128,2048]{2,1,0:T(8,128)(2,1)}, bf16[2,128,2048]{2,1,0:T(8,128)(2,1)}, u32[]{:S(2)}, u32[]{:S(2)}) collective-permute-start(bf16[2,128,2048]{2,1,0:T(8,128)(2,1)} %bitcast.65), channel_id=1, source_target_pairs={{0,1},{1,0},{2,3},{3,2},{4,5},{5,4},{6,7},{7,6},{8,9},{9,8},{10,11... | collective-permute-start | bytes 3145736 | tf_op jit(solution)/shard_map/ppermute | solution.py:81
  615.7 159.7 %collective-permute-start.40 = (bf16[2,128,2048]{2,1,0:T(8,128)(2,1)}, bf16[2,128,2048]{2,1,0:T(8,128)(2,1)S(1)}, u32[]{:S(2)}, u32[]{:S(2)}) collective-permute-start(bf16[2,128,2048]{2,1,0:T(8,128)(2,1)} %bitcast.61), channel_id=1, source_target_pairs={{0,1},{1,0},{2,3},{3,2},{4,5},{5,4},{6,7},{7,6},{8,9},{9,8},{10,11... | collective-permute-start | bytes 3145736 | tf_op jit(solution)/shard_map/ppermute | solution.py:81
  657.8 119.6 %collective-permute-start.35 = (bf16[2,128,2048]{2,1,0:T(8,128)(2,1)S(1)}, bf16[2,128,2048]{2,1,0:T(8,128)(2,1)S(1)}, u32[]{:S(2)}, u32[]{:S(2)}) collective-permute-start(bf16[2,128,2048]{2,1,0:T(8,128)(2,1)S(1)} %bitcast.386), channel_id=1, source_target_pairs={{0,1},{1,0},{2,3},{3,2},{4,5},{5,4},{6,7},{7,6},{8,9},{9,8},{10,11... | collective-permute-start | bytes 3145736 | tf_op jit(solution)/shard_map/ppermute | solution.py:81
  775.4 83.4 %collective-permute-start.58 = (bf16[128,2048]{1,0:T(8,128)(2,1)S(1)}, bf16[128,2048]{1,0:T(8,128)(2,1)S(1)}, u32[]{:S(2)}, u32[]{:S(2)}) collective-permute-start(bf16[128,2048]{1,0:T(8,128)(2,1)S(1)} %slice_bitcast_fusion), channel_id=1, source_target_pairs={{0,2},{1,3},{2,0},{3,1},{4,6},{5,7},{6,4},{7,5},{8,10},{9,11},{10,... | collective-permute-start | bytes 1572872 | tf_op jit(solution)/shard_map/ppermute | solution.py:81
  858.9 57.3 %collective-permute-start.26 = (bf16[128,2048]{1,0:T(8,128)(2,1)S(1)}, bf16[128,2048]{1,0:T(8,128)(2,1)S(1)}, u32[]{:S(2)}, u32[]{:S(2)}) collective-permute-start(bf16[128,2048]{1,0:T(8,128)(2,1)S(1)} %fusion.198), channel_id=1, source_target_pairs={{0,8},{1,9},{2,10},{3,11},{4,12},{5,13},{6,14},{7,15},{8,0},{9,1},... | collective-permute-start | bytes 1572872 | tf_op jit(solution)/shard_map/ppermute | solution.py:81
  (237 other events, 6061.5 us)
Sparse Core Ops, SparseCore 0:
  24.7 132.8 all-gather.1

commit v2 on v1

v2 whole, which is shorter than its diff:
```python
import functools
import math

import jax
import jax.numpy as jnp
from jax import lax
from jax.experimental import pallas as pl
from jax.experimental.pallas import tpu as pltpu
from jax.sharding import PartitionSpec as P

HEADS = 16
HEAD_DIM = 128
TOP = 4
HALVES = 2
CORES = 2
LINE = 4
LANES = 128
TILE = 512
VMEM = 56 << 20


epsilon = 1e-06
rope_base = 1000000.0
bf16 = jnp.bfloat16
f32 = jnp.float32


def unit_norm(values):
    factor = lax.rsqrt(jnp.mean(values * values, axis=-1, keepdims=True) + epsilon)
    return (values * factor, factor)


def norm_backward(incoming, unit_rows, factor, gain_row):
    scaled = incoming * gain_row
    inner_mean = jnp.mean(scaled * unit_rows, axis=-1, keepdims=True)
    return factor * (scaled - unit_rows * inner_mean)


def rope_tables(row_count, head_size):
    inverse = rope_base ** (-jnp.arange(0, head_size, 2, dtype=f32) / head_size)
    angles = jnp.arange(row_count, dtype=f32)[:, None] * inverse[None, :]
    angles = jnp.concatenate([angles, angles], axis=-1)
    return (jnp.cos(angles)[:, None, :], jnp.sin(angles)[:, None, :])


def dot(left, right, dims):
    return lax.dot_general(left, right, (dims, ((), ())), preferred_element_type=f32)


def tie(*values):
    return lax.optimization_barrier(values)


class Grid:
    def __init__(self):
        self.groups = lax.axis_size("dp")
        self.owners = lax.axis_size("ep")
        self.chips = self.owners // CORES
        self.na = math.gcd(LINE, self.chips)
        self.nb = self.chips // self.na
        self.group = lax.axis_index("dp")
        me = lax.axis_index("ep")
        self.chip = me // CORES
        self.core = me % CORES
        self.a = self.chip // self.nb
        self.b = self.chip % self.nb

    def place(self, a, b, c):
        return ((a % self.na) * self.nb + b % self.nb) * CORES + c % CORES

    def hop(self, values, da=0, db=0, dc=0):
        pairs = [
            (self.place(a, b, c), self.place(a + da, b + db, c + dc))
            for a in range(self.na)
            for b in range(self.nb)
            for c in range(CORES)
        ]
        return lax.ppermute(values, "ep", pairs)

    def cross(self, values, shift):
        pairs = [(g, (g + shift) % self.groups) for g in range(self.groups)]
        return lax.ppermute(values, "dp", pairs)

    def row(self, block):
        return [block] + [self.hop(block, db=db) for db in range(1, self.nb)]

    def row_sum(self, terms):
        total = terms[0].astype(f32)
        for db in range(1, self.nb):
            total = total + self.hop(terms[db], db=-db).astype(f32)
        return total

    def core_sum(self, terms):
        return (terms[0].astype(f32) + self.hop(terms[1], dc=1).astype(f32)).astype(bf16)

    def same_core(self):
        return [[k * CORES + c for k in range(self.chips)] for c in range(CORES)]

    def swap(self, blocks):
        return lax.all_to_all(
            blocks,
            "ep",
            split_axis=0,
            concat_axis=0,
            tiled=True,
            axis_index_groups=self.same_core(),
        )

    def scatter_core(self, terms, axis):
        mine = lax.dynamic_index_in_dim(terms, self.core, axis, keepdims=False)
        other = lax.dynamic_index_in_dim(terms, 1 - self.core, axis, keepdims=False)
        return mine.astype(f32) + self.hop(other, dc=1).astype(f32)

    def scatter_groups(self, terms):
        total = lax.dynamic_index_in_dim(terms, self.group, 0, keepdims=False).astype(f32)
        for shift in range(1, self.groups):
            there = (self.group + shift) % self.groups
            piece = lax.dynamic_index_in_dim(terms, there, 0, keepdims=False)
            total = total + self.cross(piece, shift).astype(f32)
        return total

    def scatter_row(self, terms):
        total = lax.dynamic_index_in_dim(terms, self.b, 1, keepdims=False).astype(f32)
        for db in range(1, self.nb):
            there = (self.b + db) % self.nb
            piece = lax.dynamic_index_in_dim(terms, there, 1, keepdims=False)
            total = total + self.hop(piece, db=db).astype(f32)
        return total.astype(terms.dtype)

    def scatter_line(self, terms):
        total = lax.dynamic_index_in_dim(terms, self.a, 0, keepdims=False).astype(f32)
        for da in range(1, self.na):
            there = (self.a + da) % self.na
            piece = lax.dynamic_index_in_dim(terms, there, 0, keepdims=False)
            total = total + self.hop(piece, da=da).astype(f32)
        return total

    def everywhere(self, small):
        parts = [small] + [self.cross(small, shift) for shift in range(1, self.groups)]
        level = yield jnp.stack(parts)
        parts = [level] + [self.hop(level, db=db) for db in range(1, self.nb)]
        level = yield jnp.stack(parts, axis=1)
        parts = [level] + [self.hop(level, da=da) for da in range(1, self.na)]
        level = yield jnp.stack(parts, axis=1)
        yield jnp.stack([level, self.hop(level, dc=1)], axis=3)


def turned_lanes(values):
    return pltpu.roll(values, HEAD_DIM // 2, 1)


def head_probabilities(query, key, length):
    scores = dot(query, key, ((1,), (1,))) / math.sqrt(HEAD_DIM)
    query_place = lax.broadcasted_iota(jnp.int32, scores.shape, 0)
    key_place = lax.broadcasted_iota(jnp.int32, scores.shape, 1)
    allowed = (key_place <= query_place) & (key_place < length)
    scores = jnp.where(allowed, scores, -1e30)
    exponent = jnp.exp(scores - jnp.max(scores, axis=1, keepdims=True))
    return exponent / jnp.sum(exponent, axis=1, keepdims=True)


def home_rows(here, sequence, sequences, rows):
    return pl.ds(pl.multiple_of(lax.rem(here[1] - sequence + sequences, sequences) * rows, rows), rows)


def attention_kernel(sequences, heads, here, raw, bias, cosine, signed_sine, low, context):
    rows = cosine.shape[0]
    width = heads * HEAD_DIM
    for sequence in range(sequences):
        at = slice(sequence * rows, (sequence + 1) * rows)
        home = home_rows(here, sequence, sequences, rows)
        length = here[2 + pl.program_id(0) * sequences + sequence]
        for head in range(heads):
            parts = []
            for part in range(3):
                low_lane = part * width + head * HEAD_DIM
                lanes = slice(low_lane, low_lane + HEAD_DIM)
                values = raw[at, lanes] + bias[:, lanes]
                if part < 2:
                    values = values * cosine[...] + turned_lanes(values) * signed_sine[...]
                values = values.astype(bf16)
                low[at, lanes] = values
                parts.append(values)
            probabilities = head_probabilities(parts[0], parts[1], length).astype(bf16)
            lanes = slice(head * HEAD_DIM, (head + 1) * HEAD_DIM)
            context[home, lanes] = dot(probabilities, parts[2], ((1,), (0,))).astype(bf16)


def attention_grad_kernel(
    sequences, heads, here, low, incoming, cosine, sine, sign, outgoing, bias_grad
):
    rows = cosine.shape[0]
    width = heads * HEAD_DIM
    root_size = math.sqrt(HEAD_DIM)

    @pl.when(pl.program_id(0) == 0)
    def _():
        bias_grad[...] = jnp.zeros_like(bias_grad)

    for sequence in range(sequences):
        at = slice(sequence * rows, (sequence + 1) * rows)
        home = home_rows(here, sequence, sequences, rows)
        length = here[2 + pl.program_id(0) * sequences + sequence]
        for head in range(heads):
            lanes = [
                slice(part * width + head * HEAD_DIM, part * width + (head + 1) * HEAD_DIM)
                for part in range(3)
            ]
            query, key, value = (low[at, part] for part in lanes)
            grad = incoming[home, lanes[0]]
            probabilities = head_probabilities(query, key, length)
            probs_grad = dot(grad, value, ((1,), (1,)))
            inner = jnp.sum(probabilities * probs_grad, axis=1, keepdims=True)
            score_grad = (probabilities * (probs_grad - inner)).astype(bf16)
            grads = [
                dot(score_grad, key, ((1,), (0,))) / root_size,
                dot(score_grad, query, ((0,), (0,))) / root_size,
                dot(probabilities.astype(bf16), grad, ((0,), (0,))),
            ]
            for part in range(3):
                values = grads[part]
                if part < 2:
                    values = values * cosine[...] - turned_lanes(values * sine[...]) * sign[...]
                values = values.astype(bf16)
                outgoing[at, lanes[part]] = values
                bias_grad[:, lanes[part]] += jnp.sum(values.astype(f32), axis=0, keepdims=True)


def rope_inputs(row_count):
    cosine, sine = (table[:, 0] for table in rope_tables(row_count, HEAD_DIM))
    sign = jnp.where(jnp.arange(HEAD_DIM) < HEAD_DIM // 2, -1.0, 1.0).astype(f32)[None]
    return cosine, sine, sign


def attention(here, raw, bias, rows, sequences, heads):
    tokens, width = raw.shape[0], heads * HEAD_DIM
    cosine, sine, sign = rope_inputs(rows)
    block = sequences * rows
    lines = tokens // block
    whole = lambda *shape: pl.BlockSpec(shape, lambda i, here: (0, 0))
    return pl.pallas_call(
        functools.partial(attention_kernel, sequences, heads),
        out_shape=[
            jax.ShapeDtypeStruct((tokens, 3 * width), bf16),
            jax.ShapeDtypeStruct((tokens, width), bf16),
        ],
        grid_spec=pltpu.PrefetchScalarGridSpec(
            num_scalar_prefetch=1,
            grid=(lines,),
            in_specs=[
                pl.BlockSpec((block, 3 * width), lambda i, here: (i, 0)),
                whole(1, 3 * width),
                whole(rows, HEAD_DIM),
                whole(rows, HEAD_DIM),
            ],
            out_specs=[
                pl.BlockSpec((block, 3 * width), lambda i, here: (i, 0)),
                pl.BlockSpec((block, width), lambda i, here: (lax.rem(here[0] - i + lines, lines), 0)),
            ],
        ),
        cost_estimate=pl.CostEstimate(
            flops=4 * tokens * rows * width, bytes_accessed=tokens * width * 20, transcendentals=0
        ),
    )(here, raw, bias, cosine, sine * sign)


def attention_grad(here, low, incoming, rows, sequences, heads):
    tokens, width = low.shape[0], heads * HEAD_DIM
    block = sequences * rows
    lines = tokens // block
    whole = lambda *shape: pl.BlockSpec(shape, lambda i, here: (0, 0))
    return pl.pallas_call(
        functools.partial(attention_grad_kernel, sequences, heads),
        out_shape=[
            jax.ShapeDtypeStruct((tokens, 3 * width), bf16),
            jax.ShapeDtypeStruct((1, 3 * width), f32),
        ],
        grid_spec=pltpu.PrefetchScalarGridSpec(
            num_scalar_prefetch=1,
            grid=(lines,),
            in_specs=[
                pl.BlockSpec((block, 3 * width), lambda i, here: (i, 0)),
                pl.BlockSpec((block, width), lambda i, here: (lax.rem(here[0] - i + lines, lines), 0)),
                whole(rows, HEAD_DIM),
                whole(rows, HEAD_DIM),
                whole(1, HEAD_DIM),
            ],
            out_specs=[
                pl.BlockSpec((block, 3 * width), lambda i, here: (i, 0)),
                whole(1, 3 * width),
            ],
        ),
        cost_estimate=pl.CostEstimate(
            flops=10 * tokens * rows * width, bytes_accessed=tokens * width * 14, transcendentals=0
        ),
    )(here, low, incoming, *rope_inputs(rows))


def pack_kernel(count, moves, blanks, order, *refs):
    sources, out, sem = refs[:count], refs[-2], refs[-1]
    copies = []
    for n, (source, low, size, to) in enumerate(moves):
        if to < 0:
            to = pl.multiple_of(order[-1 - to] * size, size)
        copies.append(
            pltpu.make_async_copy(
                sources[source].at[pl.ds(low, size), :], out.at[pl.ds(to, size), :], sem.at[n]
            )
        )
    for copy in copies:
        copy.start()
    for at, size in blanks:
        out[at : at + size, :] = jnp.zeros((size, out.shape[1]), out.dtype)
    for copy in copies:
        copy.wait()


def pack(pieces, step=1, size=None, order=None):
    moves, blanks, at = [], [], 0
    for n, piece in enumerate(pieces):
        rows = piece.shape[0]
        if order is None:
            moves.append((n, 0, rows, at))
        else:
            moves += [(n, low, size, -1 - len(moves) - low // size) for low in range(0, rows, size)]
        at += rows
        if at % step:
            blanks.append((at, -at % step))
            at += -at % step
    if order is None:
        order = jnp.zeros((1,), jnp.int32)
    return pl.pallas_call(
        functools.partial(pack_kernel, len(pieces), moves, blanks),
        out_shape=jax.ShapeDtypeStruct((at, pieces[0].shape[1]), pieces[0].dtype),
        in_specs=[pl.BlockSpec(memory_space=pltpu.SMEM)]
        + [pl.BlockSpec(memory_space=pl.ANY)] * len(pieces),
        out_specs=pl.BlockSpec(memory_space=pltpu.VMEM),
        scratch_shapes=[pltpu.SemaphoreType.DMA((len(moves),))],
        compiler_params=pltpu.CompilerParams(vmem_limit_bytes=VMEM),
        cost_estimate=pl.CostEstimate(
            flops=0, bytes_accessed=4 * at * pieces[0].shape[1], transcendentals=0
        ),
    )(order, *pieces)


def experts_kernel(blocks, start, expert, meta, vector, *refs):
    row_blocks, grad_blocks = refs[:blocks], refs[blocks : 2 * blocks]
    into_hbm, down_hbm = refs[2 * blocks : 2 * blocks + 2]
    refs = refs[2 * blocks + 2 :]
    unit_outs, refs = refs[:3], refs[3:]
    rest = blocks // CORES
    term_outs, vector_grad, refs = refs[: rest + 1], refs[rest + 1], refs[rest + 2 :]
    rows, grads, into, down, middle_all, gate_all, up_all = refs[:7]
    in_sem, weight_sem, out_sem, term_sem = refs[7:11]
    tokens, features = rows.shape
    units = down.shape[0]
    count = tokens // blocks
    tiles = [(low, min(low + TILE, units)) for low in range(0, units, TILE)]

    loads = [
        [
            pltpu.make_async_copy(
                block, held.at[pl.ds(n * count, count), :], in_sem.at[which, n]
            )
            for n, block in enumerate(arrived)
        ]
        for which, (arrived, held) in enumerate(((row_blocks, rows), (grad_blocks, grads)))
    ]
    weights = [
        [
            pltpu.make_async_copy(
                source.at[pl.ds(first + low, high - low), :],
                held.at[pl.ds(first + low, high - low), :],
                weight_sem.at[tile, which],
            )
            for which, (source, held, first) in enumerate(
                ((into_hbm, into, 0), (into_hbm, into, units), (down_hbm, down, 0))
            )
        ]
        for tile, (low, high) in enumerate(tiles)
    ]
    for copy in loads[0] + weights[0] + loads[1]:
        copy.start()
    for tile in weights[1:]:
        for copy in tile:
            copy.start()

    here = expert[0].astype(f32)
    columns = []
    for core in range(meta.shape[1]):
        for line in range(meta.shape[0]):
            told = meta[line, core]
            scale = jnp.zeros((1, count), f32)
            for k in range(TOP):
                hit = told[k : k + 1] == here
                scale = scale + jnp.where(hit, told[TOP + k : TOP + k + 1], 0.0)
            columns.append(jnp.transpose(jnp.broadcast_to(scale, (count, count)))[:, :1])
    routed_scale = jnp.concatenate(columns, axis=0)

    for copy in loads[0]:
        copy.wait()
    logit = jnp.sum(rows[...].astype(f32) * vector[...], axis=1, keepdims=True)
    shared_scale = jax.nn.sigmoid(logit)
    inner = jnp.zeros((tokens, 1), f32)
    stores = []
    for tile, (low, high) in enumerate(tiles):
        for copy in weights[tile]:
            copy.wait()
        gate = dot(rows[...], into[low:high, :], ((1,), (1,)))
        up = dot(rows[...], into[units + low : units + high, :], ((1,), (1,)))
        if tile == 0:
            for copy in loads[1]:
                copy.wait()
        back = dot(grads[...], down[low:high, :], ((1,), (1,)))
        gate_sigmoid = jax.nn.sigmoid(gate)
        silu = gate * gate_sigmoid
        middle = silu * up
        unit = lax.broadcasted_iota(jnp.int32, (1, high - low), 1) + low
        if high <= start:
            scale = routed_scale
        elif low >= start:
            scale = shared_scale
        else:
            scale = jnp.where(unit < start, routed_scale, shared_scale)
        if high > start:
            product = middle * back
            if low < start:
                product = jnp.where(unit < start, 0.0, product)
            inner = inner + jnp.sum(product, axis=1, keepdims=True)
        back = back * scale
        middle_all[:, low:high] = (middle * scale).astype(bf16)
        gate_all[:, low:high] = (back * up * (gate_sigmoid + silu * (1.0 - gate_sigmoid))).astype(
            bf16
        )
        up_all[:, low:high] = (back * silu).astype(bf16)
        for which, (held, out) in enumerate(zip((middle_all, gate_all, up_all), unit_outs)):
            lanes = pl.ds(low, high - low)
            copy = pltpu.make_async_copy(
                held.at[:, lanes], out.at[:, lanes], out_sem.at[tile, which]
            )
            copy.start()
            stores.append(copy)

    @pl.when(expert[1] == 1)
    def _():
        terms = refs[11]
        logit_grad = inner * shared_scale * (1.0 - shared_scale)
        for low in range(0, features, TILE):
            lanes = slice(low, low + TILE)
            value = dot(gate_all[...], into[:units, lanes], ((1,), (0,)))
            value = value + dot(up_all[...], into[units:, lanes], ((1,), (0,)))
            value = (value + logit_grad * vector[:, lanes]).astype(bf16)
            result = dot(middle_all[...], down[:, lanes], ((1,), (0,))).astype(bf16)
            for n in range(blocks):
                at = slice(n * count, (n + 1) * count)
                terms[2 * n * count : (2 * n + 1) * count, lanes] = value[at]
                terms[(2 * n + 1) * count : (2 * n + 2) * count, lanes] = result[at]
        at, copies = 0, []
        for n, out in enumerate(term_outs):
            copies.append(
                pltpu.make_async_copy(terms.at[pl.ds(at, out.shape[0]), :], out, term_sem.at[n])
            )
            at += out.shape[0]
        for copy in copies:
            copy.start()
        vector_grad[...] = jnp.sum(rows[...].astype(f32) * logit_grad, axis=0, keepdims=True)
        for copy in copies:
            copy.wait()

    for copy in stores:
        copy.wait()


def experts(expert, meta, vector, rows, grads, into, down, routed):
    blocks = len(rows)
    count, features = rows[0].shape
    tokens, units, rest = blocks * count, down.shape[0], blocks // CORES
    tiles = -(-units // TILE)
    anywhere = pl.BlockSpec(memory_space=pl.ANY)
    inside = pl.BlockSpec(memory_space=pltpu.VMEM)
    out_shape = [jax.ShapeDtypeStruct((tokens, units), bf16)] * 3
    out_specs = [anywhere] * 3
    scratch = [
        pltpu.VMEM((tokens, features), bf16),
        pltpu.VMEM((tokens, features), bf16),
        pltpu.VMEM(into.shape, bf16),
        pltpu.VMEM(down.shape, bf16),
        pltpu.VMEM((tokens, units), bf16),
        pltpu.VMEM((tokens, units), bf16),
        pltpu.VMEM((tokens, units), bf16),
        pltpu.SemaphoreType.DMA((2, blocks)),
        pltpu.SemaphoreType.DMA((tiles, 3)),
        pltpu.SemaphoreType.DMA((tiles, 3)),
        pltpu.SemaphoreType.DMA((rest + 1,)),
    ]
    out_shape += [jax.ShapeDtypeStruct((2 * count, features), bf16)] * rest
    out_shape += [jax.ShapeDtypeStruct((2 * (tokens - rest * count), features), bf16)]
    out_shape += [jax.ShapeDtypeStruct((1, features), f32)]
    out_specs += [anywhere] * (rest + 1) + [inside]
    scratch += [pltpu.VMEM((2 * tokens, features), bf16)]
    return pl.pallas_call(
        functools.partial(experts_kernel, blocks, routed + -routed % LANES),
        out_shape=out_shape,
        in_specs=[pl.BlockSpec(memory_space=pltpu.SMEM), inside, inside]
        + [anywhere] * (2 * blocks + 2),
        out_specs=out_specs,
        scratch_shapes=scratch,
        compiler_params=pltpu.CompilerParams(vmem_limit_bytes=VMEM),
        cost_estimate=pl.CostEstimate(
            flops=2 * tokens * features * units * 4,
            bytes_accessed=2 * (into.size + down.size + 4 * tokens * features),
            transcendentals=0,
        ),
    )(expert, meta, vector, *rows, *grads, into, down)


def weight_grad_kernel(unit_counts, row_counts, first, second, start, adds, *refs):
    some, pieces = len(unit_counts), len(unit_counts) + len(row_counts)
    units, rows = refs[:some], refs[some:pieces]
    before = refs[pieces : pieces + 2] if adds else (None, None)
    first_out, second_out, held, tiles, held_sem, tile_sem = refs[pieces + 2 * adds :]
    width = tiles.shape[-1]
    step = pl.program_id(0)
    slot = lax.rem(step, 2)
    unit_places, row_places = (
        [pl.ds(sum(counts[:n]), count) for n, count in enumerate(counts)]
        for counts in (unit_counts, row_counts)
    )

    def held_copies():
        return [
            pltpu.make_async_copy(units[n], held.at[at, :], held_sem.at[n])
            for n, at in enumerate(unit_places)
        ]

    def tile_copies(index, into):
        columns = pl.ds(pl.multiple_of(index * width, width), width)
        return [
            pltpu.make_async_copy(
                rows[n].at[:, columns], tiles.at[into, at, :], tile_sem.at[into, n]
            )
            for n, at in enumerate(row_places)
        ]

    @pl.when(step == 0)
    def _():
        for copy in held_copies() + tile_copies(0, 0):
            copy.start()
        for copy in held_copies():
            copy.wait()

    for copy in tile_copies(step, slot):
        copy.wait()

    @pl.when(step + 1 < pl.num_programs(0))
    def _():
        for copy in tile_copies(step + 1, 1 - slot):
            copy.start()

    for low, size, out, earlier in (
        (0, first, first_out, before[0]),
        (start, second, second_out, before[1]),
    ):
        value = dot(held[:, low : low + size], tiles[slot], ((0,), (0,)))
        out[...] = earlier[...] + value if adds else value


def weight_grad(units, rows, first, second, before=()):
    unit_counts = [piece.shape[0] for piece in units]
    row_counts = [piece.shape[0] for piece in rows]
    pieces, tokens = len(units) + len(rows), sum(row_counts)
    features, all_units = rows[0].shape[1], units[0].shape[1]
    start = first + -first % LANES
    adds = int(bool(before))
    anywhere = pl.BlockSpec(memory_space=pl.ANY)
    blocks = [pl.BlockSpec((size, TILE), lambda i: (0, i)) for size in (first, second)]
    return pl.pallas_call(
        functools.partial(weight_grad_kernel, unit_counts, row_counts, first, second, start, adds),
        grid=(features // TILE,),
        out_shape=[jax.ShapeDtypeStruct((size, features), f32) for size in (first, second)],
        in_specs=[anywhere] * pieces + blocks * adds,
        out_specs=blocks,
        scratch_shapes=[
            pltpu.VMEM((tokens, all_units), bf16),
            pltpu.VMEM((2, tokens, TILE), bf16),
            pltpu.SemaphoreType.DMA((len(units),)),
            pltpu.SemaphoreType.DMA((2, len(rows))),
        ],
        input_output_aliases={pieces: 0, pieces + 1: 1} if adds else {},
        compiler_params=pltpu.CompilerParams(vmem_limit_bytes=VMEM),
        cost_estimate=pl.CostEstimate(
            flops=2 * tokens * features * (first + second),
            bytes_accessed=tokens * (features + all_units) * 2
            + features * (first + second) * 4 * (1 + adds),
            transcendentals=0,
        ),
    )(*units, *rows, *before)


def local(
    layer_input,
    lengths,
    routes,
    route_weight,
    cotangent,
    norm_gain,
    w_qkv,
    b_qkv,
    w_out,
    post_gain,
    w_gate,
    w_up,
    w_down,
    shared_gate,
    shared_up,
    shared_down,
    shared_vector,
):
    grid = Grid()
    row_count, feature_count = layer_input.shape
    groups, owners, chips, na, nb = grid.groups, grid.owners, grid.chips, grid.na, grid.nb
    devices = groups * owners
    heads_here = HEADS // chips
    width = heads_here * HEAD_DIM
    own_rows = w_qkv.shape[0]
    sizes = (w_gate.shape[2], shared_gate.shape[1])
    positions = jnp.arange(row_count, dtype=jnp.int32)
    slots = range(na)
    two = groups == 2

    class Rounds:
        def __init__(self, block):
            self.far, self.blocks = [block], []

        def row(self):
            if len(self.blocks) < na:
                self.blocks.append(grid.row(self.far[len(self.blocks)]))

        def line(self):
            if len(self.far) < na:
                self.far.append(grid.hop(self.far[-1], da=1))

        def all(self):
            return [block for blocks in self.blocks for block in blocks]

    def tie_rounds(rounds, *values):
        state = [(r.far, r.blocks) for r in rounds]
        state, *values = tie(state, *values)
        for r, (far, blocks) in zip(rounds, state):
            r.far, r.blocks = far, blocks
        return values

    def place_of(da, db, dc, dg):
        group = (grid.group - dg) % groups
        chip = (grid.a - da) % na * nb + (grid.b - db) % nb
        return (group * chips + chip) * CORES + (grid.core + dc) % CORES

    def other_core(blocks):
        return [grid.hop(block, dc=1) for block in blocks]

    small = jnp.concatenate([norm_gain, post_gain, shared_vector, b_qkv]).astype(f32)
    small_count = small.shape[0]
    small = jnp.pad(small, (0, -small_count % row_count))
    meta = jnp.concatenate(
        [
            routes.T.astype(f32),
            route_weight.T.astype(f32),
            jnp.broadcast_to(lengths.astype(f32)[:, None], (1, row_count)),
            small.reshape(-1, row_count),
        ],
        axis=0,
    )
    telling = grid.everywhere(meta)

    x_rounds = Rounds(layer_input)
    x_rounds.line()
    x_rounds.row()
    sliced = jnp.transpose(w_qkv.reshape(own_rows, 3, chips, width), (2, 0, 1, 3))
    by_chip = grid.swap(sliced.reshape(chips, own_rows, 3 * width))
    level = next(telling)
    into_in = [w_gate, shared_gate, w_up, shared_up]
    down_in = [w_down, shared_down]
    level, w_out, into_in = tie_rounds([x_rounds], level, w_out, into_in)

    out_pairs, out_far = [jnp.concatenate(grid.row(w_out), axis=0)], []

    def out_line():
        if len(out_pairs) < na:
            out_pairs.append(grid.hop(out_pairs[-1], da=1))

    def out_cross():
        if len(out_far) < len(out_pairs):
            pair = out_pairs[len(out_far)]
            out_far.append([grid.cross(pair, shift) for shift in range(1, groups)])

    def tie_out(rounds, *values):
        nonlocal out_pairs, out_far
        out_pairs, out_far, *values = tie_rounds(rounds, out_pairs, out_far, *values)
        return values

    x_rounds.line()
    x_rounds.row()
    level = telling.send(level)
    into_rows = pack(
        [into_in[0][0].T, into_in[1].T, into_in[2][0].T, into_in[3].T], LANES
    )
    by_chip, level, into_rows, down_in = tie_out(
        [x_rounds], by_chip, level, into_rows, down_in
    )
    by_chip = by_chip.reshape(chips * own_rows, 3 * width)
    x_rounds.line()
    x_rounds.row()
    level = telling.send(level)
    by_group = [by_chip] + [grid.cross(by_chip, shift) for shift in range(1, groups)]
    down_rows = pack([down_in[0][0], down_in[1]], LANES)
    out_line()
    by_group, level, down_rows = tie_out([x_rounds], by_group, level, down_rows)
    weight_pieces, order = [], []
    for shift, piece in enumerate(by_group):
        for core in range(CORES):
            weight_pieces.append(grid.hop(piece, dc=1) if core else piece)
            for chip in range(chips):
                order.append(
                    ((grid.group - shift) % groups * chips + chip) * CORES
                    + (grid.core + core) % CORES
                )
    meta_all = telling.send(level)
    flat_meta = meta_all.reshape(devices, *meta.shape)
    index = jnp.arange(devices, dtype=jnp.int32)
    ig, ia, ib, ic = (
        index // owners,
        index // (nb * CORES) % na,
        index // CORES % nb,
        index % CORES,
    )
    from_here = (
        ((grid.group - ig) % groups * na + (grid.a - ia) % na) * nb + (grid.b - ib) % nb
    ) * CORES + (grid.core - ic) % CORES
    small_all = jnp.take(flat_meta[:, 2 * TOP + 1 :], from_here, axis=0).reshape(devices, -1)
    own_features = norm_gain.shape[0]
    gains_in = small_all[:, :own_features].reshape(-1)
    gains_post = small_all[:, own_features : 2 * own_features].reshape(-1)
    gate_vector = small_all[:, 2 * own_features : 3 * own_features].reshape(-1)
    qkv_bias = small_all[:, 3 * own_features : small_count].reshape(3, chips, width)
    bias_here = lax.dynamic_index_in_dim(qkv_bias, grid.chip, 1, keepdims=False).reshape(-1)
    plane_lengths = meta_all[0, :, :, 0, 2 * TOP, 0].reshape(chips).astype(jnp.int32)
    here = jnp.concatenate([jnp.stack([grid.a, grid.b]).astype(jnp.int32), plane_lengths])
    while len(x_rounds.blocks) < na:
        x_rounds.row()
    out_line()
    out_cross()
    heads_weight = pack(weight_pieces, size=own_rows, order=jnp.stack(order).astype(jnp.int32))
    normed_first = pack(
        [(unit_norm(block.astype(f32))[0] * gains_in).astype(bf16) for block in x_rounds.all()]
    )
    normed_first, heads_weight, bias_here, gains_in, cotangent, here = tie_out(
        [], normed_first, heads_weight, bias_here, gains_in, cotangent, here
    )

    valid_rows = positions < lengths[0]
    grad_rows = jnp.where(valid_rows[:, None], cotangent, jnp.zeros_like(cotangent))
    inputs = layer_input.astype(f32)
    grad_rounds = Rounds(grad_rows)
    while len(out_pairs) < na:
        out_line()
    out_cross()
    grad_rounds.line()
    grad_rounds.row()
    projected = dot(normed_first, heads_weight, ((1,), (0,)))
    low, sent = attention(here, projected, bias_here[None], row_count, nb, heads_here)
    low, sent = tie_out([grad_rounds], low, sent)

    grad_rounds.line()
    grad_rounds.row()
    while len(out_far) < na:
        out_cross()
    pieces, order = [], []
    for dc in range(CORES):
        for da in slots:
            for dg in range(groups):
                pair = out_far[da][dg - 1] if dg else out_pairs[da]
                pieces.append(grid.hop(pair, dc=1) if dc else pair)
                order += [place_of(da, db, dc, dg) for db in range(nb)]
    out_weight = pack(pieces, size=own_rows, order=jnp.stack(order).astype(jnp.int32))
    arrived = grid.swap(sent.reshape(chips, row_count, width))
    arrived, out_weight = tie_rounds([grad_rounds], arrived, out_weight)

    far_grads, far_rows = [], []
    crossings = [("grads", s) for s in slots] + [("rows", s) for s in slots]

    def cross_step():
        if crossings and two:
            what, s = crossings[0]
            source, goes = (
                (grad_rounds, far_grads) if what == "grads" else (second_rounds, far_rows)
            )
            if s < len(source.blocks):
                crossings.pop(0)
                goes.append([grid.cross(block, 1) for block in source.blocks[s]])

    grad_rounds.line()
    grad_rounds.row()
    context = jnp.transpose(arrived, (1, 0, 2)).reshape(row_count, feature_count)
    residual = inputs + dot(context, out_weight, ((1,), (0,)))
    unit_second, factor_second = unit_norm(residual)
    normed_second = (unit_second * gains_post).astype(bf16)

    expert = (lax.axis_index("ep") // HALVES).astype(jnp.int32)
    expert, far_expert = (jnp.stack([expert, jnp.int32(n)]) for n in (1, 0))
    vector_row = gate_vector[None]
    told = meta_all[..., : 2 * TOP, :]
    second_rounds = Rounds(normed_second)
    own = {"rows": [], "grads": [], "middle": [], "gate": [], "up": [], "vector": []}

    def work(s):
        own["rows"].append(second_rounds.blocks[s] + other_core(second_rounds.blocks[s]))
        own["grads"].append(grad_rounds.blocks[s] + other_core(grad_rounds.blocks[s]))
        middle, gate, up, *terms, vector = experts(
            expert, told[0, s], vector_row, own["rows"][s], own["grads"][s],
            into_rows, down_rows, sizes[0],
        )
        for name, value in (("middle", middle), ("gate", gate), ("up", up), ("vector", vector)):
            own[name].append(value)
        return terms

    def add_cores(terms):
        arriving = grid.hop(terms[-1], dc=1)
        return [
            (
                terms[t].astype(f32)
                + arriving[2 * t * row_count : 2 * (t + 1) * row_count].astype(f32)
            ).astype(bf16)
            for t in range(nb)
        ]

    def step_tie(*values):
        nonlocal own, far_grads, far_rows, into_rows, down_rows
        own, far_grads, far_rows, into_rows, down_rows, *values = tie_rounds(
            [grad_rounds, second_rounds], own, far_grads, far_rows, into_rows, down_rows, *values
        )
        return values

    def line_sum(rowed, sums, s):
        total = rowed[s] if sums is None else rowed[s] + sums.astype(f32)
        return grid.hop(total.astype(bf16), da=1) if s else total

    def far_work(shift, s):
        rows = far_rows[s] + other_core(far_rows[s])
        grads = far_grads[s] + other_core(far_grads[s])
        units = experts(
            far_expert, told[shift, s], vector_row, rows, grads,
            into_rows, down_rows, sizes[0],
        )
        return rows, grads, units[:3]

    def flat(lists):
        return [block for blocks in lists for block in blocks]

    rowed, terms, far = {}, {}, []
    sums = None
    second_rounds.line()
    second_rounds.row()
    cross_step()
    for s in slots:
        grad_rounds.line()
        grad_rounds.row()
        second_rounds.line()
        second_rounds.row()
        if s:
            cross_step()
            cross_step()
        if s >= 2:
            rowed[s - 1] = grid.row_sum(add_cores(terms[s - 1]))
        if s >= 3:
            sums = line_sum(rowed, sums, s - 2)
        terms[s] = work(s)
        rowed, terms, sums = step_tie(rowed, terms, sums)
    cross_step()
    rowed[na - 1] = grid.row_sum(add_cores(terms[na - 1]))
    if na > 2:
        sums = line_sum(rowed, sums, na - 2)
    own_gate = weight_grad(own["gate"], flat(own["rows"]), *sizes)
    rowed, terms, sums, own_gate = step_tie(rowed, terms, sums, own_gate)
    while crossings and two:
        cross_step()
    sums = line_sum(rowed, sums, na - 1)
    rowed[0] = grid.row_sum(add_cores(terms[0]))
    own_up = weight_grad(own["up"], flat(own["rows"]), *sizes)
    if two:
        far.append(far_work(1, 0))
    rowed, sums, own_up, far = step_tie(rowed, sums, own_up, far)

    both_sums = line_sum(rowed, sums, 0)
    second_grad = both_sums[:row_count]
    outs = residual + both_sums[row_count:]
    output = jnp.where(valid_rows[:, None], outs, 0.0).astype(bf16)
    grad_float = grad_rows.astype(f32)
    post_gain_grad = jnp.sum(second_grad * unit_second, axis=0)
    residual_grad = grad_float + norm_backward(
        second_grad, unit_second, factor_second, gains_post
    )
    attended_grad = residual_grad.astype(bf16)
    context_grad = dot(attended_grad, out_weight, ((1,), (1,))).astype(bf16)
    sent = jnp.transpose(context_grad.reshape(row_count, chips, width), (1, 0, 2))
    arrived = grid.swap(sent)
    own_down = weight_grad(own["middle"], flat(own["grads"]), *sizes)
    if two:
        far.append(far_work(1, 1))
    arrived, own_down, attended_grad, far = step_tie(arrived, own_down, attended_grad, far)

    def own_features_of(values, core, group):
        parts = values.reshape(row_count, groups, chips, CORES, own_rows)
        parts = lax.dynamic_index_in_dim(parts, core, 3, keepdims=False)
        parts = lax.dynamic_index_in_dim(parts, group, 1, keepdims=False)
        return parts.reshape(row_count, chips * own_rows)

    projected_grad, bias_here_grad = attention_grad(
        here, low, arrived.reshape(-1, width), row_count, nb, heads_here
    )
    first_terms = dot(projected_grad, heads_weight, ((1,), (1,))).astype(bf16)
    out_parts = []
    for shift in range(groups):
        group = (grid.group + shift) % groups
        mine, other = (
            dot(own_features_of(context, core, group), attended_grad, ((0,), (0,))).astype(bf16)
            for core in (grid.core, 1 - grid.core)
        )
        total = mine.astype(f32) + grid.hop(other, dc=1).astype(f32)
        out_parts.append(total.astype(bf16))
    first_terms, projected_grad, out_parts, far = step_tie(
        first_terms, projected_grad, out_parts, far
    )

    slot_first = first_terms.reshape(na, nb, row_count, feature_count)
    totals = [[own_gate, own_up, own_down]]

    def end_tie(*values):
        nonlocal far, far_rows, far_grads, into_rows, down_rows, own, totals
        far, far_rows, far_grads, into_rows, down_rows, own, totals, *values = tie(
            far, far_rows, far_grads, into_rows, down_rows, own, totals, *values
        )
        return values

    def far_grad(units, place):
        before = totals[0][units] if two else ()
        return weight_grad(
            [work[2][(1, 2, 0)[units]] for work in far], flat(work[place] for work in far),
            *sizes, before,
        )

    first_rowed = {s: grid.row_sum(slot_first[s]) for s in range(1, na - 1)}
    qkv_grad = dot(normed_first, projected_grad, ((0,), (0,))).astype(bf16)
    half = chips * own_rows // 2
    crossed = [[grid.cross(part[:half], n + 1)] for n, part in enumerate(out_parts[1:])]
    if two:
        far.append(far_work(1, 2))
    first_rowed, slot_first, qkv_grad, crossed, out_parts = end_tie(
        first_rowed, slot_first, qkv_grad, crossed, out_parts
    )
    for s in sorted({na - 1, 0}):
        first_rowed[s] = grid.row_sum(slot_first[s])
    first_sums = line_sum(first_rowed, None, 1)
    for n, part in enumerate(out_parts[1:]):
        crossed[n].append(grid.cross(part[half:], n + 1))
    qkv_grad = grid.scatter_core(qkv_grad.reshape(groups, chips, CORES, own_rows, 3 * width), 2)
    if two:
        far.append(far_work(1, 3 % na))
    first_rowed, qkv_grad, crossed, out_parts, first_sums = end_tie(
        first_rowed, qkv_grad.astype(bf16), crossed, out_parts, first_sums
    )
    for s in range(2, na):
        first_sums = line_sum(first_rowed, first_sums, s)
    qkv_grad = grid.scatter_groups(qkv_grad).astype(bf16)
    out_total = out_parts[0].astype(f32)
    for halves in crossed:
        out_total = out_total + jnp.concatenate(halves, axis=0).astype(f32)
    out_rowed = grid.scatter_row(
        out_total.astype(bf16).reshape(na, nb, own_rows, feature_count)
    )
    if two:
        gate_total = far_grad(0, 0)
        first_sums, qkv_grad, out_rowed, gate_total = end_tie(
            first_sums, qkv_grad, out_rowed, gate_total
        )
    first_grad = line_sum(first_rowed, first_sums, 0)
    unit_first, factor_first = unit_norm(inputs)
    input_part = norm_backward(first_grad, unit_first, factor_first, gains_in)
    layer_grad = (residual_grad + input_part).astype(bf16)
    out_weight_grad = grid.scatter_line(out_rowed)
    qkv_grad = grid.swap(qkv_grad).reshape(chips, own_rows, 3, width)
    if two:
        up_total = far_grad(1, 0)
        qkv_grad, out_weight_grad, up_total, layer_grad = end_tie(
            qkv_grad, out_weight_grad, up_total, layer_grad
        )
    qkv_weight_grad = jnp.transpose(qkv_grad, (1, 2, 0, 3)).reshape(own_rows, -1).astype(f32)
    if two:
        totals.append([gate_total, up_total, far_grad(2, 1)])
    else:
        second_blocks, grad_blocks = second_rounds.blocks, grad_rounds.blocks
        for shift in range(1, groups):
            totals, second_blocks, grad_blocks = tie(totals, second_blocks, grad_blocks)
            far_grads, far_rows = (
                [[grid.cross(block, shift) for block in blocks] for blocks in source]
                for source in (grad_blocks, second_blocks)
            )
            far = [far_work(shift, s) for s in slots]
            totals.append([far_grad(0, 0), far_grad(1, 0), far_grad(2, 1)])

        def ordered(*parts):
            total = 0.0
            for group in range(groups):
                far_by = (grid.group - group) % groups
                total = total + sum(
                    jnp.where(far_by == shift, part, 0.0) for shift, part in enumerate(parts)
                )
            return total

        totals.append(jax.tree.map(ordered, *totals))
    (
        (gate_grad, shared_gate_grad),
        (up_grad, shared_up_grad),
        (down_grad, shared_down_grad),
    ) = totals[-1]

    vector_grad = sum(own["vector"])[0]
    gain_grad = jnp.sum(first_terms.astype(f32) * normed_first.astype(f32), axis=0) / gains_in
    bias_grad = jnp.zeros((3, chips, width), f32)
    bias_grad = lax.dynamic_update_slice(
        bias_grad, bias_here_grad.reshape(3, 1, width), (0, grid.chip, 0)
    )
    vectors = jnp.concatenate(
        [
            gain_grad.reshape(devices, -1),
            post_gain_grad.reshape(devices, -1),
            vector_grad.reshape(devices, -1),
            bias_grad.reshape(devices, -1),
        ],
        axis=1,
    ).reshape(groups, na, nb, CORES, -1)
    vectors = grid.scatter_core(vectors, 3)
    vectors = grid.scatter_groups(vectors)
    vectors = grid.scatter_line(grid.scatter_row(vectors))
    return (
        output,
        layer_grad,
        vectors[:own_features],
        qkv_weight_grad,
        vectors[3 * own_features :],
        out_weight_grad,
        vectors[own_features : 2 * own_features],
        gate_grad.T[None],
        up_grad.T[None],
        down_grad[None],
        shared_gate_grad.T,
        shared_up_grad.T,
        shared_down_grad,
        vectors[2 * own_features : 3 * own_features],
    )


def solution(mesh):
    rows = P(("dp", "ep"), None)
    split = P(("dp", "ep"))
    parts = P("ep", None, None)
    return jax.shard_map(
        local,
        mesh=mesh,
        in_specs=(
            rows,
            split,
            rows,
            rows,
            rows,
            split,
            rows,
            split,
            rows,
            split,
            parts,
            parts,
            parts,
            P(None, "ep"),
            P(None, "ep"),
            P("ep", None),
            split,
        ),
        out_specs=(
            rows,
            rows,
            split,
            rows,
            split,
            rows,
            split,
            parts,
            parts,
            parts,
            P(None, "ep"),
            P(None, "ep"),
            P("ep", None),
            split,
        ),
        check_vma=False,
    )
```

time: 1170 us -> 801 us (0.68)
  Pallas kernels: 0 us -> 319 us
  matrix products: 301 us -> 29.9 us
  waiting for transfers between devices: 389 us -> 209 us
  other arithmetic: 173 us -> 72.3 us
  local copies, waits for them, and re-layouts: 142 us -> 51 us
  starting transfers between devices: 141 us -> 105 us
  between operations: 17.9 us -> 3.41 us
    pallas_call x0 -> x21, Pallas kernels: none -> 319 us  [the longest x8 181 us: experts(): pl.pallas_call(functools.partial(experts_kernel, blocks, routed + -routed...]
    dot_general x51 -> x9, matrix products: 296 us -> 29.9 us  [dot(): lax.dot_general(left, right, (dims, ((), ())), preferred_element_type=f32)]
    ppermute x83 -> x102, waiting for transfers between devices: 305 us -> 142 us  [hop(): return lax.ppermute(values, 'ep', pairs)]
    concatenate x12 -> x2, other arithmetic: 127 us -> 1.43 us  [the longest x1 0.84 us: local(): out_pairs, out_far = ([jnp.concatenate(grid.row(w_out), axis=0)], [])]
    ppermute x83 -> x102, starting transfers between devices: 109 us -> 64.8 us  [hop(): return lax.ppermute(values, 'ep', pairs)]
    unnamed x365 -> x194, local copies, waits for them, and re-layouts: 68.3 us -> 26.2 us
    concatenate x9 -> x0, local copies, waits for them, and re-layouts: 13.5 us -> none  [the longest x4 7.76 us: both(): jnp.concatenate([rows, self.hop(rows, dc=1)], axis=0)]
    add x4 -> x12, other arithmetic: 3.67 us -> 17.1 us  [the longest x7 14.8 us: row_sum(): total = total + self.hop(terms[db], db=-db).astype(f32)]
  transfers between devices with their start and end apart: 101 -> 132, of which waited for: 30 -> 39; matrix products, arithmetic and copies ran while one was open for 51% -> 15% of each run, Pallas kernels for 0% -> 40%
where the time goes in v2:
time: 801 us; the launch traced here: 790 us
  Pallas kernels  319 us (40%)
  waiting for transfers between devices  209 us (26%)
  starting transfers between devices  105 us (13%)
  other arithmetic  72.3 us (9%)
  local copies, waits for them, and re-layouts  51 us (6%)
  matrix products  29.9 us (4%)
    pallas_call x8, Pallas kernels, experts(): pl.pallas_call(functools.partial(experts_kernel, blocks, routed + -routed...  181 us
    ppermute x102, waiting for transfers between devices, hop(): return lax.ppermute(values, 'ep', pairs)  142 us
    pallas_call x6, Pallas kernels, weight_grad(): pl.pallas_call(functools.partial(weight_grad_kernel, unit_counts, row_cou...  90.3 us
    ppermute x26, waiting for transfers between devices, cross(): return lax.ppermute(values, 'dp', pairs)  65.4 us
    ppermute x102, starting transfers between devices, hop(): return lax.ppermute(values, 'ep', pairs)  64.8 us
    dot_general x9, matrix products, dot(): lax.dot_general(left, right, (dims, ((), ())), preferred_element_type=f32)  29.9 us
    pallas_call x5, Pallas kernels, pack(): pl.pallas_call(functools.partial(pack_kernel, len(pieces), moves, blanks)...  28.5 us
    unnamed x194, local copies, waits for them, and re-layouts  26.2 us
  transfers between devices with their start and end apart: 132, of which 39 were waited for; matrix products, arithmetic and copies ran while one was open for 15% of the time, Pallas kernels for 40%

profile of v2, /device:TPU:0, one launch (start us, length us, event | category | flops | bytes accessed | tf_op | source)
XLA Modules:
  0.0 790.2 jit_solution(4202182721486664768)
XLA Ops:
  54.0 21.9 %collective-permute-done.13 = f32[2,2,12,128]{3,2,1,0:T(8,128)S(1)} collective-permute-done((f32[2,2,12,128]{3,2,1,0:T(8,128)S(1)}, f32[2,2,12,128]{3,2,1,0:T(8,128)S(1)}, u32[]{:S(2)}, u32[]{:S(2)}) %collective-permute-start.13) | collective-permute-done | bytes 24608 | tf_op jit(solution)/shard_map/ppermute | solution.py:78
  127.1 8.7 %shard_map.276 = (bf16[1024,768]{1,0:T(8,128)(2,1)}, bf16[1024,256]{1,0:T(8,128)(2,1)}) custom-call(s32[10]{0:T(128)} %pad_add_fusion.here, f32[1024,768]{1,0:T(8,128)} %fusion.104.raw, f32[1,768]{1,0:T(1,128)} %broadcast_in_dim.95.bias, f32[128,128]{1,0:T(8,128)} %get-tuple-element.1519.cosine, f32[128,128]{1,0:T(8,128)} %get-tuple-element.1518.signed_sine), custom_call_target="tpu_custom_call" | custom-call | flops 134217728 | bytes 5242880 | tf_op jit(solution)/shard_map/pallas_call | solution.py:241
  158.0 10.8 %collective-permute-done.27.refs_7_ = bf16[128,2048]{1,0:T(8,128)(2,1)} collective-permute-done((bf16[128,2048]{1,0:T(8,128)(2,1)S(1)}, bf16[128,2048]{1,0:T(8,128)(2,1)}, u32[]{:S(2)}, u32[]{:S(2)}) %collective-permute-start.27) | collective-permute-done | bytes 524320 | tf_op jit(solution)/shard_map/ppermute | solution.py:82
  202.3 9.3 %collective-permute-done.41.refs_1_.refs_5_ = bf16[128,2048]{1,0:T(8,128)(2,1)} collective-permute-done((bf16[128,2048]{1,0:T(8,128)(2,1)S(1)}, bf16[128,2048]{1,0:T(8,128)(2,1)}, u32[]{:S(2)}, u32[]{:S(2)}) %collective-permute-start.41) | collective-permute-done | bytes 524320 | tf_op jit(solution)/shard_map/ppermute | solution.py:78
  217.8 27.8 %shard_map.278 = (bf16[512,1152]{1,0:T(8,128)(2,1)}, bf16[512,1152]{1,0:T(8,128)(2,1)}, bf16[512,1152]{1,0:T(8,128)(2,1)}, bf16[256,2048]{1,0:T(8,128)(2,1)}, bf...) custom-call(s32[2]{0:T(128)} %pad_add_fusion.1.expert, ...), custom_call_target="tpu_custom_call" | custom-call | flops 9663676416 | bytes 22544384 | tf_op jit(solution)/shard_map/pallas_call | solution.py:501
  247.3 12.0 %collective-permute-done.57.refs_4_.refs_12_ = bf16[128,2048]{1,0:T(8,128)(2,1)} collective-permute-done((bf16[128,2048]{1,0:T(8,128)(2,1)}, bf16[128,2048]{1,0:T(8,128)(2,1)}, u32[]{:S(2)}, u32[]{:S(2)}) %collective-permute-start.57) | collective-permute-done | bytes 524320 | tf_op jit(solution)/shard_map/ppermute | solution.py:82
  262.8 27.9 %shard_map.279 = (bf16[512,1152]{1,0:T(8,128)(2,1)}, bf16[512,1152]{1,0:T(8,128)(2,1)}, bf16[512,1152]{1,0:T(8,128)(2,1)}, bf16[256,2048]{1,0:T(8,128)(2,1)}, bf...) custom-call(s32[2]{0:T(128)} %pad_add_fusion.1.expert, ...), custom_call_target="tpu_custom_call" | custom-call | flops 9663676416 | bytes 22544384 | tf_op jit(solution)/shard_map/pallas_call | solution.py:501
  306.4 27.7 %shard_map.280 = (bf16[512,1152]{1,0:T(8,128)(2,1)}, bf16[512,1152]{1,0:T(8,128)(2,1)}, bf16[512,1152]{1,0:T(8,128)(2,1)}, bf16[256,2048]{1,0:T(8,128)(2,1)}, bf...) custom-call(s32[2]{0:T(128)} %pad_add_fusion.1.expert, ...), custom_call_target="tpu_custom_call" | custom-call | flops 9663676416 | bytes 22544384 | tf_op jit(solution)/shard_map/pallas_call | solution.py:501
  340.7 10.0 %collective-permute-done.67.refs_1_.refs_5_ = bf16[128,2048]{1,0:T(8,128)(2,1)S(1)} collective-permute-done((bf16[128,2048]{1,0:T(8,128)(2,1)}, bf16[128,2048]{1,0:T(8,128)(2,1)S(1)}, u32[]{:S(2)}, u32[]{:S(2)}) %collective-permute-start.67) | collective-permute-done | bytes 524320 | tf_op jit(solution)/shard_map/ppermute | solution.py:82
  362.4 27.5 %shard_map.281 = (bf16[512,1152]{1,0:T(8,128)(2,1)}, bf16[512,1152]{1,0:T(8,128)(2,1)}, bf16[512,1152]{1,0:T(8,128)(2,1)}, bf16[256,2048]{1,0:T(8,128)(2,1)}, bf...) custom-call(s32[2]{0:T(128)} %pad_add_fusion.1.expert, ...), custom_call_target="tpu_custom_call" | custom-call | flops 9663676416 | bytes 22544384 | tf_op jit(solution)/shard_map/pallas_call | solution.py:501
  396.6 10.1 %collective-permute-done.77.refs_1_.refs_13_ = bf16[128,2048]{1,0:T(8,128)(2,1)} collective-permute-done((bf16[128,2048]{1,0:T(8,128)(2,1)}, bf16[128,2048]{1,0:T(8,128)(2,1)}, u32[]{:S(2)}, u32[]{:S(2)}) %collective-permute-start.77) | collective-permute-done | bytes 524320 | tf_op jit(solution)/shard_map/ppermute | solution.py:82
  416.7 14.3 %shard_map.282 = (f32[704,2048]{1,0:T(8,128)}, f32[352,2048]{1,0:T(8,128)}) custom-call(bf16[512,1152]{1,0:T(8,128)(2,1)} %get-tuple-element.984.refs_0_, bf16[512,1152]{1,0:T(8,128)(2,1)} %get-tuple-element.985.refs_1_, bf16[512,1152]{1,0:T(8,128)(2,1)} %get-tuple-element.986.refs_2_, bf16[512,1152]{1,0:T(8,128)(2,1)} %get-tuple-element.987.refs_3_, ...), custom_call_target="tpu_custom_call" | custom-call | flops 8858370048 | bytes 21757952 | tf_op jit(solution)/shard_map/pallas_call | solution.py:577
  446.0 14.3 %shard_map.283 = (f32[704,2048]{1,0:T(8,128)}, f32[352,2048]{1,0:T(8,128)}) custom-call(bf16[512,1152]{1,0:T(8,128)(2,1)} %get-tuple-element.1094.refs_0_, bf16[512,1152]{1,0:T(8,128)(2,1)} %get-tuple-element.1095.refs_1_, bf16[512,1152]{1,0:T(8,128)(2,1)} %get-tuple-element.1096.refs_2_, bf16[512,1152]{1,0:T(8,128)(2,1)} %get-tuple-element.1097.refs_3_, ...), custom_call_target="tpu_custom_call" | custom-call | flops 8858370048 | bytes 21757952 | tf_op jit(solution)/shard_map/pallas_call | solution.py:577
  464.9 17.6 %shard_map.284 = (bf16[512,1152]{1,0:T(8,128)(2,1)}, bf16[512,1152]{1,0:T(8,128)(2,1)}, bf16[512,1152]{1,0:T(8,128)(2,1)}, bf16[256,2048]{1,0:T(8,128)(2,1)}, bf...) custom-call(s32[2]{0:T(128)} %pad_add_fusion.2.expert, ...), custom_call_target="tpu_custom_call" | custom-call | flops 9663676416 | bytes 22544384 | tf_op jit(solution)/shard_map/pallas_call | solution.py:501
  503.2 14.2 %shard_map.285 = (f32[704,2048]{1,0:T(8,128)}, f32[352,2048]{1,0:T(8,128)}) custom-call(bf16[512,1152]{1,0:T(8,128)(2,1)} %get-tuple-element.1148.refs_0_, bf16[512,1152]{1,0:T(8,128)(2,1)} %get-tuple-element.1149.refs_1_, bf16[512,1152]{1,0:T(8,128)(2,1)} %get-tuple-element.1150.refs_2_, bf16[512,1152]{1,0:T(8,128)(2,1)} %get-tuple-element.1151.refs_3_, ...), custom_call_target="tpu_custom_call" | custom-call | flops 8858370048 | bytes 21757952 | tf_op jit(solution)/shard_map/pallas_call | solution.py:577
  518.8 17.4 %shard_map.286 = (bf16[512,1152]{1,0:T(8,128)(2,1)}, bf16[512,1152]{1,0:T(8,128)(2,1)}, bf16[512,1152]{1,0:T(8,128)(2,1)}, bf16[256,2048]{1,0:T(8,128)(2,1)}, bf...) custom-call(s32[2]{0:T(128)} %pad_add_fusion.2.expert, ...), custom_call_target="tpu_custom_call" | custom-call | flops 9663676416 | bytes 22544384 | tf_op jit(solution)/shard_map/pallas_call | solution.py:501
  542.6 10.8 %shard_map.287 = (bf16[1024,768]{1,0:T(8,128)(2,1)}, f32[1,768]{1,0:T(1,128)}) custom-call(s32[10]{0:T(128)} %pad_add_fusion.here, bf16[1024,768]{1,0:T(8,128)(2,1)} %get-tuple-element.1200.low, bf16[1024,256]{1,0:T(8,128)(2,1)} %bitcast.271, f32[128,128]{1,0:T(8,128)} %get-tuple-element.1519.cosine, f32[128,128]{1,0:T(8,128)} %get-tuple-element.1517.sine, ...), custom_call_target="tpu_custom_call" | custom-call | flops 335544320 | bytes 3670016 | tf_op jit(solution)/shard_map/pallas_call | solution.py:272
  581.6 9.0 %collective-permute-done.104 = bf16[128,2048]{1,0:T(8,128)(2,1)} collective-permute-done((bf16[128,2048]{1,0:T(8,128)(2,1)}, bf16[128,2048]{1,0:T(8,128)(2,1)}, u32[]{:S(2)}, u32[]{:S(2)}) %collective-permute-start.104) | collective-permute-done | bytes 524320 | tf_op jit(solution)/shard_map/ppermute | solution.py:78
  592.9 8.3 %collective-permute-done.103 = bf16[128,2048]{1,0:T(8,128)(2,1)} collective-permute-done((bf16[128,2048]{1,0:T(8,128)(2,1)}, bf16[128,2048]{1,0:T(8,128)(2,1)}, u32[]{:S(2)}, u32[]{:S(2)}) %collective-permute-start.103) | collective-permute-done | bytes 524320 | tf_op jit(solution)/shard_map/ppermute | solution.py:78
  605.1 17.7 %shard_map.288 = (bf16[512,1152]{1,0:T(8,128)(2,1)}, bf16[512,1152]{1,0:T(8,128)(2,1)}, bf16[512,1152]{1,0:T(8,128)(2,1)}, bf16[256,2048]{1,0:T(8,128)(2,1)}, bf...) custom-call(s32[2]{0:T(128)} %pad_add_fusion.2.expert, ...), custom_call_target="tpu_custom_call" | custom-call | flops 9663676416 | bytes 22544384 | tf_op jit(solution)/shard_map/pallas_call | solution.py:501
  636.1 17.5 %shard_map.289 = (bf16[512,1152]{1,0:T(8,128)(2,1)}, bf16[512,1152]{1,0:T(8,128)(2,1)}, bf16[512,1152]{1,0:T(8,128)(2,1)}, bf16[256,2048]{1,0:T(8,128)(2,1)}, bf...) custom-call(s32[2]{0:T(128)} %pad_add_fusion.2.expert, ...), custom_call_target="tpu_custom_call" | custom-call | flops 9663676416 | bytes 22544384 | tf_op jit(solution)/shard_map/pallas_call | solution.py:501
  676.9 15.9 %shard_map.290 = (f32[704,2048]{1,0:T(8,128)}, f32[352,2048]{1,0:T(8,128)}) custom-call(bf16[512,1152]{1,0:T(8,128)(2,1)} %get-tuple-element.1343.refs_0_, bf16[512,1152]{1,0:T(8,128)(2,1)} %get-tuple-element.1354.refs_1_, bf16[512,1152]{1,0:T(8,128)(2,1)} %get-tuple-element.1365.refs_2_, ...), custom_call_target="tpu_custom_call", output_to_operand_aliasing={{0}: (20, {}), {1}: (21, {})} | custom-call | flops 8858370048 | bytes 30408704 | tf_op jit(solution)/shard_map/pallas_call | solution.py:577
  728.4 15.9 %shard_map.291 = (f32[704,2048]{1,0:T(8,128)}, f32[352,2048]{1,0:T(8,128)}) custom-call(bf16[512,1152]{1,0:T(8,128)(2,1)} %get-tuple-element.1406.refs_0_, bf16[512,1152]{1,0:T(8,128)(2,1)} %get-tuple-element.1416.refs_1_, bf16[512,1152]{1,0:T(8,128)(2,1)} %get-tuple-element.1426.refs_2_, ...), custom_call_target="tpu_custom_call", output_to_operand_aliasing={{0}: (20, {}), {1}: (21, {})} | custom-call | flops 8858370048 | bytes 30408704 | tf_op jit(solution)/shard_map/pallas_call | solution.py:577
  764.5 15.8 %shard_map.292 = (f32[704,2048]{1,0:T(8,128)}, f32[352,2048]{1,0:T(8,128)}) custom-call(bf16[512,1152]{1,0:T(8,128)(2,1)} %get-tuple-element.1462.refs_0_, bf16[512,1152]{1,0:T(8,128)(2,1)} %get-tuple-element.1463.refs_1_, bf16[512,1152]{1,0:T(8,128)(2,1)} %get-tuple-element.1464.refs_2_, ...), custom_call_target="tpu_custom_call", output_to_operand_aliasing={{0}: (20, {}), {1}: (21, {})} | custom-call | flops 8858370048 | bytes 30408704 | tf_op jit(solution)/shard_map/pallas_call | solution.py:577
  (589 shorter events, 404.5 us)
Async XLA Ops:
  8.7 37.3 %all-to-all-start = ((bf16[8,64,768]{2,1,0:T(8,128)(2,1)}), bf16[8,64,768]{2,1,0:T(8,128)(2,1)S(1)}, u32[]{:S(2)}, u32[]{:S(2)}) async-start(bf16[8,64,768]{2,1,0:T(8,128)(2,1)} %reshape.609), calls=%async_computation | async-start | bytes 1572864 | tf_op jit(solution)/shard_map/all_to_all | solution.py:100
  46.0 42.1 %collective-permute-start.10 = (bf16[512,768]{1,0:T(8,128)(2,1)S(1)}, bf16[512,768]{1,0:T(8,128)(2,1)}, u32[]{:S(2)}, u32[]{:S(2)}) collective-permute-start(bf16[512,768]{1,0:T(8,128)(2,1)S(1)} %bitcast.258), channel_id=1, source_target_pairs={{0,16},{16,0},{1,17},{17,1},{2,18},{18,2},{3,19},{19,3},{4,20},{20... | collective-permute-start | bytes 2359304 | tf_op jit(solution)/shard_map/ppermute | solution.py:82
  48.5 39.6 %collective-permute-start.8 = (bf16[128,2048]{1,0:T(8,128)(2,1)}, bf16[128,2048]{1,0:T(8,128)(2,1)}, u32[]{:S(2)}, u32[]{:S(2)}) collective-permute-start(bf16[128,2048]{1,0:T(8,128)(2,1)} %collective-permute-done.3), channel_id=1, source_target_pairs={{0,2},{1,3},{2,0},{3,1},{4,6},{5,7},{6,4},{7,5},{8,10},{9,11},{10,... | collective-permute-start | bytes 1572872 | tf_op jit(solution)/shard_map/ppermute | solution.py:78
  50.0 38.0 %collective-permute-start.7 = (bf16[128,2048]{1,0:T(8,128)(2,1)}, bf16[128,2048]{1,0:T(8,128)(2,1)}, u32[]{:S(2)}, u32[]{:S(2)}) collective-permute-start(bf16[128,2048]{1,0:T(8,128)(2,1)} %collective-permute-done.3), channel_id=1, source_target_pairs={{0,4},{1,5},{2,6},{3,7},{4,8},{5,9},{6,10},{7,11},{8,12},{9,13},{1... | collective-permute-start | bytes 1572872 | tf_op jit(solution)/shard_map/ppermute | solution.py:78
  50.0 38.0 %collective-permute-start.9 = (bf16[128,2048]{1,0:T(8,128)(2,1)}, bf16[128,2048]{1,0:T(8,128)(2,1)}, u32[]{:S(2)}, u32[]{:S(2)}) collective-permute-start(bf16[128,2048]{1,0:T(8,128)(2,1)} %pad_maximum_fusion.1.refs_0_), channel_id=1, source_target_pairs={{0,4},{1,5},{2,6},{3,7},{4,8},{5,9},{6,10},{7,11},{8,12},{9,13},{1... | collective-permute-start | bytes 1572872 | tf_op jit(solution)/shard_map/ppermute | solution.py:78
  148.2 38.6 %all-to-all-start.1 = ((bf16[8,128,256]{1,2,0:T(8,128)(2,1)}), bf16[8,128,256]{1,2,0:T(8,128)(2,1)S(1)}, u32[]{:S(2)}, u32[]{:S(2)}) async-start(bf16[8,128,256]{1,2,0:T(8,128)(2,1)} %copy.63), calls=%async_computation.1 | async-start | bytes 1048576 | tf_op jit(solution)/shard_map/all_to_all | solution.py:100
  259.3 35.1 %collective-permute-start.50 = (bf16[128,2048]{1,0:T(8,128)(2,1)}, bf16[128,2048]{1,0:T(8,128)(2,1)}, u32[]{:S(2)}, u32[]{:S(2)}) collective-permute-start(bf16[128,2048]{1,0:T(8,128)(2,1)} %collective-permute-done.40.refs_0_.refs_12_), channel_id=1, source_target_pairs={{0,2},{1,3},{2,0},{3,1},{4,6},{5,7},{6,4},{7,5},{8,10},{9,11},{10,... | collective-permute-start | bytes 1572872 | tf_op jit(solution)/shard_map/ppermute | solution.py:78
  259.7 34.7 %collective-permute-start.49 = (bf16[128,2048]{1,0:T(8,128)(2,1)}, bf16[128,2048]{1,0:T(8,128)(2,1)}, u32[]{:S(2)}, u32[]{:S(2)}) collective-permute-start(bf16[128,2048]{1,0:T(8,128)(2,1)} %collective-permute-done.40.refs_0_.refs_12_), channel_id=1, source_target_pairs={{0,4},{1,5},{2,6},{3,7},{4,8},{5,9},{6,10},{7,11},{8,12},{9,13},{1... | collective-permute-start | bytes 1572872 | tf_op jit(solution)/shard_map/ppermute | solution.py:78
  259.8 34.6 %collective-permute-start.55 = (bf16[128,2048]{1,0:T(8,128)(2,1)S(1)}, bf16[128,2048]{1,0:T(8,128)(2,1)S(1)}, u32[]{:S(2)}, u32[]{:S(2)}) collective-permute-start(bf16[128,2048]{1,0:T(8,128)(2,1)S(1)} %copy-done.60), channel_id=1, source_target_pairs={{0,16},{16,0},{1,17},{17,1},{2,18},{18,2},{3,19},{19,3},{4,20},{20... | collective-permute-start | bytes 1572872 | tf_op jit(solution)/shard_map/ppermute | solution.py:82
  260.5 33.9 %collective-permute-start.56 = (bf16[128,2048]{1,0:T(8,128)(2,1)}, bf16[128,2048]{1,0:T(8,128)(2,1)S(1)}, u32[]{:S(2)}, u32[]{:S(2)}) collective-permute-start(bf16[128,2048]{1,0:T(8,128)(2,1)} %collective-permute-done.25.refs_5_.refs_9_), channel_id=1, source_target_pairs={{0,16},{16,0},{1,17},{17,1},{2,18},{18,2},{3,19},{19,3},{4,20},{20... | collective-permute-start | bytes 1572872 | tf_op jit(solution)/shard_map/ppermute | solution.py:82
  303.1 35.4 %collective-permute-start.64 = (bf16[128,2048]{1,0:T(8,128)(2,1)}, bf16[128,2048]{1,0:T(8,128)(2,1)S(1)}, u32[]{:S(2)}, u32[]{:S(2)}) collective-permute-start(bf16[128,2048]{1,0:T(8,128)(2,1)} %collective-permute-done.36.refs_4_.refs_16_), channel_id=1, source_target_pairs={{0,16},{16,0},{1,17},{17,1},{2,18},{18,2},{3,19},{19,3},{4,20},{20... | collective-permute-start | bytes 1572872 | tf_op jit(solution)/shard_map/ppermute | solution.py:82
  303.7 34.9 %collective-permute-start.65 = (bf16[128,2048]{1,0:T(8,128)(2,1)}, bf16[128,2048]{1,0:T(8,128)(2,1)}, u32[]{:S(2)}, u32[]{:S(2)}) collective-permute-start(bf16[128,2048]{1,0:T(8,128)(2,1)} %collective-permute-done.38.refs_5_.refs_17_), channel_id=1, source_target_pairs={{0,16},{16,0},{1,17},{17,1},{2,18},{18,2},{3,19},{19,3},{4,20},{20... | collective-permute-start | bytes 1572872 | tf_op jit(solution)/shard_map/ppermute | solution.py:82
  305.2 33.4 %collective-permute-start.59 = (bf16[128,2048]{1,0:T(8,128)(2,1)}, bf16[128,2048]{1,0:T(8,128)(2,1)}, u32[]{:S(2)}, u32[]{:S(2)}) collective-permute-start(bf16[128,2048]{1,0:T(8,128)(2,1)} %collective-permute-done.49.refs_0_.refs_16_), channel_id=1, source_target_pairs={{0,2},{1,3},{2,0},{3,1},{4,6},{5,7},{6,4},{7,5},{8,10},{9,11},{10,... | collective-permute-start | bytes 1572872 | tf_op jit(solution)/shard_map/ppermute | solution.py:78
  305.6 35.2 %collective-permute-start.66 = (bf16[128,2048]{1,0:T(8,128)(2,1)S(1)}, bf16[128,2048]{1,0:T(8,128)(2,1)}, u32[]{:S(2)}, u32[]{:S(2)}) collective-permute-start(bf16[128,2048]{1,0:T(8,128)(2,1)S(1)} %copy-done.29), channel_id=1, source_target_pairs={{0,16},{16,0},{1,17},{17,1},{2,18},{18,2},{3,19},{19,3},{4,20},{20... | collective-permute-start | bytes 1572872 | tf_op jit(solution)/shard_map/ppermute | solution.py:82
  359.0 34.3 %collective-permute-start.74 = (bf16[128,2048]{1,0:T(8,128)(2,1)}, bf16[128,2048]{1,0:T(8,128)(2,1)S(1)}, u32[]{:S(2)}, u32[]{:S(2)}) collective-permute-start(bf16[128,2048]{1,0:T(8,128)(2,1)} %collective-permute-done.39.refs_0_.refs_8_), channel_id=1, source_target_pairs={{0,16},{16,0},{1,17},{17,1},{2,18},{18,2},{3,19},{19,3},{4,20},{20... | collective-permute-start | bytes 1572872 | tf_op jit(solution)/shard_map/ppermute | solution.py:82
  359.6 33.7 %collective-permute-start.75 = (bf16[128,2048]{1,0:T(8,128)(2,1)}, bf16[128,2048]{1,0:T(8,128)(2,1)}, u32[]{:S(2)}, u32[]{:S(2)}) collective-permute-start(bf16[128,2048]{1,0:T(8,128)(2,1)} %collective-permute-done.42.refs_1_.refs_9_), channel_id=1, source_target_pairs={{0,16},{16,0},{1,17},{17,1},{2,18},{18,2},{3,19},{19,3},{4,20},{20... | collective-permute-start | bytes 1572872 | tf_op jit(solution)/shard_map/ppermute | solution.py:82
  361.0 35.6 %collective-permute-start.76 = (bf16[128,2048]{1,0:T(8,128)(2,1)}, bf16[128,2048]{1,0:T(8,128)(2,1)}, u32[]{:S(2)}, u32[]{:S(2)}) collective-permute-start(bf16[128,2048]{1,0:T(8,128)(2,1)} %collective-permute-done.40.refs_0_.refs_12_), channel_id=1, source_target_pairs={{0,16},{16,0},{1,17},{17,1},{2,18},{18,2},{3,19},{19,3},{4,20},{20... | collective-permute-start | bytes 1572872 | tf_op jit(solution)/shard_map/ppermute | solution.py:82
  361.6 45.1 %collective-permute-start.80 = (bf16[256,2048]{1,0:T(8,128)(2,1)}, bf16[256,2048]{1,0:T(8,128)(2,1)}, u32[]{:S(2)}, u32[]{:S(2)}) collective-permute-start(bf16[256,2048]{1,0:T(8,128)(2,1)} %convert_add_fusion.6), channel_id=1, source_target_pairs={{0,4},{1,5},{2,6},{3,7},{4,8},{5,9},{6,10},{7,11},{8,12},{9,13},{1... | collective-permute-start | bytes 3145736 | tf_op jit(solution)/shard_map/ppermute | solution.py:78
  406.7 32.9 %collective-permute-start.81 = (bf16[128,2048]{1,0:T(8,128)(2,1)}, bf16[128,2048]{1,0:T(8,128)(2,1)}, u32[]{:S(2)}, u32[]{:S(2)}) collective-permute-start(bf16[128,2048]{1,0:T(8,128)(2,1)} %collective-permute-done.49.refs_0_.refs_16_), channel_id=1, source_target_pairs={{0,16},{16,0},{1,17},{17,1},{2,18},{18,2},{3,19},{19,3},{4,20},{20... | collective-permute-start | bytes 1572872 | tf_op jit(solution)/shard_map/ppermute | solution.py:82
  498.4 37.7 %all-to-all-start.2 = ((bf16[8,128,256]{2,1,0:T(8,128)(2,1)}), bf16[8,128,256]{2,1,0:T(8,128)(2,1)S(1)}, u32[]{:S(2)}, u32[]{:S(2)}) async-start(bf16[8,128,256]{2,1,0:T(8,128)(2,1)} %bitcast.270), calls=%async_computation.2 | async-start | bytes 1048576 | tf_op jit(solution)/shard_map/all_to_all | solution.py:100
  708.3 46.8 %all-to-all-start.3 = ((bf16[8,64,768]{2,1,0:T(8,128)(2,1)}), bf16[8,64,768]{2,1,0:T(8,128)(2,1)}, u32[]{:S(2)}, u32[]{:S(2)}) async-start(bf16[8,64,768]{2,1,0:T(8,128)(2,1)} %fusion.2), calls=%async_computation.3 | async-start | bytes 1572864 | tf_op jit(solution)/shard_map/all_to_all | solution.py:100
  713.7 35.2 %collective-permute-start.119 = (bf16[64,2048]{1,0:T(8,128)(2,1)S(1)}, bf16[64,2048]{1,0:T(8,128)(2,1)S(1)}, u32[]{:S(2)}, u32[]{:S(2)}) collective-permute-start(bf16[64,2048]{1,0:T(8,128)(2,1)S(1)} %get-tuple-element.1502), channel_id=1, source_target_pairs={{0,4},{1,5},{2,6},{3,7},{4,8},{5,9},{6,10},{7,11},{8,12},{9,13},{1... | collective-permute-start | bytes 786440 | tf_op jit(solution)/shard_map/ppermute | solution.py:78
  715.7 33.3 %collective-permute-start.121 = (bf16[64,2048]{1,0:T(8,128)(2,1)S(1)}, bf16[64,2048]{1,0:T(8,128)(2,1)S(1)}, u32[]{:S(2)}, u32[]{:S(2)}) collective-permute-start(bf16[64,2048]{1,0:T(8,128)(2,1)S(1)} %get-tuple-element.1503), channel_id=1, source_target_pairs={{0,12},{1,13},{2,14},{3,15},{4,0},{5,1},{6,2},{7,3},{8,4},{9,5},{1... | collective-permute-start | bytes 786440 | tf_op jit(solution)/shard_map/ppermute | solution.py:78
  717.8 35.4 %collective-permute-start.120 = (bf16[64,2048]{1,0:T(8,128)(2,1)S(1)}, bf16[64,2048]{1,0:T(8,128)(2,1)S(1)}, u32[]{:S(2)}, u32[]{:S(2)}) collective-permute-start(bf16[64,2048]{1,0:T(8,128)(2,1)S(1)} %get-tuple-element.1504), channel_id=1, source_target_pairs={{0,8},{1,9},{2,10},{3,11},{4,12},{5,13},{6,14},{7,15},{8,0},{9,1},... | collective-permute-start | bytes 786440 | tf_op jit(solution)/shard_map/ppermute | solution.py:78
  (201 other events, 2794.4 us)

commit v3 on v2

--- a/solution.py
+++ b/solution.py
@@ -17,6 +17,7 @@
 LANES = 128
 TILE = 512
 VMEM = 56 << 20
+EXTRA = 16
 
 
 epsilon = 1e-06
@@ -134,15 +135,6 @@
             piece = lax.dynamic_index_in_dim(terms, there, 0, keepdims=False)
             total = total + self.hop(piece, da=da).astype(f32)
         return total
-
-    def everywhere(self, small):
-        parts = [small] + [self.cross(small, shift) for shift in range(1, self.groups)]
-        level = yield jnp.stack(parts)
-        parts = [level] + [self.hop(level, db=db) for db in range(1, self.nb)]
-        level = yield jnp.stack(parts, axis=1)
-        parts = [level] + [self.hop(level, da=da) for da in range(1, self.na)]
-        level = yield jnp.stack(parts, axis=1)
-        yield jnp.stack([level, self.hop(level, dc=1)], axis=3)
 
 
 def turned_lanes(values):
@@ -343,46 +335,124 @@
     )(order, *pieces)
 
 
-def experts_kernel(blocks, start, expert, meta, vector, *refs):
-    row_blocks, grad_blocks = refs[:blocks], refs[blocks : 2 * blocks]
-    into_hbm, down_hbm = refs[2 * blocks : 2 * blocks + 2]
-    refs = refs[2 * blocks + 2 :]
+def project_kernel(counts, size, step, order, gain, *refs):
+    blocks, pieces = refs[: counts[0]], refs[counts[0] : sum(counts)]
+    normed_out, weight_out, raw, arrived, normed, weight, in_sem, weight_sem, out_sem = refs[
+        sum(counts) :
+    ]
+    rows = blocks[0].shape[0]
+    loads = [
+        pltpu.make_async_copy(block, arrived.at[pl.ds(n * rows, rows), :], in_sem.at[n])
+        for n, block in enumerate(blocks)
+    ]
+    parts = pieces[0].shape[0] // step
+    moves = []
+    for n, piece in enumerate(pieces):
+        for part in range(parts):
+            to = pl.multiple_of(order[n * parts + part] * size, size)
+            moves.append(
+                pltpu.make_async_copy(
+                    piece.at[pl.ds(part * step, size), :],
+                    weight.at[pl.ds(to, size), :],
+                    weight_sem.at[n * parts + part],
+                )
+            )
+    for copy in loads + moves:
+        copy.start()
+    stores = []
+    for n, load in enumerate(loads):
+        load.wait()
+        at = slice(n * rows, (n + 1) * rows)
+        values = arrived[at, :].astype(f32)
+        mean = jnp.mean(values * values, axis=1, keepdims=True)
+        normed[at, :] = (values * lax.rsqrt(mean + epsilon) * gain[...]).astype(bf16)
+    stores.append(pltpu.make_async_copy(normed, normed_out, out_sem.at[0]))
+    for copy in moves:
+        copy.wait()
+    stores.append(pltpu.make_async_copy(weight, weight_out, out_sem.at[1]))
+    for copy in stores:
+        copy.start()
+    raw[...] = dot(normed[...], weight[...], ((1,), (0,)))
+    for copy in stores:
+        copy.wait()
+
+
+def project(blocks, gain, pieces, size, step, order):
+    tokens, features = sum(block.shape[0] for block in blocks), blocks[0].shape[1]
+    weight_rows = sum(piece.shape[0] for piece in pieces) // step * size
+    columns = pieces[0].shape[1]
+    anywhere = pl.BlockSpec(memory_space=pl.ANY)
+    inside = pl.BlockSpec(memory_space=pltpu.VMEM)
+    return pl.pallas_call(
+        functools.partial(project_kernel, (len(blocks), len(pieces)), size, step),
+        out_shape=[
+            jax.ShapeDtypeStruct((tokens, features), bf16),
+            jax.ShapeDtypeStruct((weight_rows, columns), bf16),
+            jax.ShapeDtypeStruct((tokens, columns), f32),
+        ],
+        in_specs=[pl.BlockSpec(memory_space=pltpu.SMEM), inside]
+        + [anywhere] * (len(blocks) + len(pieces)),
+        out_specs=[anywhere, anywhere, inside],
+        scratch_shapes=[
+            pltpu.VMEM((tokens, features), bf16),
+            pltpu.VMEM((tokens, features), bf16),
+            pltpu.VMEM((weight_rows, columns), bf16),
+            pltpu.SemaphoreType.DMA((len(blocks),)),
+            pltpu.SemaphoreType.DMA((weight_rows // size,)),
+            pltpu.SemaphoreType.DMA((2,)),
+        ],
+        compiler_params=pltpu.CompilerParams(vmem_limit_bytes=VMEM),
+        cost_estimate=pl.CostEstimate(
+            flops=2 * tokens * features * columns,
+            bytes_accessed=4 * (tokens * features + weight_rows * columns + tokens * columns),
+            transcendentals=0,
+        ),
+    )(order, gain, *blocks, *pieces)
+
+
+def experts_kernel(pieces, start, expert, meta, vector, *refs):
+    row_pieces, grad_pieces = refs[:pieces], refs[pieces : 2 * pieces]
+    into_hbm, down_hbm = refs[2 * pieces : 2 * pieces + 2]
+    refs = refs[2 * pieces + 2 :]
     unit_outs, refs = refs[:3], refs[3:]
-    rest = blocks // CORES
+    rest, count = meta.shape[0], meta.shape[-1]
+    blocks = rest * CORES
     term_outs, vector_grad, refs = refs[: rest + 1], refs[rest + 1], refs[rest + 2 :]
     rows, grads, into, down, middle_all, gate_all, up_all = refs[:7]
-    in_sem, weight_sem, out_sem, term_sem = refs[7:11]
+    in_sem, weight_sem, out_sem, term_sem, terms = refs[7:12]
     tokens, features = rows.shape
     units = down.shape[0]
-    count = tokens // blocks
-    tiles = [(low, min(low + TILE, units)) for low in range(0, units, TILE)]
+    size = tokens // pieces
+    parts = ((0, start), (start, units))
 
     loads = [
         [
             pltpu.make_async_copy(
-                block, held.at[pl.ds(n * count, count), :], in_sem.at[which, n]
+                piece, held.at[pl.ds(n * size, size), :], in_sem.at[which, n]
             )
-            for n, block in enumerate(arrived)
+            for n, piece in enumerate(arrived)
         ]
-        for which, (arrived, held) in enumerate(((row_blocks, rows), (grad_blocks, grads)))
+        for which, (arrived, held) in enumerate(((row_pieces, rows), (grad_pieces, grads)))
     ]
     weights = [
         [
             pltpu.make_async_copy(
                 source.at[pl.ds(first + low, high - low), :],
                 held.at[pl.ds(first + low, high - low), :],
-                weight_sem.at[tile, which],
+                weight_sem.at[part, which],
             )
             for which, (source, held, first) in enumerate(
                 ((into_hbm, into, 0), (into_hbm, into, units), (down_hbm, down, 0))
             )
         ]
-        for tile, (low, high) in enumerate(tiles)
+        for part, (low, high) in enumerate(parts)
     ]
     for copy in loads[0] + weights[0] + loads[1]:
         copy.start()
-    for tile in weights[1:]:
-        for copy in tile:
+
+    @pl.when(expert[1] == 1)
+    def _():
+        for copy in weights[1]:
             copy.start()
 
     here = expert[0].astype(f32)
@@ -397,53 +467,41 @@
             columns.append(jnp.transpose(jnp.broadcast_to(scale, (count, count)))[:, :1])
     routed_scale = jnp.concatenate(columns, axis=0)
 
-    for copy in loads[0]:
-        copy.wait()
-    logit = jnp.sum(rows[...].astype(f32) * vector[...], axis=1, keepdims=True)
-    shared_scale = jax.nn.sigmoid(logit)
-    inner = jnp.zeros((tokens, 1), f32)
-    stores = []
-    for tile, (low, high) in enumerate(tiles):
-        for copy in weights[tile]:
-            copy.wait()
+    def work(part, scale):
+        low, high = parts[part]
         gate = dot(rows[...], into[low:high, :], ((1,), (1,)))
         up = dot(rows[...], into[units + low : units + high, :], ((1,), (1,)))
-        if tile == 0:
-            for copy in loads[1]:
-                copy.wait()
         back = dot(grads[...], down[low:high, :], ((1,), (1,)))
         gate_sigmoid = jax.nn.sigmoid(gate)
         silu = gate * gate_sigmoid
         middle = silu * up
-        unit = lax.broadcasted_iota(jnp.int32, (1, high - low), 1) + low
-        if high <= start:
-            scale = routed_scale
-        elif low >= start:
-            scale = shared_scale
-        else:
-            scale = jnp.where(unit < start, routed_scale, shared_scale)
-        if high > start:
-            product = middle * back
-            if low < start:
-                product = jnp.where(unit < start, 0.0, product)
-            inner = inner + jnp.sum(product, axis=1, keepdims=True)
+        inner = jnp.sum(middle * back, axis=1, keepdims=True) if part else None
         back = back * scale
         middle_all[:, low:high] = (middle * scale).astype(bf16)
         gate_all[:, low:high] = (back * up * (gate_sigmoid + silu * (1.0 - gate_sigmoid))).astype(
             bf16
         )
         up_all[:, low:high] = (back * silu).astype(bf16)
-        for which, (held, out) in enumerate(zip((middle_all, gate_all, up_all), unit_outs)):
-            lanes = pl.ds(low, high - low)
-            copy = pltpu.make_async_copy(
-                held.at[:, lanes], out.at[:, lanes], out_sem.at[tile, which]
-            )
+        lanes = pl.ds(low, high - low)
+        copies = [
+            pltpu.make_async_copy(held.at[:, lanes], out.at[:, lanes], out_sem.at[part, which])
+            for which, (held, out) in enumerate(zip((middle_all, gate_all, up_all), unit_outs))
+        ]
+        for copy in copies:
             copy.start()
-            stores.append(copy)
+        return inner, copies
+
+    for copy in loads[0] + weights[0] + loads[1]:
+        copy.wait()
+    _, stores = work(0, routed_scale)
 
     @pl.when(expert[1] == 1)
     def _():
-        terms = refs[11]
+        for copy in weights[1]:
+            copy.wait()
+        logit = jnp.sum(rows[...].astype(f32) * vector[...], axis=1, keepdims=True)
+        shared_scale = jax.nn.sigmoid(logit)
+        inner, copies = work(1, shared_scale)
         logit_grad = inner * shared_scale * (1.0 - shared_scale)
         for low in range(0, features, TILE):
             lanes = slice(low, low + TILE)
@@ -455,14 +513,14 @@
                 at = slice(n * count, (n + 1) * count)
                 terms[2 * n * count : (2 * n + 1) * count, lanes] = value[at]
                 terms[(2 * n + 1) * count : (2 * n + 2) * count, lanes] = result[at]
-        at, copies = 0, []
+        at = 0
         for n, out in enumerate(term_outs):
-            copies.append(
-                pltpu.make_async_copy(terms.at[pl.ds(at, out.shape[0]), :], out, term_sem.at[n])
+            copy = pltpu.make_async_copy(
+                terms.at[pl.ds(at, out.shape[0]), :], out, term_sem.at[n]
             )
+            copy.start()
+            copies.append(copy)
             at += out.shape[0]
-        for copy in copies:
-            copy.start()
         vector_grad[...] = jnp.sum(rows[...].astype(f32) * logit_grad, axis=0, keepdims=True)
         for copy in copies:
             copy.wait()
@@ -472,10 +530,9 @@
 
 
 def experts(expert, meta, vector, rows, grads, into, down, routed):
-    blocks = len(rows)
-    count, features = rows[0].shape
-    tokens, units, rest = blocks * count, down.shape[0], blocks // CORES
-    tiles = -(-units // TILE)
+    pieces, features = len(rows), rows[0].shape[1]
+    tokens, units = sum(piece.shape[0] for piece in rows), down.shape[0]
+    rest, count = meta.shape[0], meta.shape[-1]
     anywhere = pl.BlockSpec(memory_space=pl.ANY)
     inside = pl.BlockSpec(memory_space=pltpu.VMEM)
     out_shape = [jax.ShapeDtypeStruct((tokens, units), bf16)] * 3
@@ -488,9 +545,9 @@
         pltpu.VMEM((tokens, units), bf16),
         pltpu.VMEM((tokens, units), bf16),
         pltpu.VMEM((tokens, units), bf16),
-        pltpu.SemaphoreType.DMA((2, blocks)),
-        pltpu.SemaphoreType.DMA((tiles, 3)),
-        pltpu.SemaphoreType.DMA((tiles, 3)),
+        pltpu.SemaphoreType.DMA((2, pieces)),
+        pltpu.SemaphoreType.DMA((2, 3)),
+        pltpu.SemaphoreType.DMA((2, 3)),
         pltpu.SemaphoreType.DMA((rest + 1,)),
     ]
     out_shape += [jax.ShapeDtypeStruct((2 * count, features), bf16)] * rest
@@ -499,10 +556,10 @@
     out_specs += [anywhere] * (rest + 1) + [inside]
     scratch += [pltpu.VMEM((2 * tokens, features), bf16)]
     return pl.pallas_call(
-        functools.partial(experts_kernel, blocks, routed + -routed % LANES),
+        functools.partial(experts_kernel, pieces, routed + -routed % LANES),
         out_shape=out_shape,
         in_specs=[pl.BlockSpec(memory_space=pltpu.SMEM), inside, inside]
-        + [anywhere] * (2 * blocks + 2),
+        + [anywhere] * (2 * pieces + 2),
         out_specs=out_specs,
         scratch_shapes=scratch,
         compiler_params=pltpu.CompilerParams(vmem_limit_bytes=VMEM),
@@ -514,14 +571,15 @@
     )(expert, meta, vector, *rows, *grads, into, down)
 
 
-def weight_grad_kernel(unit_counts, row_counts, first, second, start, adds, *refs):
+def weight_grad_kernel(unit_counts, row_counts, parts, adds, *refs):
     some, pieces = len(unit_counts), len(unit_counts) + len(row_counts)
     units, rows = refs[:some], refs[some:pieces]
-    before = refs[pieces : pieces + 2] if adds else (None, None)
-    first_out, second_out, held, tiles, held_sem, tile_sem = refs[pieces + 2 * adds :]
+    before, refs = refs[pieces : pieces + adds * len(parts)], refs[pieces + adds * len(parts) :]
+    outs, (held, tiles, held_sem, tile_sem) = refs[: len(parts)], refs[len(parts) :]
     width = tiles.shape[-1]
     step = pl.program_id(0)
     slot = lax.rem(step, 2)
+    used = pl.ds(0, held.shape[1])
     unit_places, row_places = (
         [pl.ds(sum(counts[:n]), count) for n, count in enumerate(counts)]
         for counts in (unit_counts, row_counts)
@@ -529,7 +587,7 @@
 
     def held_copies():
         return [
-            pltpu.make_async_copy(units[n], held.at[at, :], held_sem.at[n])
+            pltpu.make_async_copy(units[n].at[:, used], held.at[at, :], held_sem.at[n])
             for n, at in enumerate(unit_places)
         ]
 
@@ -557,41 +615,44 @@
         for copy in tile_copies(step + 1, 1 - slot):
             copy.start()
 
-    for low, size, out, earlier in (
-        (0, first, first_out, before[0]),
-        (start, second, second_out, before[1]),
-    ):
+    for n, (low, size) in enumerate(parts):
         value = dot(held[:, low : low + size], tiles[slot], ((0,), (0,)))
-        out[...] = earlier[...] + value if adds else value
-
-
-def weight_grad(units, rows, first, second, before=()):
+        outs[n][...] = before[n][...] + value if adds else value.astype(outs[n].dtype)
+
+
+def weight_grad(units, rows, sizes, before=()):
     unit_counts = [piece.shape[0] for piece in units]
     row_counts = [piece.shape[0] for piece in rows]
     pieces, tokens = len(units) + len(rows), sum(row_counts)
-    features, all_units = rows[0].shape[1], units[0].shape[1]
-    start = first + -first % LANES
+    features = rows[0].shape[1]
+    parts, used = [], 0
+    for size in sizes:
+        parts.append((used, size))
+        used += size + -size % LANES
     adds = int(bool(before))
     anywhere = pl.BlockSpec(memory_space=pl.ANY)
-    blocks = [pl.BlockSpec((size, TILE), lambda i: (0, i)) for size in (first, second)]
+    blocks = [pl.BlockSpec((size, TILE), lambda i: (0, i)) for size in sizes]
     return pl.pallas_call(
-        functools.partial(weight_grad_kernel, unit_counts, row_counts, first, second, start, adds),
+        functools.partial(weight_grad_kernel, unit_counts, row_counts, parts, adds),
         grid=(features // TILE,),
-        out_shape=[jax.ShapeDtypeStruct((size, features), f32) for size in (first, second)],
+        out_shape=[
+            jax.ShapeDtypeStruct((size, features), bf16 if n else f32)
+            for n, size in enumerate(sizes)
+        ],
         in_specs=[anywhere] * pieces + blocks * adds,
         out_specs=blocks,
         scratch_shapes=[
-            pltpu.VMEM((tokens, all_units), bf16),
+            pltpu.VMEM((tokens, used), bf16),
             pltpu.VMEM((2, tokens, TILE), bf16),
             pltpu.SemaphoreType.DMA((len(units),)),
             pltpu.SemaphoreType.DMA((2, len(rows))),
         ],
-        input_output_aliases={pieces: 0, pieces + 1: 1} if adds else {},
+        input_output_aliases={pieces + n: n for n in range(len(sizes))} if adds else {},
         compiler_params=pltpu.CompilerParams(vmem_limit_bytes=VMEM),
         cost_estimate=pl.CostEstimate(
-            flops=2 * tokens * features * (first + second),
-            bytes_accessed=tokens * (features + all_units) * 2
-            + features * (first + second) * 4 * (1 + adds),
+            flops=2 * tokens * features * sum(sizes),
+            bytes_accessed=tokens * (features + used) * 2
+            + features * sum(sizes) * 4 * (1 + adds),
             transcendentals=0,
         ),
     )(*units, *rows, *before)
@@ -643,6 +704,28 @@
         def all(self):
             return [block for blocks in self.blocks for block in blocks]
 
+    class RowRounds(Rounds):
+        def row(self):
+            if len(self.blocks) < len(self.far):
+                blocks = grid.row(self.far[len(self.blocks)])
+                self.blocks.append(jnp.concatenate(blocks, axis=0))
+
+        def rest(self):
+            left = self.far[len(self.blocks) :]
+            if left:
+                blocks = grid.row(jnp.concatenate(left, axis=0))
+                for n in range(len(left)):
+                    part = slice(n * row_count, (n + 1) * row_count)
+                    self.blocks.append(jnp.concatenate([b[part] for b in blocks], axis=0))
+
+    class PairRounds:
+        def __init__(self, block):
+            self.far, self.blocks = [], [jnp.concatenate(grid.row(block), axis=0)]
+
+        def line(self):
+            if len(self.blocks) < na:
+                self.blocks.append(grid.hop(self.blocks[-1], da=1))
+
     def tie_rounds(rounds, *values):
         state = [(r.far, r.blocks) for r in rounds]
         state, *values = tie(state, *values)
@@ -655,8 +738,8 @@
         chip = (grid.a - da) % na * nb + (grid.b - db) % nb
         return (group * chips + chip) * CORES + (grid.core + dc) % CORES
 
-    def other_core(blocks):
-        return [grid.hop(block, dc=1) for block in blocks]
+    def with_other(rows):
+        return [rows, grid.hop(rows, dc=1)]
 
     small = jnp.concatenate([norm_gain, post_gain, shared_vector, b_qkv]).astype(f32)
     small_count = small.shape[0]
@@ -670,51 +753,50 @@
         ],
         axis=0,
     )
-    telling = grid.everywhere(meta)
+    meta_rows = meta.shape[0]
 
     x_rounds = Rounds(layer_input)
     x_rounds.line()
     x_rounds.row()
     sliced = jnp.transpose(w_qkv.reshape(own_rows, 3, chips, width), (2, 0, 1, 3))
-    by_chip = grid.swap(sliced.reshape(chips, own_rows, 3 * width))
-    level = next(telling)
+    sliced = sliced.reshape(chips, own_rows, 3 * width)
+    extra = jnp.pad(meta.astype(bf16).reshape(-1), (0, EXTRA * 3 * width - meta.size))
+    extra = jnp.broadcast_to(extra.reshape(1, EXTRA, 3 * width), (chips, EXTRA, 3 * width))
+    sliced = jnp.concatenate([sliced, extra], axis=1)
+    out_rounds = RowRounds(w_out)
+    out_rounds.line()
     into_in = [w_gate, shared_gate, w_up, shared_up]
     down_in = [w_down, shared_down]
-    level, w_out, into_in = tie_rounds([x_rounds], level, w_out, into_in)
-
-    out_pairs, out_far = [jnp.concatenate(grid.row(w_out), axis=0)], []
-
-    def out_line():
-        if len(out_pairs) < na:
-            out_pairs.append(grid.hop(out_pairs[-1], da=1))
+    out_far = []
 
     def out_cross():
-        if len(out_far) < len(out_pairs):
-            pair = out_pairs[len(out_far)]
+        if len(out_far) < len(out_rounds.blocks):
+            pair = out_rounds.blocks[len(out_far)]
             out_far.append([grid.cross(pair, shift) for shift in range(1, groups)])
 
     def tie_out(rounds, *values):
-        nonlocal out_pairs, out_far
-        out_pairs, out_far, *values = tie_rounds(rounds, out_pairs, out_far, *values)
+        nonlocal out_far
+        out_far, *values = tie_rounds([out_rounds] + rounds, out_far, *values)
         return values
 
+    into_in, sliced = tie_out([x_rounds], into_in, sliced)
     x_rounds.line()
     x_rounds.row()
-    level = telling.send(level)
+    by_chip = grid.swap(sliced)
+    out_rounds.row()
     into_rows = pack(
         [into_in[0][0].T, into_in[1].T, into_in[2][0].T, into_in[3].T], LANES
     )
-    by_chip, level, into_rows, down_in = tie_out(
-        [x_rounds], by_chip, level, into_rows, down_in
-    )
-    by_chip = by_chip.reshape(chips * own_rows, 3 * width)
+    by_chip, into_rows, down_in = tie_out([x_rounds], by_chip, into_rows, down_in)
+    part_rows = own_rows + EXTRA
+    by_chip = by_chip.reshape(chips * part_rows, 3 * width)
     x_rounds.line()
     x_rounds.row()
-    level = telling.send(level)
+    out_rounds.line()
+    out_rounds.row()
     by_group = [by_chip] + [grid.cross(by_chip, shift) for shift in range(1, groups)]
     down_rows = pack([down_in[0][0], down_in[1]], LANES)
-    out_line()
-    by_group, level, down_rows = tie_out([x_rounds], by_group, level, down_rows)
+    by_group, down_rows, cotangent = tie_out([x_rounds], by_group, down_rows, cotangent)
     weight_pieces, order = [], []
     for shift, piece in enumerate(by_group):
         for core in range(CORES):
@@ -724,68 +806,84 @@
                     ((grid.group - shift) % groups * chips + chip) * CORES
                     + (grid.core + core) % CORES
                 )
-    meta_all = telling.send(level)
-    flat_meta = meta_all.reshape(devices, *meta.shape)
-    index = jnp.arange(devices, dtype=jnp.int32)
-    ig, ia, ib, ic = (
-        index // owners,
-        index // (nb * CORES) % na,
-        index // CORES % nb,
-        index % CORES,
-    )
-    from_here = (
-        ((grid.group - ig) % groups * na + (grid.a - ia) % na) * nb + (grid.b - ib) % nb
-    ) * CORES + (grid.core - ic) % CORES
-    small_all = jnp.take(flat_meta[:, 2 * TOP + 1 :], from_here, axis=0).reshape(devices, -1)
+    used = -(-meta.size // (3 * width))
+    meta_all = jnp.stack(
+        [
+            piece.reshape(chips, part_rows, 3 * width)[:, own_rows : own_rows + used]
+            for piece in weight_pieces
+        ]
+    ).reshape(devices, -1)
+    meta_all = meta_all[:, : meta.size].astype(f32).reshape(devices, meta_rows, row_count)
+
+    def told_by(dg, chip, dc):
+        return (dg * CORES + dc) * chips + chip
+
+    by_place = jnp.stack(
+        [
+            told_by((grid.group - g) % groups, jnp.int32(chip), (grid.core - c) % CORES)
+            for g in range(groups)
+            for chip in range(chips)
+            for c in range(CORES)
+        ]
+    )
+    small_all = jnp.take(meta_all[:, 2 * TOP + 1 :], by_place, axis=0).reshape(devices, -1)
     own_features = norm_gain.shape[0]
     gains_in = small_all[:, :own_features].reshape(-1)
     gains_post = small_all[:, own_features : 2 * own_features].reshape(-1)
     gate_vector = small_all[:, 2 * own_features : 3 * own_features].reshape(-1)
     qkv_bias = small_all[:, 3 * own_features : small_count].reshape(3, chips, width)
     bias_here = lax.dynamic_index_in_dim(qkv_bias, grid.chip, 1, keepdims=False).reshape(-1)
-    plane_lengths = meta_all[0, :, :, 0, 2 * TOP, 0].reshape(chips).astype(jnp.int32)
+    offsets = [
+        told_by(dg, (grid.a - da) % na * nb + (grid.b - db) % nb, dc)
+        for dg in range(groups)
+        for da in slots
+        for dc in range(CORES)
+        for db in range(nb)
+    ]
+    told = jnp.take(meta_all[:, : 2 * TOP + 1], jnp.stack(offsets), axis=0)
+    told = told.reshape(groups, na, CORES, nb, 2 * TOP + 1, row_count)
+    plane_lengths = told[0, :, 0, :, 2 * TOP, 0].reshape(chips).astype(jnp.int32)
     here = jnp.concatenate([jnp.stack([grid.a, grid.b]).astype(jnp.int32), plane_lengths])
+    valid_rows = positions < lengths[0]
+    grad_rows = jnp.where(valid_rows[:, None], cotangent, jnp.zeros_like(cotangent))
+    grad_rounds = RowRounds(grad_rows)
     while len(x_rounds.blocks) < na:
         x_rounds.row()
-    out_line()
+    out_rounds.line()
+    out_rounds.row()
     out_cross()
-    heads_weight = pack(weight_pieces, size=own_rows, order=jnp.stack(order).astype(jnp.int32))
-    normed_first = pack(
-        [(unit_norm(block.astype(f32))[0] * gains_in).astype(bf16) for block in x_rounds.all()]
-    )
-    normed_first, heads_weight, bias_here, gains_in, cotangent, here = tie_out(
-        [], normed_first, heads_weight, bias_here, gains_in, cotangent, here
-    )
-
-    valid_rows = positions < lengths[0]
-    grad_rows = jnp.where(valid_rows[:, None], cotangent, jnp.zeros_like(cotangent))
+    x_blocks, weight_pieces, bias_here, gains_in, here = tie_out(
+        [grad_rounds], x_rounds.all(), weight_pieces, bias_here, gains_in, here
+    )
+
     inputs = layer_input.astype(f32)
-    grad_rounds = Rounds(grad_rows)
-    while len(out_pairs) < na:
-        out_line()
+    out_rounds.row()
+    out_cross()
     out_cross()
     grad_rounds.line()
     grad_rounds.row()
-    projected = dot(normed_first, heads_weight, ((1,), (0,)))
-    low, sent = attention(here, projected, bias_here[None], row_count, nb, heads_here)
-    low, sent = tie_out([grad_rounds], low, sent)
-
-    grad_rounds.line()
-    grad_rounds.row()
+    normed_first, heads_weight, raw = project(
+        x_blocks, gains_in[None], weight_pieces, own_rows, part_rows,
+        jnp.stack(order).astype(jnp.int32),
+    )
+    low, sent = attention(here, raw, bias_here[None], row_count, nb, heads_here)
+    low, sent = tie_out([], low, sent)
+
     while len(out_far) < na:
         out_cross()
+    grad_rounds.line()
     pieces, order = [], []
     for dc in range(CORES):
         for da in slots:
             for dg in range(groups):
-                pair = out_far[da][dg - 1] if dg else out_pairs[da]
+                pair = out_far[da][dg - 1] if dg else out_rounds.blocks[da]
                 pieces.append(grid.hop(pair, dc=1) if dc else pair)
                 order += [place_of(da, db, dc, dg) for db in range(nb)]
     out_weight = pack(pieces, size=own_rows, order=jnp.stack(order).astype(jnp.int32))
     arrived = grid.swap(sent.reshape(chips, row_count, width))
-    arrived, out_weight = tie_rounds([grad_rounds], arrived, out_weight)
-
-    far_grads, far_rows = [], []
+    arrived, out_weight = tie(arrived, out_weight)
+
+    far_grads, far_rows, flying = [], [], []
     crossings = [("grads", s) for s in slots] + [("rows", s) for s in slots]
 
     def cross_step():
@@ -796,10 +894,11 @@
             )
             if s < len(source.blocks):
                 crossings.pop(0)
-                goes.append([grid.cross(block, 1) for block in source.blocks[s]])
+                flying.append((goes, grid.cross(source.blocks[s], 1)))
 
     grad_rounds.line()
     grad_rounds.row()
+    cross_step()
     context = jnp.transpose(arrived, (1, 0, 2)).reshape(row_count, feature_count)
     residual = inputs + dot(context, out_weight, ((1,), (0,)))
     unit_second, factor_second = unit_norm(residual)
@@ -808,13 +907,13 @@
     expert = (lax.axis_index("ep") // HALVES).astype(jnp.int32)
     expert, far_expert = (jnp.stack([expert, jnp.int32(n)]) for n in (1, 0))
     vector_row = gate_vector[None]
-    told = meta_all[..., : 2 * TOP, :]
-    second_rounds = Rounds(normed_second)
+    told = jnp.swapaxes(told[..., : 2 * TOP, :], 2, 3)
+    second_rounds = PairRounds(normed_second)
     own = {"rows": [], "grads": [], "middle": [], "gate": [], "up": [], "vector": []}
 
     def work(s):
-        own["rows"].append(second_rounds.blocks[s] + other_core(second_rounds.blocks[s]))
-        own["grads"].append(grad_rounds.blocks[s] + other_core(grad_rounds.blocks[s]))
+        own["rows"].append(with_other(second_rounds.blocks[s]))
+        own["grads"].append(with_other(grad_rounds.blocks[s]))
         middle, gate, up, *terms, vector = experts(
             expert, told[0, s], vector_row, own["rows"][s], own["grads"][s],
             into_rows, down_rows, sizes[0],
@@ -834,10 +933,14 @@
         ]
 
     def step_tie(*values):
-        nonlocal own, far_grads, far_rows, into_rows, down_rows
-        own, far_grads, far_rows, into_rows, down_rows, *values = tie_rounds(
-            [grad_rounds, second_rounds], own, far_grads, far_rows, into_rows, down_rows, *values
+        nonlocal own, into_rows, down_rows, flying
+        arrivals = [rows for _, rows in flying]
+        own, arrivals, into_rows, down_rows, *values = tie_rounds(
+            [grad_rounds, second_rounds], own, arrivals, into_rows, down_rows, *values
         )
+        for (goes, _), rows in zip(flying, arrivals):
+            goes.append(rows)
+        flying = []
         return values
 
     def line_sum(rowed, sums, s):
@@ -845,8 +948,7 @@
         return grid.hop(total.astype(bf16), da=1) if s else total
 
     def far_work(shift, s):
-        rows = far_rows[s] + other_core(far_rows[s])
-        grads = far_grads[s] + other_core(far_grads[s])
+        rows, grads = with_other(far_rows[s]), with_other(far_grads[s])
         units = experts(
             far_expert, told[shift, s], vector_row, rows, grads,
             into_rows, down_rows, sizes[0],
@@ -858,17 +960,11 @@
 
     rowed, terms, far = {}, {}, []
     sums = None
-    second_rounds.line()
-    second_rounds.row()
-    cross_step()
     for s in slots:
-        grad_rounds.line()
-        grad_rounds.row()
         second_rounds.line()
-        second_rounds.row()
         if s:
-            cross_step()
-            cross_step()
+            grad_rounds.rest()
+        cross_step()
         if s >= 2:
             rowed[s - 1] = grid.row_sum(add_cores(terms[s - 1]))
         if s >= 3:
@@ -879,16 +975,14 @@
     rowed[na - 1] = grid.row_sum(add_cores(terms[na - 1]))
     if na > 2:
         sums = line_sum(rowed, sums, na - 2)
-    own_gate = weight_grad(own["gate"], flat(own["rows"]), *sizes)
+    own_gate = weight_grad(own["gate"], flat(own["rows"]), sizes)
     rowed, terms, sums, own_gate = step_tie(rowed, terms, sums, own_gate)
-    while crossings and two:
-        cross_step()
+    cross_step()
     sums = line_sum(rowed, sums, na - 1)
     rowed[0] = grid.row_sum(add_cores(terms[0]))
-    own_up = weight_grad(own["up"], flat(own["rows"]), *sizes)
-    if two:
-        far.append(far_work(1, 0))
-    rowed, sums, own_up, far = step_tie(rowed, sums, own_up, far)
+    own_up = weight_grad(own["up"], flat(own["rows"]), sizes)
+    own_down = weight_grad(own["middle"], flat(own["grads"]), sizes)
+    rowed, sums, own_up, own_down = step_tie(rowed, sums, own_up, own_down)
 
     both_sums = line_sum(rowed, sums, 0)
     second_grad = both_sums[:row_count]
@@ -903,10 +997,14 @@
     context_grad = dot(attended_grad, out_weight, ((1,), (1,))).astype(bf16)
     sent = jnp.transpose(context_grad.reshape(row_count, chips, width), (1, 0, 2))
     arrived = grid.swap(sent)
-    own_down = weight_grad(own["middle"], flat(own["grads"]), *sizes)
+    cross_step()
     if two:
-        far.append(far_work(1, 1))
-    arrived, own_down, attended_grad, far = step_tie(arrived, own_down, attended_grad, far)
+        far.append(far_work(1, 0))
+    totals = [[own_gate[0], own_up[0], own_down[0]]]
+    shared = [part[1] for part in (own_gate, own_up, own_down)]
+    arrived, attended_grad, far, shared, totals = step_tie(
+        arrived, attended_grad, far, shared, totals
+    )
 
     def own_features_of(values, core, group):
         parts = values.reshape(row_count, groups, chips, CORES, own_rows)
@@ -927,49 +1025,62 @@
         )
         total = mine.astype(f32) + grid.hop(other, dc=1).astype(f32)
         out_parts.append(total.astype(bf16))
-    first_terms, projected_grad, out_parts, far = step_tie(
-        first_terms, projected_grad, out_parts, far
-    )
-
-    slot_first = first_terms.reshape(na, nb, row_count, feature_count)
-    totals = [[own_gate, own_up, own_down]]
+    while crossings and two:
+        cross_step()
+    shared_far = [
+        [grid.cross(part, shift) for shift in range(1, groups)] for part in shared[:1]
+    ]
+    first_terms, projected_grad, out_parts, far, shared_far = step_tie(
+        first_terms, projected_grad, out_parts, far, shared_far
+    )
+
+    def in_order(*parts):
+        parts = [part.astype(f32) for part in parts]
+        if two:
+            return parts[0] + parts[1]
+        total = 0.0
+        for group in range(groups):
+            far_by = (grid.group - group) % groups
+            total = total + sum(
+                jnp.where(far_by == shift, part, 0.0) for shift, part in enumerate(parts)
+            )
+        return total
+
+    slot_first = first_terms.reshape(na, nb * row_count, feature_count)
 
     def end_tie(*values):
-        nonlocal far, far_rows, far_grads, into_rows, down_rows, own, totals
-        far, far_rows, far_grads, into_rows, down_rows, own, totals, *values = tie(
-            far, far_rows, far_grads, into_rows, down_rows, own, totals, *values
-        )
+        nonlocal far, into_rows, down_rows
+        far, into_rows, down_rows, *values = tie(far, into_rows, down_rows, *values)
         return values
 
     def far_grad(units, place):
-        before = totals[0][units] if two else ()
+        before = [totals[0][units]] if two else ()
         return weight_grad(
             [work[2][(1, 2, 0)[units]] for work in far], flat(work[place] for work in far),
-            *sizes, before,
-        )
-
-    first_rowed = {s: grid.row_sum(slot_first[s]) for s in range(1, na - 1)}
+            sizes[:1], before,
+        )[0]
+
     qkv_grad = dot(normed_first, projected_grad, ((0,), (0,))).astype(bf16)
     half = chips * own_rows // 2
+    first_sums = line_sum(slot_first, None, 1) if na > 1 else None
     crossed = [[grid.cross(part[:half], n + 1)] for n, part in enumerate(out_parts[1:])]
     if two:
-        far.append(far_work(1, 2))
-    first_rowed, slot_first, qkv_grad, crossed, out_parts = end_tie(
-        first_rowed, slot_first, qkv_grad, crossed, out_parts
-    )
-    for s in sorted({na - 1, 0}):
-        first_rowed[s] = grid.row_sum(slot_first[s])
-    first_sums = line_sum(first_rowed, None, 1)
+        far.append(far_work(1, 1))
+    slot_first, qkv_grad, crossed, out_parts, first_sums = end_tie(
+        slot_first, qkv_grad, crossed, out_parts, first_sums
+    )
+    if na > 2:
+        first_sums = line_sum(slot_first, first_sums, 2)
     for n, part in enumerate(out_parts[1:]):
         crossed[n].append(grid.cross(part[half:], n + 1))
     qkv_grad = grid.scatter_core(qkv_grad.reshape(groups, chips, CORES, own_rows, 3 * width), 2)
     if two:
-        far.append(far_work(1, 3 % na))
-    first_rowed, qkv_grad, crossed, out_parts, first_sums = end_tie(
-        first_rowed, qkv_grad.astype(bf16), crossed, out_parts, first_sums
-    )
-    for s in range(2, na):
-        first_sums = line_sum(first_rowed, first_sums, s)
+        far.append(far_work(1, 2 % na))
+    slot_first, qkv_grad, crossed, out_parts, first_sums, shared = end_tie(
+        slot_first, qkv_grad.astype(bf16), crossed, out_parts, first_sums, shared
+    )
+    for s in range(3, na):
+        first_sums = line_sum(slot_first, first_sums, s)
     qkv_grad = grid.scatter_groups(qkv_grad).astype(bf16)
     out_total = out_parts[0].astype(f32)
     for halves in crossed:
@@ -977,51 +1088,45 @@
     out_rowed = grid.scatter_row(
         out_total.astype(bf16).reshape(na, nb, own_rows, feature_count)
     )
+    shared_far.append([grid.cross(shared[1], shift) for shift in range(1, groups)])
+    if two:
+        if na > 3:
+            far.append(far_work(1, 3))
+        slot_first, first_sums, qkv_grad, out_rowed, shared = end_tie(
+            slot_first, first_sums, qkv_grad, out_rowed, shared
+        )
+    first_terms_here = slot_first[0] if first_sums is None else line_sum(slot_first, first_sums, 0)
+    first_grad = grid.row_sum(
+        first_terms_here.astype(bf16).reshape(nb, row_count, feature_count)
+    )
+    qkv_grad = grid.swap(qkv_grad).reshape(chips, own_rows, 3, width)
     if two:
         gate_total = far_grad(0, 0)
-        first_sums, qkv_grad, out_rowed, gate_total = end_tie(
-            first_sums, qkv_grad, out_rowed, gate_total
+        gate_total, first_grad, shared_far, shared, qkv_grad, out_rowed = end_tie(
+            gate_total, first_grad, shared_far, shared, qkv_grad, out_rowed
         )
-    first_grad = line_sum(first_rowed, first_sums, 0)
+    out_weight_grad = grid.scatter_line(out_rowed)
+    shared_far.append([grid.cross(shared[2], shift) for shift in range(1, groups)])
     unit_first, factor_first = unit_norm(inputs)
     input_part = norm_backward(first_grad, unit_first, factor_first, gains_in)
     layer_grad = (residual_grad + input_part).astype(bf16)
-    out_weight_grad = grid.scatter_line(out_rowed)
-    qkv_grad = grid.swap(qkv_grad).reshape(chips, own_rows, 3, width)
-    if two:
-        up_total = far_grad(1, 0)
-        qkv_grad, out_weight_grad, up_total, layer_grad = end_tie(
-            qkv_grad, out_weight_grad, up_total, layer_grad
-        )
     qkv_weight_grad = jnp.transpose(qkv_grad, (1, 2, 0, 3)).reshape(own_rows, -1).astype(f32)
     if two:
-        totals.append([gate_total, up_total, far_grad(2, 1)])
+        gate_grad, up_grad, down_grad = gate_total, far_grad(1, 0), far_grad(2, 1)
     else:
         second_blocks, grad_blocks = second_rounds.blocks, grad_rounds.blocks
         for shift in range(1, groups):
             totals, second_blocks, grad_blocks = tie(totals, second_blocks, grad_blocks)
             far_grads, far_rows = (
-                [[grid.cross(block, shift) for block in blocks] for blocks in source]
+                [grid.cross(rows, shift) for rows in source]
                 for source in (grad_blocks, second_blocks)
             )
             far = [far_work(shift, s) for s in slots]
             totals.append([far_grad(0, 0), far_grad(1, 0), far_grad(2, 1)])
-
-        def ordered(*parts):
-            total = 0.0
-            for group in range(groups):
-                far_by = (grid.group - group) % groups
-                total = total + sum(
-                    jnp.where(far_by == shift, part, 0.0) for shift, part in enumerate(parts)
-                )
-            return total
-
-        totals.append(jax.tree.map(ordered, *totals))
-    (
-        (gate_grad, shared_gate_grad),
-        (up_grad, shared_up_grad),
-        (down_grad, shared_down_grad),
-    ) = totals[-1]
+        gate_grad, up_grad, down_grad = (in_order(*parts) for parts in zip(*totals))
+    shared_gate_grad, shared_up_grad, shared_down_grad = (
+        in_order(here_part, *parts) for here_part, parts in zip(shared, shared_far)
+    )
 
     vector_grad = sum(own["vector"])[0]
     gain_grad = jnp.sum(first_terms.astype(f32) * normed_first.astype(f32), axis=0) / gains_in

time: 801 us -> 714 us (0.89)
  waiting for transfers between devices: 209 us -> 152 us
  Pallas kernels: 319 us -> 290 us
    ppermute x26 -> x20, waiting for transfers between devices: 65.4 us -> 14.5 us  [cross(): return lax.ppermute(values, 'dp', pairs)]
    pallas_call x6, Pallas kernels: 90.3 us -> 80 us  [weight_grad(): pl.pallas_call(functools.partial(weight_grad_kernel, unit_counts, row_cou...]
    unnamed x194 -> x154, local copies, waits for them, and re-layouts: 26.2 us -> 16.3 us
    pallas_call x5 -> x3, Pallas kernels: 28.5 us -> 19.1 us  [pack(): pl.pallas_call(functools.partial(pack_kernel, len(pieces), moves, blanks)...]
    pallas_call x8 -> x9, Pallas kernels: 181 us -> 172 us  [the longest x8 162 us: experts(): pl.pallas_call(functools.partial(experts_kernel, pieces, routed + -routed...]
    ppermute x102 -> x77, waiting for transfers between devices: 142 us -> 133 us  [hop(): return lax.ppermute(values, 'ep', pairs)]
    ppermute x102 -> x77, starting transfers between devices: 64.8 us -> 62.3 us  [hop(): return lax.ppermute(values, 'ep', pairs)]
    ppermute x26 -> x20, starting transfers between devices: 25.3 us -> 22.8 us  [cross(): return lax.ppermute(values, 'dp', pairs)]
  transfers between devices with their start and end apart: 132 -> 101, of which waited for: 39 -> 31; matrix products, arithmetic and copies ran while one was open for 15% -> 18% of each run, Pallas kernels for 40% -> 41%
where the time goes in v3:
time: 714 us; the launch traced here: 704 us
  Pallas kernels  290 us (41%)
  waiting for transfers between devices  152 us (21%)
  starting transfers between devices  106 us (15%)
  other arithmetic  76.3 us (11%)
  local copies, waits for them, and re-layouts  47.7 us (7%)
  matrix products  27.8 us (4%)
    pallas_call x8, Pallas kernels, experts(): pl.pallas_call(functools.partial(experts_kernel, pieces, routed + -routed...  162 us
    ppermute x77, waiting for transfers between devices, hop(): return lax.ppermute(values, 'ep', pairs)  133 us
    pallas_call x6, Pallas kernels, weight_grad(): pl.pallas_call(functools.partial(weight_grad_kernel, unit_counts, row_cou...  80 us
    ppermute x77, starting transfers between devices, hop(): return lax.ppermute(values, 'ep', pairs)  62.3 us
    dot_general x8, matrix products, dot(): lax.dot_general(left, right, (dims, ((), ())), preferred_element_type=f32)  27.8 us
    ppermute x20, starting transfers between devices, cross(): return lax.ppermute(values, 'dp', pairs)  22.8 us
    all_to_all x4, starting transfers between devices, swap(): lax.all_to_all(blocks, 'ep', split_axis=0, concat_axis=0, tiled=True, axi...  21.3 us
    pallas_call x3, Pallas kernels, pack(): pl.pallas_call(functools.partial(pack_kernel, len(pieces), moves, blanks)...  19.1 us
  transfers between devices with their start and end apart: 101, of which 31 were waited for; matrix products, arithmetic and copies ran while one was open for 18% of the time, Pallas kernels for 41%

profile of v3, /device:TPU:0, one launch (start us, length us, event | category | flops | bytes accessed | tf_op | source)
XLA Modules:
  0.0 703.7 jit_solution(15703871577558162835)
XLA Ops:
  13.5 10.0 %collective-permute-done = bf16[64,2048]{1,0:T(8,128)(2,1)S(1)} collective-permute-done((bf16[64,2048]{1,0:T(8,128)(2,1)}, bf16[64,2048]{1,0:T(8,128)(2,1)S(1)}, u32[]{:S(2)}, u32[]{:S(2)}) %collective-permute-start) | collective-permute-done | bytes 262176 | tf_op jit(solution)/shard_map/ppermute | solution.py:79
  40.3 17.5 %collective-permute-done.3 = bf16[64,2048]{1,0:T(8,128)(2,1)S(1)} collective-permute-done((bf16[64,2048]{1,0:T(8,128)(2,1)S(1)}, bf16[64,2048]{1,0:T(8,128)(2,1)S(1)}, u32[]{:S(2)}, u32[]{:S(2)}) %collective-permute-start.3) | collective-permute-done | bytes 262176 | tf_op jit(solution)/shard_map/ppermute | solution.py:79
  73.1 10.6 %collective-permute-done.7 = bf16[64,2048]{1,0:T(8,128)(2,1)S(1)} collective-permute-done((bf16[64,2048]{1,0:T(8,128)(2,1)S(1)}, bf16[64,2048]{1,0:T(8,128)(2,1)S(1)}, u32[]{:S(2)}, u32[]{:S(2)}) %collective-permute-start.7) | collective-permute-done | bytes 262176 | tf_op jit(solution)/shard_map/ppermute | solution.py:79
  112.9 10.0 %shard_map.274 = (bf16[1024,2048]{1,0:T(8,128)(2,1)}, bf16[2048,768]{1,0:T(8,128)(2,1)}, f32[1024,768]{1,0:T(8,128)}) custom-call(s32[32]{0:T(128)} %stack.733.order, f32[1,2048]{1,0:T(1,128)} %bitcast.403, bf16[128,2048]{1,0:T(8,128)(2,1)} %refs_0_, bf16[128,2048]{1,0:T(8,128)(2,1)} %copy-done.69, bf16[128,2048]{1,0:T(8,128)(2,1)} %copy-done.68, ...), custom_call_target="tpu_custom_call" | custom-call | flops 3221225472 | bytes 17825792 | tf_op jit(solution)/shard_map/pallas_call | solution.py:386
  122.9 8.8 %shard_map.275 = (bf16[1024,768]{1,0:T(8,128)(2,1)}, bf16[1024,256]{1,0:T(8,128)(2,1)}) custom-call(s32[10]{0:T(128)} %pad_add_fusion.here, f32[1024,768]{1,0:T(8,128)} %get-tuple-element.537.raw, f32[1,768]{1,0:T(1,128)} %broadcast_in_dim.112.bias, f32[128,128]{1,0:T(8,128)} %get-tuple-element.983.cosine, f32[128,128]{1,0:T(8,128)} %get-tuple-element.982.signed_sine), custom_call_target="tpu_custom_call" | custom-call | flops 134217728 | bytes 5242880 | tf_op jit(solution)/shard_map/pallas_call | solution.py:233
  151.1 7.5 %shard_map.276 = bf16[2048,2048]{1,0:T(8,128)(2,1)} custom-call(s32[32]{0:T(128)} %stack.766.order, bf16[128,2048]{1,0:T(8,128)(2,1)} %copy-done.22, bf16[128,2048]{1,0:T(8,128)(2,1)} %copy-done.42, bf16[128,2048]{1,0:T(8,128)(2,1)} %copy-done.23, bf16[128,2048]{1,0:T(8,128)(2,1)} %copy-done.44, bf16[128,2048]{1,0:T(8,128)(2,1)} %copy-done.24, ...), custom_call_target="tpu_custom_call" | custom-call | bytes 16777216 | tf_op jit(solution)/shard_map/pallas_call | solution.py:324
  170.0 7.9 %collective-permute-done.34 = bf16[128,2048]{1,0:T(8,128)(2,1)S(1)} collective-permute-done((bf16[128,2048]{1,0:T(8,128)(2,1)S(1)}, bf16[128,2048]{1,0:T(8,128)(2,1)S(1)}, u32[]{:S(2)}, u32[]{:S(2)}) %collective-permute-start.34) | collective-permute-done | bytes 524320 | tf_op jit(solution)/shard_map/ppermute | solution.py:79
  198.4 27.4 %shard_map.277 = (bf16[512,1152]{1,0:T(8,128)(2,1)}, bf16[512,1152]{1,0:T(8,128)(2,1)}, bf16[512,1152]{1,0:T(8,128)(2,1)}, bf16[256,2048]{1,0:T(8,128)(2,1)}, bf...) custom-call(s32[2]{0:T(128)} %pad_add_fusion.1.expert, ...), custom_call_target="tpu_custom_call" | custom-call | flops 9663676416 | bytes 22544384 | tf_op jit(solution)/shard_map/pallas_call | solution.py:558
  225.8 7.4 %collective-permute-done.31 = bf16[128,2048]{1,0:T(8,128)(2,1)S(1)} collective-permute-done((bf16[128,2048]{1,0:T(8,128)(2,1)S(1)}, bf16[128,2048]{1,0:T(8,128)(2,1)S(1)}, u32[]{:S(2)}, u32[]{:S(2)}) %collective-permute-start.31) | collective-permute-done | bytes 524320 | tf_op jit(solution)/shard_map/ppermute | solution.py:79
  235.6 20.3 %collective-permute-done.40 = bf16[256,2048]{1,0:T(8,128)(2,1)S(1)} collective-permute-done((bf16[256,2048]{1,0:T(8,128)(2,1)S(1)}, bf16[256,2048]{1,0:T(8,128)(2,1)S(1)}, u32[]{:S(2)}, u32[]{:S(2)}) %collective-permute-start.40) | collective-permute-done | bytes 1048608 | tf_op jit(solution)/shard_map/ppermute | solution.py:79
  258.5 27.1 %shard_map.278 = (bf16[512,1152]{1,0:T(8,128)(2,1)}, bf16[512,1152]{1,0:T(8,128)(2,1)}, bf16[512,1152]{1,0:T(8,128)(2,1)}, bf16[256,2048]{1,0:T(8,128)(2,1)}, bf...) custom-call(s32[2]{0:T(128)} %pad_add_fusion.1.expert, ...), custom_call_target="tpu_custom_call" | custom-call | flops 9663676416 | bytes 22544384 | tf_op jit(solution)/shard_map/pallas_call | solution.py:558
  301.7 27.0 %shard_map.279 = (bf16[512,1152]{1,0:T(8,128)(2,1)}, bf16[512,1152]{1,0:T(8,128)(2,1)}, bf16[512,1152]{1,0:T(8,128)(2,1)}, bf16[256,2048]{1,0:T(8,128)(2,1)}, bf...) custom-call(s32[2]{0:T(128)} %pad_add_fusion.1.expert, ...), custom_call_target="tpu_custom_call" | custom-call | flops 9663676416 | bytes 22544384 | tf_op jit(solution)/shard_map/pallas_call | solution.py:558
  342.3 27.1 %shard_map.280 = (bf16[512,1152]{1,0:T(8,128)(2,1)}, bf16[512,1152]{1,0:T(8,128)(2,1)}, bf16[512,1152]{1,0:T(8,128)(2,1)}, bf16[256,2048]{1,0:T(8,128)(2,1)}, bf...) custom-call(s32[2]{0:T(128)} %pad_add_fusion.1.expert, ...), custom_call_target="tpu_custom_call" | custom-call | flops 9663676416 | bytes 22544384 | tf_op jit(solution)/shard_map/pallas_call | solution.py:558
  380.8 13.8 %shard_map.281 = (f32[704,2048]{1,0:T(8,128)}, bf16[352,2048]{1,0:T(8,128)(2,1)}) custom-call(bf16[512,1152]{1,0:T(8,128)(2,1)} %get-tuple-element.670.refs_0_, bf16[512,1152]{1,0:T(8,128)(2,1)} %get-tuple-element.671.refs_1_, bf16[512,1152]{1,0:T(8,128)(2,1)} %get-tuple-element.672.refs_2_, bf16[512,1152]{1,0:T(8,128)(2,1)} %get-tuple-element.673.refs_3_, ...), custom_call_target="tpu_custom_call" | custom-call | flops 8858370048 | bytes 21757952 | tf_op jit(solution)/shard_map/pallas_call | solution.py:635
  413.8 13.8 %shard_map.282 = (f32[704,2048]{1,0:T(8,128)}, bf16[352,2048]{1,0:T(8,128)(2,1)}) custom-call(bf16[512,1152]{1,0:T(8,128)(2,1)} %get-tuple-element.736.refs_0_, bf16[512,1152]{1,0:T(8,128)(2,1)} %get-tuple-element.737.refs_1_, bf16[512,1152]{1,0:T(8,128)(2,1)} %get-tuple-element.738.refs_2_, bf16[512,1152]{1,0:T(8,128)(2,1)} %get-tuple-element.739.refs_3_, ...), custom_call_target="tpu_custom_call" | custom-call | flops 8858370048 | bytes 21757952 | tf_op jit(solution)/shard_map/pallas_call | solution.py:635
  427.6 13.9 %shard_map.283 = (f32[704,2048]{1,0:T(8,128)}, bf16[352,2048]{1,0:T(8,128)(2,1)}) custom-call(bf16[512,1152]{1,0:T(8,128)(2,1)} %get-tuple-element.724.refs_0_, bf16[512,1152]{1,0:T(8,128)(2,1)} %get-tuple-element.725.refs_1_, bf16[512,1152]{1,0:T(8,128)(2,1)} %get-tuple-element.726.refs_2_, bf16[512,1152]{1,0:T(8,128)(2,1)} %get-tuple-element.727.refs_3_, ...), custom_call_target="tpu_custom_call" | custom-call | flops 8858370048 | bytes 21757952 | tf_op jit(solution)/shard_map/pallas_call | solution.py:635
  457.9 13.2 %shard_map.284 = (bf16[512,1152]{1,0:T(8,128)(2,1)}, bf16[512,1152]{1,0:T(8,128)(2,1)}, bf16[512,1152]{1,0:T(8,128)(2,1)}, bf16[256,2048]{1,0:T(8,128)(2,1)}, bf...) custom-call(s32[2]{0:T(128)} %pad_add_fusion.2.expert, ...), custom_call_target="tpu_custom_call" | custom-call | flops 9663676416 | bytes 22544384 | tf_op jit(solution)/shard_map/pallas_call | solution.py:558
  478.9 10.8 %shard_map.285 = (bf16[1024,768]{1,0:T(8,128)(2,1)}, f32[1,768]{1,0:T(1,128)}) custom-call(s32[10]{0:T(128)} %pad_add_fusion.here, bf16[1024,768]{1,0:T(8,128)(2,1)} %get-tuple-element.781.low, bf16[1024,256]{1,0:T(8,128)(2,1)} %bitcast.232.incoming, f32[128,128]{1,0:T(8,128)} %get-tuple-element.983.cosine, f32[128,128]{1,0:T(8,128)} %get-tuple-element.981.sine, ...), custom_call_target="tpu_custom_call" | custom-call | flops 335544320 | bytes 3670016 | tf_op jit(solution)/shard_map/pallas_call | solution.py:264
  528.1 13.2 %shard_map.286 = (bf16[512,1152]{1,0:T(8,128)(2,1)}, bf16[512,1152]{1,0:T(8,128)(2,1)}, bf16[512,1152]{1,0:T(8,128)(2,1)}, bf16[256,2048]{1,0:T(8,128)(2,1)}, bf...) custom-call(s32[2]{0:T(128)} %pad_add_fusion.2.expert, ...), custom_call_target="tpu_custom_call" | custom-call | flops 9663676416 | bytes 22544384 | tf_op jit(solution)/shard_map/pallas_call | solution.py:558
  562.4 13.4 %shard_map.287 = (bf16[512,1152]{1,0:T(8,128)(2,1)}, bf16[512,1152]{1,0:T(8,128)(2,1)}, bf16[512,1152]{1,0:T(8,128)(2,1)}, bf16[256,2048]{1,0:T(8,128)(2,1)}, bf...) custom-call(s32[2]{0:T(128)} %pad_add_fusion.2.expert, ...), custom_call_target="tpu_custom_call" | custom-call | flops 9663676416 | bytes 22544384 | tf_op jit(solution)/shard_map/pallas_call | solution.py:558
  598.4 13.3 %shard_map.288 = (bf16[512,1152]{1,0:T(8,128)(2,1)}, bf16[512,1152]{1,0:T(8,128)(2,1)}, bf16[512,1152]{1,0:T(8,128)(2,1)}, bf16[256,2048]{1,0:T(8,128)(2,1)}, bf...) custom-call(s32[2]{0:T(128)} %pad_add_fusion.2.expert, ...), custom_call_target="tpu_custom_call" | custom-call | flops 9663676416 | bytes 22544384 | tf_op jit(solution)/shard_map/pallas_call | solution.py:558
  632.9 12.9 %shard_map.289 = f32[704,2048]{1,0:T(8,128)} custom-call(bf16[512,1152]{1,0:T(8,128)(2,1)} %get-tuple-element.884.refs_0_, bf16[512,1152]{1,0:T(8,128)(2,1)} %get-tuple-element.891.refs_1_, bf16[512,1152]{1,0:T(8,128)(2,1)} %get-tuple-element.898.refs_2_, bf16[512,1152]{1,0:T(8,128)(2,1)} %get-tuple-element.905.refs_3_, ...), custom_call_target="tpu_custom_call", output_to_operand_aliasing={{}: (12, {})} | custom-call | flops 5905580032 | bytes 23068672 | tf_op jit(solution)/shard_map/pallas_call | solution.py:635
  667.7 12.8 %shard_map.290 = f32[704,2048]{1,0:T(8,128)} custom-call(bf16[512,1152]{1,0:T(8,128)(2,1)} %get-tuple-element.925.refs_0_, bf16[512,1152]{1,0:T(8,128)(2,1)} %get-tuple-element.926.refs_1_, bf16[512,1152]{1,0:T(8,128)(2,1)} %get-tuple-element.927.refs_2_, bf16[512,1152]{1,0:T(8,128)(2,1)} %get-tuple-element.928.refs_3_, ...), custom_call_target="tpu_custom_call", output_to_operand_aliasing={{}: (12, {})} | custom-call | flops 5905580032 | bytes 23068672 | tf_op jit(solution)/shard_map/pallas_call | solution.py:635
  680.5 12.9 %shard_map.291 = f32[704,2048]{1,0:T(8,128)} custom-call(bf16[512,1152]{1,0:T(8,128)(2,1)} %get-tuple-element.938.refs_0_, bf16[512,1152]{1,0:T(8,128)(2,1)} %get-tuple-element.939.refs_1_, bf16[512,1152]{1,0:T(8,128)(2,1)} %get-tuple-element.940.refs_2_, bf16[512,1152]{1,0:T(8,128)(2,1)} %get-tuple-element.941.refs_3_, ...), custom_call_target="tpu_custom_call", output_to_operand_aliasing={{}: (12, {})} | custom-call | flops 5905580032 | bytes 23068672 | tf_op jit(solution)/shard_map/pallas_call | solution.py:635
  (497 shorter events, 348.1 us)
Async XLA Ops:
  24.4 39.0 %all-to-all-start = ((bf16[8,80,768]{2,1,0:T(8,128)(2,1)}), bf16[8,80,768]{2,1,0:T(8,128)(2,1)S(1)}, u32[]{:S(2)}, u32[]{:S(2)}) async-start(bf16[8,80,768]{2,1,0:T(8,128)(2,1)} %pad_maximum_fusion.4), calls=%async_computation | async-start | bytes 1966080 | tf_op jit(solution)/shard_map/all_to_all | solution.py:101
  183.6 49.6 %collective-permute-start.38 = (bf16[256,2048]{1,0:T(8,128)(2,1)}, bf16[256,2048]{1,0:T(8,128)(2,1)S(1)}, u32[]{:S(2)}, u32[]{:S(2)}) collective-permute-start(bf16[256,2048]{1,0:T(8,128)(2,1)} %constant_dynamic-update-slice_fusion.refs_2_.refs_4_), channel_id=1, source_target_pairs={{0,16},{16,0},{1,17},{17,1},{2,18},{18,2},{3,19},{19,3},{4,20},{20... | collective-permute-start | bytes 3145736 | tf_op jit(solution)/shard_map/ppermute | solution.py:83
  194.2 39.1 %collective-permute-start.39 = (bf16[256,2048]{1,0:T(8,128)(2,1)}, bf16[256,2048]{1,0:T(8,128)(2,1)}, u32[]{:S(2)}, u32[]{:S(2)}) collective-permute-start(bf16[256,2048]{1,0:T(8,128)(2,1)} %constant_dynamic-update-slice_fusion.2.refs_2_.refs_6_), channel_id=1, source_target_pairs={{0,16},{16,0},{1,17},{17,1},{2,18},{18,2},{3,19},{19,3},{4,20},{20... | collective-permute-start | bytes 3145736 | tf_op jit(solution)/shard_map/ppermute | solution.py:83
  196.5 36.7 %collective-permute-start.35 = (bf16[256,2048]{1,0:T(8,128)(2,1)}, bf16[256,2048]{1,0:T(8,128)(2,1)}, u32[]{:S(2)}, u32[]{:S(2)}) collective-permute-start(bf16[256,2048]{1,0:T(8,128)(2,1)} %pad_maximum_fusion.2.refs_0_.refs_4_), channel_id=1, source_target_pairs={{0,4},{1,5},{2,6},{3,7},{4,8},{5,9},{6,10},{7,11},{8,12},{9,13},{1... | collective-permute-start | bytes 3145736 | tf_op jit(solution)/shard_map/ppermute | solution.py:79
  198.3 34.9 %collective-permute-start.31 = (bf16[128,2048]{1,0:T(8,128)(2,1)S(1)}, bf16[128,2048]{1,0:T(8,128)(2,1)S(1)}, u32[]{:S(2)}, u32[]{:S(2)}) collective-permute-start(bf16[128,2048]{1,0:T(8,128)(2,1)S(1)} %collective-permute-done.30), channel_id=1, source_target_pairs={{0,4},{1,5},{2,6},{3,7},{4,8},{5,9},{6,10},{7,11},{8,12},{9,13},{1... | collective-permute-start | bytes 1572872 | tf_op jit(solution)/shard_map/ppermute | solution.py:79
  235.2 50.5 %collective-permute-start.41 = (bf16[256,2048]{1,0:T(8,128)(2,1)}, bf16[256,2048]{1,0:T(8,128)(2,1)S(1)}, u32[]{:S(2)}, u32[]{:S(2)}) collective-permute-start(bf16[256,2048]{1,0:T(8,128)(2,1)} %collective-permute-done.35.refs_0_.refs_6_), channel_id=1, source_target_pairs={{0,4},{1,5},{2,6},{3,7},{4,8},{5,9},{6,10},{7,11},{8,12},{9,13},{1... | collective-permute-start | bytes 3145736 | tf_op jit(solution)/shard_map/ppermute | solution.py:79
  295.7 33.1 %collective-permute-start.50 = (bf16[256,2048]{1,0:T(8,128)(2,1)S(1)}, bf16[256,2048]{1,0:T(8,128)(2,1)S(1)}, u32[]{:S(2)}, u32[]{:S(2)}) collective-permute-start(bf16[256,2048]{1,0:T(8,128)(2,1)S(1)} %add_convert_fusion.11), channel_id=1, source_target_pairs={{0,2},{1,3},{2,0},{3,1},{4,6},{5,7},{6,4},{7,5},{8,10},{9,11},{10,... | collective-permute-start | bytes 3145736 | tf_op jit(solution)/shard_map/ppermute | solution.py:79
  296.7 33.7 %collective-permute-start.45 = (bf16[256,2048]{1,0:T(8,128)(2,1)S(1)}, bf16[256,2048]{1,0:T(8,128)(2,1)}, u32[]{:S(2)}, u32[]{:S(2)}) collective-permute-start(bf16[256,2048]{1,0:T(8,128)(2,1)S(1)} %collective-permute-done.41.refs_0_.refs_8_), channel_id=1, source_target_pairs={{0,4},{1,5},{2,6},{3,7},{4,8},{5,9},{6,10},{7,11},{8,12},{9,13},{1... | collective-permute-start | bytes 3145736 | tf_op jit(solution)/shard_map/ppermute | solution.py:79
  298.2 32.1 %collective-permute-start.48 = (bf16[256,2048]{1,0:T(8,128)(2,1)}, bf16[256,2048]{1,0:T(8,128)(2,1)}, u32[]{:S(2)}, u32[]{:S(2)}) collective-permute-start(bf16[256,2048]{1,0:T(8,128)(2,1)} %pad_maximum_fusion.3.refs_2_.refs_10_), channel_id=1, source_target_pairs={{0,16},{16,0},{1,17},{17,1},{2,18},{18,2},{3,19},{19,3},{4,20},{20... | collective-permute-start | bytes 3145736 | tf_op jit(solution)/shard_map/ppermute | solution.py:83
  337.2 32.3 %collective-permute-start.55 = (bf16[256,2048]{1,0:T(8,128)(2,1)S(1)}, bf16[256,2048]{1,0:T(8,128)(2,1)S(1)}, u32[]{:S(2)}, u32[]{:S(2)}) collective-permute-start(bf16[256,2048]{1,0:T(8,128)(2,1)S(1)} %add_convert_fusion.9), channel_id=1, source_target_pairs={{0,2},{1,3},{2,0},{3,1},{4,6},{5,7},{6,4},{7,5},{8,10},{9,11},{10,... | collective-permute-start | bytes 3145736 | tf_op jit(solution)/shard_map/ppermute | solution.py:79
  407.0 50.8 %collective-permute-start.67 = (bf16[256,2048]{1,0:T(8,128)(2,1)}, bf16[256,2048]{1,0:T(8,128)(2,1)}, u32[]{:S(2)}, u32[]{:S(2)}) collective-permute-start(bf16[256,2048]{1,0:T(8,128)(2,1)} %copy-done.29), channel_id=1, source_target_pairs={{0,1},{1,0},{2,3},{3,2},{4,5},{5,4},{6,7},{7,6},{8,9},{9,8},{10,11... | collective-permute-start | bytes 3145736 | tf_op jit(solution)/shard_map/ppermute | solution.py:79
  407.6 50.3 %collective-permute-start.66 = (bf16[256,2048]{1,0:T(8,128)(2,1)}, bf16[256,2048]{1,0:T(8,128)(2,1)}, u32[]{:S(2)}, u32[]{:S(2)}) collective-permute-start(bf16[256,2048]{1,0:T(8,128)(2,1)} %copy-done.14), channel_id=1, source_target_pairs={{0,1},{1,0},{2,3},{3,2},{4,5},{5,4},{6,7},{7,6},{8,9},{9,8},{10,11... | collective-permute-start | bytes 3145736 | tf_op jit(solution)/shard_map/ppermute | solution.py:79
  407.6 35.9 %collective-permute-start.61 = (bf16[256,2048]{1,0:T(8,128)(2,1)}, bf16[256,2048]{1,0:T(8,128)(2,1)S(1)}, u32[]{:S(2)}, u32[]{:S(2)}) collective-permute-start(bf16[256,2048]{1,0:T(8,128)(2,1)} %copy-done.63), channel_id=1, source_target_pairs={{0,16},{16,0},{1,17},{17,1},{2,18},{18,2},{3,19},{19,3},{4,20},{20... | collective-permute-start | bytes 3145736 | tf_op jit(solution)/shard_map/ppermute | solution.py:83
  411.1 32.4 %collective-permute-start.64 = (bf16[256,2048]{1,0:T(8,128)(2,1)}, bf16[256,2048]{1,0:T(8,128)(2,1)S(1)}, u32[]{:S(2)}, u32[]{:S(2)}) collective-permute-start(bf16[256,2048]{1,0:T(8,128)(2,1)} %add_convert_fusion.3), channel_id=1, source_target_pairs={{0,4},{1,5},{2,6},{3,7},{4,8},{5,9},{6,10},{7,11},{8,12},{9,13},{1... | collective-permute-start | bytes 3145736 | tf_op jit(solution)/shard_map/ppermute | solution.py:79
  477.3 50.8 %collective-permute-start.72 = (bf16[256,2048]{1,0:T(8,128)(2,1)}, bf16[256,2048]{1,0:T(8,128)(2,1)}, u32[]{:S(2)}, u32[]{:S(2)}) collective-permute-start(bf16[256,2048]{1,0:T(8,128)(2,1)} %collective-permute-done.39.refs_2_.refs_6_), channel_id=1, source_target_pairs={{0,1},{1,0},{2,3},{3,2},{4,5},{5,4},{6,7},{7,6},{8,9},{9,8},{10,11... | collective-permute-start | bytes 3145736 | tf_op jit(solution)/shard_map/ppermute | solution.py:79
  477.3 50.8 %collective-permute-start.71 = (bf16[256,2048]{1,0:T(8,128)(2,1)}, bf16[256,2048]{1,0:T(8,128)(2,1)}, u32[]{:S(2)}, u32[]{:S(2)}) collective-permute-start(bf16[256,2048]{1,0:T(8,128)(2,1)} %collective-permute-done.57.refs_0_.refs_6_), channel_id=1, source_target_pairs={{0,1},{1,0},{2,3},{3,2},{4,5},{5,4},{6,7},{7,6},{8,9},{9,8},{10,11... | collective-permute-start | bytes 3145736 | tf_op jit(solution)/shard_map/ppermute | solution.py:79
  477.9 33.8 %collective-permute-start.70 = (bf16[352,2048]{1,0:T(8,128)(2,1)}, bf16[352,2048]{1,0:T(8,128)(2,1)}, u32[]{:S(2)}, u32[]{:S(2)}) collective-permute-start(bf16[352,2048]{1,0:T(8,128)(2,1)} %get-tuple-element.951), channel_id=1, source_target_pairs={{0,16},{16,0},{1,17},{17,1},{2,18},{18,2},{3,19},{19,3},{4,20},{20... | collective-permute-start | bytes 4325384 | tf_op jit(solution)/shard_map/ppermute | solution.py:83
  551.5 45.9 %collective-permute-start.81 = (bf16[256,2048]{1,0:T(8,128)(2,1)}, bf16[256,2048]{1,0:T(8,128)(2,1)}, u32[]{:S(2)}, u32[]{:S(2)}) collective-permute-start(bf16[256,2048]{1,0:T(8,128)(2,1)} %collective-permute-done.48.refs_2_.refs_10_), channel_id=1, source_target_pairs={{0,1},{1,0},{2,3},{3,2},{4,5},{5,4},{6,7},{7,6},{8,9},{9,8},{10,11... | collective-permute-start | bytes 3145736 | tf_op jit(solution)/shard_map/ppermute | solution.py:79
  553.0 45.4 %collective-permute-start.80 = (bf16[256,2048]{1,0:T(8,128)(2,1)}, bf16[256,2048]{1,0:T(8,128)(2,1)}, u32[]{:S(2)}, u32[]{:S(2)}) collective-permute-start(bf16[256,2048]{1,0:T(8,128)(2,1)} %collective-permute-done.65.refs_0_.refs_10_), channel_id=1, source_target_pairs={{0,1},{1,0},{2,3},{3,2},{4,5},{5,4},{6,7},{7,6},{8,9},{9,8},{10,11... | collective-permute-start | bytes 3145736 | tf_op jit(solution)/shard_map/ppermute | solution.py:79
  597.4 56.8 %collective-permute-start.86 = (bf16[352,2048]{1,0:T(8,128)(2,1)}, bf16[352,2048]{1,0:T(8,128)(2,1)}, u32[]{:S(2)}, u32[]{:S(2)}) collective-permute-start(bf16[352,2048]{1,0:T(8,128)(2,1)} %get-tuple-element.953), channel_id=1, source_target_pairs={{0,16},{16,0},{1,17},{17,1},{2,18},{18,2},{3,19},{19,3},{4,20},{20... | collective-permute-start | bytes 4325384 | tf_op jit(solution)/shard_map/ppermute | solution.py:83
  659.2 41.1 %collective-permute-start.95 = (bf16[64,2048]{1,0:T(8,128)(2,1)S(1)}, bf16[64,2048]{1,0:T(8,128)(2,1)S(1)}, u32[]{:S(2)}, u32[]{:S(2)}) collective-permute-start(bf16[64,2048]{1,0:T(8,128)(2,1)S(1)} %get-tuple-element.965), channel_id=1, source_target_pairs={{0,12},{1,13},{2,14},{3,15},{4,0},{5,1},{6,2},{7,3},{8,4},{9,5},{1... | collective-permute-start | bytes 786440 | tf_op jit(solution)/shard_map/ppermute | solution.py:79
  662.6 37.6 %collective-permute-start.94 = (bf16[64,2048]{1,0:T(8,128)(2,1)S(1)}, bf16[64,2048]{1,0:T(8,128)(2,1)S(1)}, u32[]{:S(2)}, u32[]{:S(2)}) collective-permute-start(bf16[64,2048]{1,0:T(8,128)(2,1)S(1)} %get-tuple-element.966), channel_id=1, source_target_pairs={{0,8},{1,9},{2,10},{3,11},{4,12},{5,13},{6,14},{7,15},{8,0},{9,1},... | collective-permute-start | bytes 786440 | tf_op jit(solution)/shard_map/ppermute | solution.py:79
  662.6 37.6 %collective-permute-start.93 = (bf16[64,2048]{1,0:T(8,128)(2,1)S(1)}, bf16[64,2048]{1,0:T(8,128)(2,1)S(1)}, u32[]{:S(2)}, u32[]{:S(2)}) collective-permute-start(bf16[64,2048]{1,0:T(8,128)(2,1)S(1)} %get-tuple-element.964), channel_id=1, source_target_pairs={{0,4},{1,5},{2,6},{3,7},{4,8},{5,9},{6,10},{7,11},{8,12},{9,13},{1... | collective-permute-start | bytes 786440 | tf_op jit(solution)/shard_map/ppermute | solution.py:79
  663.3 37.9 %collective-permute-start.96 = (bf16[352,2048]{1,0:T(8,128)(2,1)S(1)}, bf16[352,2048]{1,0:T(8,128)(2,1)S(1)}, u32[]{:S(2)}, u32[]{:S(2)}) collective-permute-start(bf16[352,2048]{1,0:T(8,128)(2,1)S(1)} %copy-done.28), channel_id=1, source_target_pairs={{0,16},{16,0},{1,17},{17,1},{2,18},{18,2},{3,19},{19,3},{4,20},{20... | collective-permute-start | bytes 4325384 | tf_op jit(solution)/shard_map/ppermute | solution.py:83
  (151 other events, 2709.2 us)

commit v4 on v3

--- a/solution.py
+++ b/solution.py
@@ -251,7 +251,7 @@
             ],
         ),
         cost_estimate=pl.CostEstimate(
-            flops=4 * tokens * rows * width, bytes_accessed=tokens * width * 20, transcendentals=0
+            flops=300 * tokens * rows * width, bytes_accessed=tokens * width * 20, transcendentals=0
         ),
     )(here, raw, bias, cosine, sine * sign)
 
@@ -283,7 +283,7 @@
             ],
         ),
         cost_estimate=pl.CostEstimate(
-            flops=10 * tokens * rows * width, bytes_accessed=tokens * width * 14, transcendentals=0
+            flops=370 * tokens * rows * width, bytes_accessed=tokens * width * 14, transcendentals=0
         ),
     )(here, low, incoming, *rope_inputs(rows))
 
@@ -403,7 +403,7 @@
         ],
         compiler_params=pltpu.CompilerParams(vmem_limit_bytes=VMEM),
         cost_estimate=pl.CostEstimate(
-            flops=2 * tokens * features * columns,
+            flops=7 * tokens * features * columns,
             bytes_accessed=4 * (tokens * features + weight_rows * columns + tokens * columns),
             transcendentals=0,
         ),
@@ -529,7 +529,7 @@
         copy.wait()
 
 
-def experts(expert, meta, vector, rows, grads, into, down, routed):
+def experts(expert, meta, vector, rows, grads, into, down, routed, terms_too):
     pieces, features = len(rows), rows[0].shape[1]
     tokens, units = sum(piece.shape[0] for piece in rows), down.shape[0]
     rest, count = meta.shape[0], meta.shape[-1]
@@ -564,7 +564,7 @@
         scratch_shapes=scratch,
         compiler_params=pltpu.CompilerParams(vmem_limit_bytes=VMEM),
         cost_estimate=pl.CostEstimate(
-            flops=2 * tokens * features * units * 4,
+            flops=2 * tokens * features * units * (12 if terms_too else 6),
             bytes_accessed=2 * (into.size + down.size + 4 * tokens * features),
             transcendentals=0,
         ),
@@ -650,7 +650,7 @@
         input_output_aliases={pieces + n: n for n in range(len(sizes))} if adds else {},
         compiler_params=pltpu.CompilerParams(vmem_limit_bytes=VMEM),
         cost_estimate=pl.CostEstimate(
-            flops=2 * tokens * features * sum(sizes),
+            flops=4 * tokens * features * sum(sizes),
             bytes_accessed=tokens * (features + used) * 2
             + features * sum(sizes) * 4 * (1 + adds),
             transcendentals=0,
@@ -884,7 +884,7 @@
     arrived, out_weight = tie(arrived, out_weight)
 
     far_grads, far_rows, flying = [], [], []
-    crossings = [("grads", s) for s in slots] + [("rows", s) for s in slots]
+    crossings = [(what, s) for s in slots for what in ("grads", "rows")]
 
     def cross_step():
         if crossings and two:
@@ -916,7 +916,7 @@
         own["grads"].append(with_other(grad_rounds.blocks[s]))
         middle, gate, up, *terms, vector = experts(
             expert, told[0, s], vector_row, own["rows"][s], own["grads"][s],
-            into_rows, down_rows, sizes[0],
+            into_rows, down_rows, sizes[0], True,
         )
         for name, value in (("middle", middle), ("gate", gate), ("up", up), ("vector", vector)):
             own[name].append(value)
@@ -951,7 +951,7 @@
         rows, grads = with_other(far_rows[s]), with_other(far_grads[s])
         units = experts(
             far_expert, told[shift, s], vector_row, rows, grads,
-            into_rows, down_rows, sizes[0],
+            into_rows, down_rows, sizes[0], False,
         )
         return rows, grads, units[:3]
 
@@ -962,9 +962,9 @@
     sums = None
     for s in slots:
         second_rounds.line()
+        cross_step()
         if s:
             grad_rounds.rest()
-        cross_step()
         if s >= 2:
             rowed[s - 1] = grid.row_sum(add_cores(terms[s - 1]))
         if s >= 3:

time: 714 us -> 692 us (0.969)
  starting transfers between devices: 106 us -> 96.8 us
  other arithmetic: 76.3 us -> 68.8 us
    ppermute x77, waiting for transfers between devices: 133 us -> 122 us  [hop(): return lax.ppermute(values, 'ep', pairs)]
    ppermute x77, starting transfers between devices: 62.3 us -> 54.6 us  [hop(): return lax.ppermute(values, 'ep', pairs)]
    unnamed x154 -> x159, local copies, waits for them, and re-layouts: 16.3 us -> 16.6 us
  transfers between devices with their start and end apart: 101 -> 101, of which waited for: 31 -> 35; matrix products, arithmetic and copies ran while one was open for 18% -> 18% of each run, Pallas kernels for 41% -> 43%
where the time goes in v4:
time: 692 us; the launch traced here: 681 us
  Pallas kernels  290 us (42%)
  waiting for transfers between devices  153 us (22%)
  starting transfers between devices  96.8 us (14%)
  other arithmetic  68.8 us (10%)
  local copies, waits for them, and re-layouts  43.9 us (6%)
  matrix products  26 us (4%)
    pallas_call x8, Pallas kernels, experts(): pl.pallas_call(functools.partial(experts_kernel, pieces, routed + -routed...  160 us
    ppermute x77, waiting for transfers between devices, hop(): return lax.ppermute(values, 'ep', pairs)  122 us
    pallas_call x6, Pallas kernels, weight_grad(): pl.pallas_call(functools.partial(weight_grad_kernel, unit_counts, row_cou...  80.5 us
    ppermute x77, starting transfers between devices, hop(): return lax.ppermute(values, 'ep', pairs)  54.6 us
    dot_general x8, matrix products, dot(): lax.dot_general(left, right, (dims, ((), ())), preferred_element_type=f32)  26 us
    ppermute x20, starting transfers between devices, cross(): return lax.ppermute(values, 'dp', pairs)  23.8 us
    ppermute x20, waiting for transfers between devices, cross(): return lax.ppermute(values, 'dp', pairs)  20.4 us
    pallas_call x3, Pallas kernels, pack(): pl.pallas_call(functools.partial(pack_kernel, len(pieces), moves, blanks)...  19.2 us
  transfers between devices with their start and end apart: 101, of which 35 were waited for; matrix products, arithmetic and copies ran while one was open for 18% of the time, Pallas kernels for 43%

profile of v4, /device:TPU:0, one launch (start us, length us, event | category | flops | bytes accessed | tf_op | source)
XLA Modules:
  0.0 681.3 jit_solution(17851440893796145112)
XLA Ops:
  13.5 10.0 %collective-permute-done = bf16[64,2048]{1,0:T(8,128)(2,1)S(1)} collective-permute-done((bf16[64,2048]{1,0:T(8,128)(2,1)}, bf16[64,2048]{1,0:T(8,128)(2,1)S(1)}, u32[]{:S(2)}, u32[]{:S(2)}) %collective-permute-start) | collective-permute-done | bytes 262176 | tf_op jit(solution)/shard_map/ppermute | solution.py:79
  39.6 17.8 %collective-permute-done.3 = bf16[64,2048]{1,0:T(8,128)(2,1)S(1)} collective-permute-done((bf16[64,2048]{1,0:T(8,128)(2,1)S(1)}, bf16[64,2048]{1,0:T(8,128)(2,1)S(1)}, u32[]{:S(2)}, u32[]{:S(2)}) %collective-permute-start.3) | collective-permute-done | bytes 262176 | tf_op jit(solution)/shard_map/ppermute | solution.py:79
  72.7 10.5 %collective-permute-done.7 = bf16[64,2048]{1,0:T(8,128)(2,1)S(1)} collective-permute-done((bf16[64,2048]{1,0:T(8,128)(2,1)S(1)}, bf16[64,2048]{1,0:T(8,128)(2,1)S(1)}, u32[]{:S(2)}, u32[]{:S(2)}) %collective-permute-start.7) | collective-permute-done | bytes 262176 | tf_op jit(solution)/shard_map/ppermute | solution.py:79
  113.6 10.0 %shard_map.274 = (bf16[1024,2048]{1,0:T(8,128)(2,1)}, bf16[2048,768]{1,0:T(8,128)(2,1)}, f32[1024,768]{1,0:T(8,128)}) custom-call(s32[32]{0:T(128)} %stack.733.order, f32[1,2048]{1,0:T(1,128)} %bitcast.397, bf16[128,2048]{1,0:T(8,128)(2,1)} %refs_0_, bf16[128,2048]{1,0:T(8,128)(2,1)} %copy-done.71, bf16[128,2048]{1,0:T(8,128)(2,1)} %copy-done.70, ...), custom_call_target="tpu_custom_call" | custom-call | flops 11274289152 | bytes 17825792 | tf_op jit(solution)/shard_map/pallas_call | solution.py:386
  123.6 8.7 %shard_map.275 = (bf16[1024,768]{1,0:T(8,128)(2,1)}, bf16[1024,256]{1,0:T(8,128)(2,1)}) custom-call(s32[10]{0:T(128)} %pad_add_fusion.here, f32[1024,768]{1,0:T(8,128)} %get-tuple-element.534.raw, f32[1,768]{1,0:T(1,128)} %broadcast_in_dim.112.bias, f32[128,128]{1,0:T(8,128)} %get-tuple-element.977.cosine, f32[128,128]{1,0:T(8,128)} %get-tuple-element.976.signed_sine), custom_call_target="tpu_custom_call" | custom-call | flops 10066329600 | bytes 5242880 | tf_op jit(solution)/shard_map/pallas_call | solution.py:233
  170.3 9.0 %collective-permute-done.34 = bf16[128,2048]{1,0:T(8,128)(2,1)S(1)} collective-permute-done((bf16[128,2048]{1,0:T(8,128)(2,1)S(1)}, bf16[128,2048]{1,0:T(8,128)(2,1)S(1)}, u32[]{:S(2)}, u32[]{:S(2)}) %collective-permute-start.34) | collective-permute-done | bytes 524320 | tf_op jit(solution)/shard_map/ppermute | solution.py:79
  186.5 9.9 %collective-permute-done.30 = bf16[128,2048]{1,0:T(8,128)(2,1)S(1)} collective-permute-done((bf16[128,2048]{1,0:T(8,128)(2,1)S(1)}, bf16[128,2048]{1,0:T(8,128)(2,1)S(1)}, u32[]{:S(2)}, u32[]{:S(2)}) %collective-permute-start.30) | collective-permute-done | bytes 524320 | tf_op jit(solution)/shard_map/ppermute | solution.py:79
  199.4 27.2 %shard_map.277 = (bf16[512,1152]{1,0:T(8,128)(2,1)}, bf16[512,1152]{1,0:T(8,128)(2,1)}, bf16[512,1152]{1,0:T(8,128)(2,1)}, bf16[256,2048]{1,0:T(8,128)(2,1)}, bf...) custom-call(s32[2]{0:T(128)} %pad_add_fusion.1.expert, ...), custom_call_target="tpu_custom_call" | custom-call | flops 28991029248 | bytes 22544384 | tf_op jit(solution)/shard_map/pallas_call | solution.py:558
  237.7 27.0 %shard_map.278 = (bf16[512,1152]{1,0:T(8,128)(2,1)}, bf16[512,1152]{1,0:T(8,128)(2,1)}, bf16[512,1152]{1,0:T(8,128)(2,1)}, bf16[256,2048]{1,0:T(8,128)(2,1)}, bf...) custom-call(s32[2]{0:T(128)} %pad_add_fusion.1.expert, ...), custom_call_target="tpu_custom_call" | custom-call | flops 28991029248 | bytes 22544384 | tf_op jit(solution)/shard_map/pallas_call | solution.py:558
  276.0 26.9 %shard_map.279 = (bf16[512,1152]{1,0:T(8,128)(2,1)}, bf16[512,1152]{1,0:T(8,128)(2,1)}, bf16[512,1152]{1,0:T(8,128)(2,1)}, bf16[256,2048]{1,0:T(8,128)(2,1)}, bf...) custom-call(s32[2]{0:T(128)} %pad_add_fusion.1.expert, ...), custom_call_target="tpu_custom_call" | custom-call | flops 28991029248 | bytes 22544384 | tf_op jit(solution)/shard_map/pallas_call | solution.py:558
  315.0 26.9 %shard_map.280 = (bf16[512,1152]{1,0:T(8,128)(2,1)}, bf16[512,1152]{1,0:T(8,128)(2,1)}, bf16[512,1152]{1,0:T(8,128)(2,1)}, bf16[256,2048]{1,0:T(8,128)(2,1)}, bf...) custom-call(s32[2]{0:T(128)} %pad_add_fusion.1.expert, ...), custom_call_target="tpu_custom_call" | custom-call | flops 28991029248 | bytes 22544384 | tf_op jit(solution)/shard_map/pallas_call | solution.py:558
  352.4 13.8 %shard_map.281 = (f32[704,2048]{1,0:T(8,128)}, bf16[352,2048]{1,0:T(8,128)(2,1)}) custom-call(bf16[512,1152]{1,0:T(8,128)(2,1)} %get-tuple-element.664.refs_0_, bf16[512,1152]{1,0:T(8,128)(2,1)} %get-tuple-element.665.refs_1_, bf16[512,1152]{1,0:T(8,128)(2,1)} %get-tuple-element.666.refs_2_, bf16[512,1152]{1,0:T(8,128)(2,1)} %get-tuple-element.667.refs_3_, ...), custom_call_target="tpu_custom_call" | custom-call | flops 17716740096 | bytes 21757952 | tf_op jit(solution)/shard_map/pallas_call | solution.py:635
  366.2 10.0 %collective-permute-done.59 = bf16[256,2048]{1,0:T(8,128)(2,1)S(1)} collective-permute-done((bf16[256,2048]{1,0:T(8,128)(2,1)S(1)}, bf16[256,2048]{1,0:T(8,128)(2,1)S(1)}, u32[]{:S(2)}, u32[]{:S(2)}) %collective-permute-start.59) | collective-permute-done | bytes 1048608 | tf_op jit(solution)/shard_map/ppermute | solution.py:79
  382.9 13.8 %shard_map.282 = (f32[704,2048]{1,0:T(8,128)}, bf16[352,2048]{1,0:T(8,128)(2,1)}) custom-call(bf16[512,1152]{1,0:T(8,128)(2,1)} %get-tuple-element.730.refs_0_, bf16[512,1152]{1,0:T(8,128)(2,1)} %get-tuple-element.731.refs_1_, bf16[512,1152]{1,0:T(8,128)(2,1)} %get-tuple-element.732.refs_2_, bf16[512,1152]{1,0:T(8,128)(2,1)} %get-tuple-element.733.refs_3_, ...), custom_call_target="tpu_custom_call" | custom-call | flops 17716740096 | bytes 21757952 | tf_op jit(solution)/shard_map/pallas_call | solution.py:635
  398.2 13.8 %shard_map.283 = (f32[704,2048]{1,0:T(8,128)}, bf16[352,2048]{1,0:T(8,128)(2,1)}) custom-call(bf16[512,1152]{1,0:T(8,128)(2,1)} %get-tuple-element.718.refs_0_, bf16[512,1152]{1,0:T(8,128)(2,1)} %get-tuple-element.719.refs_1_, bf16[512,1152]{1,0:T(8,128)(2,1)} %get-tuple-element.720.refs_2_, bf16[512,1152]{1,0:T(8,128)(2,1)} %get-tuple-element.721.refs_3_, ...), custom_call_target="tpu_custom_call" | custom-call | flops 17716740096 | bytes 21757952 | tf_op jit(solution)/shard_map/pallas_call | solution.py:635
  412.0 10.4 %collective-permute-done.63 = bf16[256,2048]{1,0:T(8,128)(2,1)S(1)} collective-permute-done((bf16[256,2048]{1,0:T(8,128)(2,1)S(1)}, bf16[256,2048]{1,0:T(8,128)(2,1)S(1)}, u32[]{:S(2)}, u32[]{:S(2)}) %collective-permute-start.63) | collective-permute-done | bytes 1048608 | tf_op jit(solution)/shard_map/ppermute | solution.py:79
  435.0 13.0 %shard_map.284 = (bf16[512,1152]{1,0:T(8,128)(2,1)}, bf16[512,1152]{1,0:T(8,128)(2,1)}, bf16[512,1152]{1,0:T(8,128)(2,1)}, bf16[256,2048]{1,0:T(8,128)(2,1)}, bf...) custom-call(s32[2]{0:T(128)} %pad_add_fusion.2.expert, ...), custom_call_target="tpu_custom_call" | custom-call | flops 14495514624 | bytes 22544384 | tf_op jit(solution)/shard_map/pallas_call | solution.py:558
  455.1 10.8 %shard_map.285 = (bf16[1024,768]{1,0:T(8,128)(2,1)}, f32[1,768]{1,0:T(1,128)}) custom-call(s32[10]{0:T(128)} %pad_add_fusion.here, bf16[1024,768]{1,0:T(8,128)(2,1)} %get-tuple-element.775.low, bf16[1024,256]{1,0:T(8,128)(2,1)} %bitcast.390, f32[128,128]{1,0:T(8,128)} %get-tuple-element.977.cosine, f32[128,128]{1,0:T(8,128)} %get-tuple-element.975.sine, ...), custom_call_target="tpu_custom_call" | custom-call | flops 12415139840 | bytes 3670016 | tf_op jit(solution)/shard_map/pallas_call | solution.py:264
  502.7 13.1 %shard_map.286 = (bf16[512,1152]{1,0:T(8,128)(2,1)}, bf16[512,1152]{1,0:T(8,128)(2,1)}, bf16[512,1152]{1,0:T(8,128)(2,1)}, bf16[256,2048]{1,0:T(8,128)(2,1)}, bf...) custom-call(s32[2]{0:T(128)} %pad_add_fusion.2.expert, ...), custom_call_target="tpu_custom_call" | custom-call | flops 14495514624 | bytes 22544384 | tf_op jit(solution)/shard_map/pallas_call | solution.py:558
  538.0 13.3 %shard_map.287 = (bf16[512,1152]{1,0:T(8,128)(2,1)}, bf16[512,1152]{1,0:T(8,128)(2,1)}, bf16[512,1152]{1,0:T(8,128)(2,1)}, bf16[256,2048]{1,0:T(8,128)(2,1)}, bf...) custom-call(s32[2]{0:T(128)} %pad_add_fusion.2.expert, ...), custom_call_target="tpu_custom_call" | custom-call | flops 14495514624 | bytes 22544384 | tf_op jit(solution)/shard_map/pallas_call | solution.py:558
  573.6 13.2 %shard_map.288 = (bf16[512,1152]{1,0:T(8,128)(2,1)}, bf16[512,1152]{1,0:T(8,128)(2,1)}, bf16[512,1152]{1,0:T(8,128)(2,1)}, bf16[256,2048]{1,0:T(8,128)(2,1)}, bf...) custom-call(s32[2]{0:T(128)} %pad_add_fusion.2.expert, ...), custom_call_target="tpu_custom_call" | custom-call | flops 14495514624 | bytes 22544384 | tf_op jit(solution)/shard_map/pallas_call | solution.py:558
  607.2 12.9 %shard_map.289 = f32[704,2048]{1,0:T(8,128)} custom-call(bf16[512,1152]{1,0:T(8,128)(2,1)} %get-tuple-element.878.refs_0_, bf16[512,1152]{1,0:T(8,128)(2,1)} %get-tuple-element.885.refs_1_, bf16[512,1152]{1,0:T(8,128)(2,1)} %get-tuple-element.892.refs_2_, bf16[512,1152]{1,0:T(8,128)(2,1)} %get-tuple-element.899.refs_3_, ...), custom_call_target="tpu_custom_call", output_to_operand_aliasing={{}: (12, {})} | custom-call | flops 11811160064 | bytes 23068672 | tf_op jit(solution)/shard_map/pallas_call | solution.py:635
  631.0 12.8 %shard_map.290 = f32[704,2048]{1,0:T(8,128)} custom-call(bf16[512,1152]{1,0:T(8,128)(2,1)} %get-tuple-element.919.refs_0_, bf16[512,1152]{1,0:T(8,128)(2,1)} %get-tuple-element.920.refs_1_, bf16[512,1152]{1,0:T(8,128)(2,1)} %get-tuple-element.921.refs_2_, bf16[512,1152]{1,0:T(8,128)(2,1)} %get-tuple-element.922.refs_3_, ...), custom_call_target="tpu_custom_call", output_to_operand_aliasing={{}: (12, {})} | custom-call | flops 11811160064 | bytes 23068672 | tf_op jit(solution)/shard_map/pallas_call | solution.py:635
  643.9 13.4 %shard_map.291 = f32[704,2048]{1,0:T(8,128)} custom-call(bf16[512,1152]{1,0:T(8,128)(2,1)} %get-tuple-element.932.refs_0_, bf16[512,1152]{1,0:T(8,128)(2,1)} %get-tuple-element.933.refs_1_, bf16[512,1152]{1,0:T(8,128)(2,1)} %get-tuple-element.934.refs_2_, bf16[512,1152]{1,0:T(8,128)(2,1)} %get-tuple-element.935.refs_3_, ...), custom_call_target="tpu_custom_call", output_to_operand_aliasing={{}: (12, {})} | custom-call | flops 11811160064 | bytes 23068672 | tf_op jit(solution)/shard_map/pallas_call | solution.py:635
  (502 shorter events, 329.9 us)
Async XLA Ops:
  23.5 39.7 %all-to-all-start = ((bf16[8,80,768]{2,1,0:T(8,128)(2,1)}), bf16[8,80,768]{2,1,0:T(8,128)(2,1)}, u32[]{:S(2)}, u32[]{:S(2)}) async-start(bf16[8,80,768]{2,1,0:T(8,128)(2,1)} %pad_maximum_fusion.5), calls=%async_computation | async-start | bytes 1966080 | tf_op jit(solution)/shard_map/all_to_all | solution.py:101
  184.7 41.9 %collective-permute-start.38 = (bf16[256,2048]{1,0:T(8,128)(2,1)}, bf16[256,2048]{1,0:T(8,128)(2,1)S(1)}, u32[]{:S(2)}, u32[]{:S(2)}) collective-permute-start(bf16[256,2048]{1,0:T(8,128)(2,1)} %constant_dynamic-update-slice_fusion.refs_2_.refs_4_), channel_id=1, source_target_pairs={{0,16},{16,0},{1,17},{17,1},{2,18},{18,2},{3,19},{19,3},{4,20},{20... | collective-permute-start | bytes 3145736 | tf_op jit(solution)/shard_map/ppermute | solution.py:83
  197.5 35.1 %collective-permute-start.35 = (bf16[256,2048]{1,0:T(8,128)(2,1)S(1)}, bf16[256,2048]{1,0:T(8,128)(2,1)}, u32[]{:S(2)}, u32[]{:S(2)}) collective-permute-start(bf16[256,2048]{1,0:T(8,128)(2,1)S(1)} %pad_maximum_fusion.3.refs_0_.refs_4_), channel_id=1, source_target_pairs={{0,4},{1,5},{2,6},{3,7},{4,8},{5,9},{6,10},{7,11},{8,12},{9,13},{1... | collective-permute-start | bytes 3145736 | tf_op jit(solution)/shard_map/ppermute | solution.py:79
  197.6 35.0 %collective-permute-start.39 = (bf16[256,2048]{1,0:T(8,128)(2,1)S(1)}, bf16[256,2048]{1,0:T(8,128)(2,1)S(1)}, u32[]{:S(2)}, u32[]{:S(2)}) collective-permute-start(bf16[256,2048]{1,0:T(8,128)(2,1)S(1)} %pad_maximum_fusion.3.refs_0_.refs_4_), channel_id=1, source_target_pairs={{0,16},{16,0},{1,17},{17,1},{2,18},{18,2},{3,19},{19,3},{4,20},{20... | collective-permute-start | bytes 3145736 | tf_op jit(solution)/shard_map/ppermute | solution.py:83
  233.1 32.9 %collective-permute-start.41 = (bf16[256,2048]{1,0:T(8,128)(2,1)}, bf16[256,2048]{1,0:T(8,128)(2,1)}, u32[]{:S(2)}, u32[]{:S(2)}) collective-permute-start(bf16[256,2048]{1,0:T(8,128)(2,1)} %collective-permute-done.35.refs_0_.refs_6_), channel_id=1, source_target_pairs={{0,4},{1,5},{2,6},{3,7},{4,8},{5,9},{6,10},{7,11},{8,12},{9,13},{1... | collective-permute-start | bytes 3145736 | tf_op jit(solution)/shard_map/ppermute | solution.py:79
  233.1 32.9 %collective-permute-start.44 = (bf16[256,2048]{1,0:T(8,128)(2,1)S(1)}, bf16[256,2048]{1,0:T(8,128)(2,1)}, u32[]{:S(2)}, u32[]{:S(2)}) collective-permute-start(bf16[256,2048]{1,0:T(8,128)(2,1)S(1)} %pad_maximum_fusion.2.refs_2_.refs_6_), channel_id=1, source_target_pairs={{0,16},{16,0},{1,17},{17,1},{2,18},{18,2},{3,19},{19,3},{4,20},{20... | collective-permute-start | bytes 3145736 | tf_op jit(solution)/shard_map/ppermute | solution.py:83
  267.4 38.4 %collective-permute-start.45 = (bf16[256,2048]{1,0:T(8,128)(2,1)}, bf16[256,2048]{1,0:T(8,128)(2,1)}, u32[]{:S(2)}, u32[]{:S(2)}) collective-permute-start(bf16[256,2048]{1,0:T(8,128)(2,1)} %collective-permute-done.41.refs_0_.refs_8_), channel_id=1, source_target_pairs={{0,4},{1,5},{2,6},{3,7},{4,8},{5,9},{6,10},{7,11},{8,12},{9,13},{1... | collective-permute-start | bytes 3145736 | tf_op jit(solution)/shard_map/ppermute | solution.py:79
  268.1 37.7 %collective-permute-start.48 = (bf16[256,2048]{1,0:T(8,128)(2,1)}, bf16[256,2048]{1,0:T(8,128)(2,1)}, u32[]{:S(2)}, u32[]{:S(2)}) collective-permute-start(bf16[256,2048]{1,0:T(8,128)(2,1)} %collective-permute-done.35.refs_0_.refs_6_), channel_id=1, source_target_pairs={{0,16},{16,0},{1,17},{17,1},{2,18},{18,2},{3,19},{19,3},{4,20},{20... | collective-permute-start | bytes 3145736 | tf_op jit(solution)/shard_map/ppermute | solution.py:83
  306.5 35.9 %collective-permute-start.53 = (bf16[256,2048]{1,0:T(8,128)(2,1)}, bf16[256,2048]{1,0:T(8,128)(2,1)}, u32[]{:S(2)}, u32[]{:S(2)}) collective-permute-start(bf16[256,2048]{1,0:T(8,128)(2,1)} %pad_maximum_fusion.1.refs_2_.refs_8_), channel_id=1, source_target_pairs={{0,16},{16,0},{1,17},{17,1},{2,18},{18,2},{3,19},{19,3},{4,20},{20... | collective-permute-start | bytes 3145736 | tf_op jit(solution)/shard_map/ppermute | solution.py:83
  308.3 34.1 %collective-permute-start.56 = (bf16[256,2048]{1,0:T(8,128)(2,1)}, bf16[256,2048]{1,0:T(8,128)(2,1)}, u32[]{:S(2)}, u32[]{:S(2)}) collective-permute-start(bf16[256,2048]{1,0:T(8,128)(2,1)} %convert_add_fusion.10), channel_id=1, source_target_pairs={{0,4},{1,5},{2,6},{3,7},{4,8},{5,9},{6,10},{7,11},{8,12},{9,13},{1... | collective-permute-start | bytes 3145736 | tf_op jit(solution)/shard_map/ppermute | solution.py:79
  344.6 90.4 %collective-permute-start.66 = (bf16[256,2048]{1,0:T(8,128)(2,1)}, bf16[256,2048]{1,0:T(8,128)(2,1)}, u32[]{:S(2)}, u32[]{:S(2)}) collective-permute-start(bf16[256,2048]{1,0:T(8,128)(2,1)} %copy-done.63), channel_id=1, source_target_pairs={{0,1},{1,0},{2,3},{3,2},{4,5},{5,4},{6,7},{7,6},{8,9},{9,8},{10,11... | collective-permute-start | bytes 3145736 | tf_op jit(solution)/shard_map/ppermute | solution.py:79
  344.8 90.2 %collective-permute-start.67 = (bf16[256,2048]{1,0:T(8,128)(2,1)}, bf16[256,2048]{1,0:T(8,128)(2,1)}, u32[]{:S(2)}, u32[]{:S(2)}) collective-permute-start(bf16[256,2048]{1,0:T(8,128)(2,1)} %copy-done.62), channel_id=1, source_target_pairs={{0,1},{1,0},{2,3},{3,2},{4,5},{5,4},{6,7},{7,6},{8,9},{9,8},{10,11... | collective-permute-start | bytes 3145736 | tf_op jit(solution)/shard_map/ppermute | solution.py:79
  345.1 32.8 %collective-permute-start.57 = (bf16[256,2048]{1,0:T(8,128)(2,1)}, bf16[256,2048]{1,0:T(8,128)(2,1)}, u32[]{:S(2)}, u32[]{:S(2)}) collective-permute-start(bf16[256,2048]{1,0:T(8,128)(2,1)} %collective-permute-done.41.refs_0_.refs_8_), channel_id=1, source_target_pairs={{0,16},{16,0},{1,17},{17,1},{2,18},{18,2},{3,19},{19,3},{4,20},{20... | collective-permute-start | bytes 3145736 | tf_op jit(solution)/shard_map/ppermute | solution.py:83
  378.0 45.1 %collective-permute-start.61 = (bf16[256,2048]{1,0:T(8,128)(2,1)S(1)}, bf16[256,2048]{1,0:T(8,128)(2,1)}, u32[]{:S(2)}, u32[]{:S(2)}) collective-permute-start(bf16[256,2048]{1,0:T(8,128)(2,1)S(1)} %copy-done.35), channel_id=1, source_target_pairs={{0,16},{16,0},{1,17},{17,1},{2,18},{18,2},{3,19},{19,3},{4,20},{20... | collective-permute-start | bytes 3145736 | tf_op jit(solution)/shard_map/ppermute | solution.py:83
  380.6 43.0 %collective-permute-start.64 = (bf16[256,2048]{1,0:T(8,128)(2,1)}, bf16[256,2048]{1,0:T(8,128)(2,1)S(1)}, u32[]{:S(2)}, u32[]{:S(2)}) collective-permute-start(bf16[256,2048]{1,0:T(8,128)(2,1)} %add_convert_fusion.3), channel_id=1, source_target_pairs={{0,4},{1,5},{2,6},{3,7},{4,8},{5,9},{6,10},{7,11},{8,12},{9,13},{1... | collective-permute-start | bytes 3145736 | tf_op jit(solution)/shard_map/ppermute | solution.py:79
  422.5 80.2 %collective-permute-start.72 = (bf16[256,2048]{1,0:T(8,128)(2,1)}, bf16[256,2048]{1,0:T(8,128)(2,1)}, u32[]{:S(2)}, u32[]{:S(2)}) collective-permute-start(bf16[256,2048]{1,0:T(8,128)(2,1)} %collective-permute-done.44.refs_2_.refs_6_), channel_id=1, source_target_pairs={{0,1},{1,0},{2,3},{3,2},{4,5},{5,4},{6,7},{7,6},{8,9},{9,8},{10,11... | collective-permute-start | bytes 3145736 | tf_op jit(solution)/shard_map/ppermute | solution.py:79
  423.1 79.6 %collective-permute-start.71 = (bf16[256,2048]{1,0:T(8,128)(2,1)}, bf16[256,2048]{1,0:T(8,128)(2,1)}, u32[]{:S(2)}, u32[]{:S(2)}) collective-permute-start(bf16[256,2048]{1,0:T(8,128)(2,1)} %collective-permute-done.48.refs_0_.refs_6_), channel_id=1, source_target_pairs={{0,1},{1,0},{2,3},{3,2},{4,5},{5,4},{6,7},{7,6},{8,9},{9,8},{10,11... | collective-permute-start | bytes 3145736 | tf_op jit(solution)/shard_map/ppermute | solution.py:79
  454.6 33.8 %collective-permute-start.70 = (bf16[352,2048]{1,0:T(8,128)(2,1)}, bf16[352,2048]{1,0:T(8,128)(2,1)}, u32[]{:S(2)}, u32[]{:S(2)}) collective-permute-start(bf16[352,2048]{1,0:T(8,128)(2,1)} %get-tuple-element.945), channel_id=1, source_target_pairs={{0,16},{16,0},{1,17},{17,1},{2,18},{18,2},{3,19},{19,3},{4,20},{20... | collective-permute-start | bytes 4325384 | tf_op jit(solution)/shard_map/ppermute | solution.py:83
  528.9 44.3 %collective-permute-start.81 = (bf16[256,2048]{1,0:T(8,128)(2,1)}, bf16[256,2048]{1,0:T(8,128)(2,1)}, u32[]{:S(2)}, u32[]{:S(2)}) collective-permute-start(bf16[256,2048]{1,0:T(8,128)(2,1)} %collective-permute-done.61.refs_2_.refs_10_), channel_id=1, source_target_pairs={{0,1},{1,0},{2,3},{3,2},{4,5},{5,4},{6,7},{7,6},{8,9},{9,8},{10,11... | collective-permute-start | bytes 3145736 | tf_op jit(solution)/shard_map/ppermute | solution.py:79
  530.4 43.2 %collective-permute-start.80 = (bf16[256,2048]{1,0:T(8,128)(2,1)}, bf16[256,2048]{1,0:T(8,128)(2,1)}, u32[]{:S(2)}, u32[]{:S(2)}) collective-permute-start(bf16[256,2048]{1,0:T(8,128)(2,1)} %collective-permute-done.65.refs_0_.refs_10_), channel_id=1, source_target_pairs={{0,1},{1,0},{2,3},{3,2},{4,5},{5,4},{6,7},{7,6},{8,9},{9,8},{10,11... | collective-permute-start | bytes 3145736 | tf_op jit(solution)/shard_map/ppermute | solution.py:79
  566.2 32.8 %collective-permute-start.82 = (bf16[256,2048]{1,0:T(8,128)(2,1)}, bf16[256,2048]{1,0:T(8,128)(2,1)}, u32[]{:S(2)}, u32[]{:S(2)}) collective-permute-start(bf16[256,2048]{1,0:T(8,128)(2,1)} %fusion.3), channel_id=1, source_target_pairs={{0,4},{1,5},{2,6},{3,7},{4,8},{5,9},{6,10},{7,11},{8,12},{9,13},{1... | collective-permute-start | bytes 3145736 | tf_op jit(solution)/shard_map/ppermute | solution.py:79
  573.1 52.8 %collective-permute-start.86 = (bf16[352,2048]{1,0:T(8,128)(2,1)}, bf16[352,2048]{1,0:T(8,128)(2,1)}, u32[]{:S(2)}, u32[]{:S(2)}) collective-permute-start(bf16[352,2048]{1,0:T(8,128)(2,1)} %get-tuple-element.947), channel_id=1, source_target_pairs={{0,16},{16,0},{1,17},{17,1},{2,18},{18,2},{3,19},{19,3},{4,20},{20... | collective-permute-start | bytes 4325384 | tf_op jit(solution)/shard_map/ppermute | solution.py:83
  626.3 50.0 %collective-permute-start.93 = (bf16[64,2048]{1,0:T(8,128)(2,1)S(1)}, bf16[64,2048]{1,0:T(8,128)(2,1)S(1)}, u32[]{:S(2)}, u32[]{:S(2)}) collective-permute-start(bf16[64,2048]{1,0:T(8,128)(2,1)S(1)} %get-tuple-element.958), channel_id=1, source_target_pairs={{0,4},{1,5},{2,6},{3,7},{4,8},{5,9},{6,10},{7,11},{8,12},{9,13},{1... | collective-permute-start | bytes 786440 | tf_op jit(solution)/shard_map/ppermute | solution.py:79
  626.6 50.6 %collective-permute-start.96 = (bf16[352,2048]{1,0:T(8,128)(2,1)}, bf16[352,2048]{1,0:T(8,128)(2,1)}, u32[]{:S(2)}, u32[]{:S(2)}) collective-permute-start(bf16[352,2048]{1,0:T(8,128)(2,1)} %get-tuple-element.949), channel_id=1, source_target_pairs={{0,16},{16,0},{1,17},{17,1},{2,18},{18,2},{3,19},{19,3},{4,20},{20... | collective-permute-start | bytes 4325384 | tf_op jit(solution)/shard_map/ppermute | solution.py:83
  (154 other events, 2158.6 us)

commit v5 on v4

--- a/solution.py
+++ b/solution.py
@@ -447,7 +447,8 @@
         ]
         for part, (low, high) in enumerate(parts)
     ]
-    for copy in loads[0] + weights[0] + loads[1]:
+    arrivals = (loads[0] + weights[0][:1], weights[0][1:2], loads[1] + weights[0][2:])
+    for copy in arrivals[0] + arrivals[1] + arrivals[2]:
         copy.start()
 
     @pl.when(expert[1] == 1)
@@ -469,8 +470,15 @@
 
     def work(part, scale):
         low, high = parts[part]
+        waits = arrivals if part == 0 else ((), (), ())
+        for copy in waits[0]:
+            copy.wait()
         gate = dot(rows[...], into[low:high, :], ((1,), (1,)))
+        for copy in waits[1]:
+            copy.wait()
         up = dot(rows[...], into[units + low : units + high, :], ((1,), (1,)))
+        for copy in waits[2]:
+            copy.wait()
         back = dot(grads[...], down[low:high, :], ((1,), (1,)))
         gate_sigmoid = jax.nn.sigmoid(gate)
         silu = gate * gate_sigmoid
@@ -491,8 +499,6 @@
             copy.start()
         return inner, copies
 
-    for copy in loads[0] + weights[0] + loads[1]:
-        copy.wait()
     _, stores = work(0, routed_scale)
 
     @pl.when(expert[1] == 1)

time: 692 us -> 694 us (level)
  transfers between devices with their start and end apart: 101 -> 101, of which waited for: 35 -> 33; matrix products, arithmetic and copies ran while one was open for 18% -> 18% of each run, Pallas kernels for 43% -> 43%
where the time goes in v5:
time: 694 us; the launch traced here: 684 us
  Pallas kernels  293 us (42%)
  waiting for transfers between devices  149 us (21%)
  starting transfers between devices  98.6 us (14%)
  other arithmetic  68.9 us (10%)
  local copies, waits for them, and re-layouts  44 us (6%)
  matrix products  26 us (4%)
    pallas_call x8, Pallas kernels, experts(): pl.pallas_call(functools.partial(experts_kernel, pieces, routed + -routed...  164 us
    ppermute x77, waiting for transfers between devices, hop(): return lax.ppermute(values, 'ep', pairs)  122 us
    pallas_call x6, Pallas kernels, weight_grad(): pl.pallas_call(functools.partial(weight_grad_kernel, unit_counts, row_cou...  80.5 us
    ppermute x77, starting transfers between devices, hop(): return lax.ppermute(values, 'ep', pairs)  56.3 us
    dot_general x8, matrix products, dot(): lax.dot_general(left, right, (dims, ((), ())), preferred_element_type=f32)  26 us
    ppermute x20, starting transfers between devices, cross(): return lax.ppermute(values, 'dp', pairs)  23.8 us
    pallas_call x3, Pallas kernels, pack(): pl.pallas_call(functools.partial(pack_kernel, len(pieces), moves, blanks)...  19.2 us
    all_to_all x4, starting transfers between devices, swap(): lax.all_to_all(blocks, 'ep', split_axis=0, concat_axis=0, tiled=True, axi...  18.5 us
  transfers between devices with their start and end apart: 101, of which 33 were waited for; matrix products, arithmetic and copies ran while one was open for 18% of the time, Pallas kernels for 43%

profile of v5, /device:TPU:0, one launch (start us, length us, event | category | flops | bytes accessed | tf_op | source)
XLA Modules:
  0.0 683.7 jit_solution(12078088984215240043)
XLA Ops:
  13.5 10.0 %collective-permute-done = bf16[64,2048]{1,0:T(8,128)(2,1)S(1)} collective-permute-done((bf16[64,2048]{1,0:T(8,128)(2,1)}, bf16[64,2048]{1,0:T(8,128)(2,1)S(1)}, u32[]{:S(2)}, u32[]{:S(2)}) %collective-permute-start) | collective-permute-done | bytes 262176 | tf_op jit(solution)/shard_map/ppermute | solution.py:79
  39.6 17.8 %collective-permute-done.3 = bf16[64,2048]{1,0:T(8,128)(2,1)S(1)} collective-permute-done((bf16[64,2048]{1,0:T(8,128)(2,1)S(1)}, bf16[64,2048]{1,0:T(8,128)(2,1)S(1)}, u32[]{:S(2)}, u32[]{:S(2)}) %collective-permute-start.3) | collective-permute-done | bytes 262176 | tf_op jit(solution)/shard_map/ppermute | solution.py:79
  72.7 10.5 %collective-permute-done.7 = bf16[64,2048]{1,0:T(8,128)(2,1)S(1)} collective-permute-done((bf16[64,2048]{1,0:T(8,128)(2,1)S(1)}, bf16[64,2048]{1,0:T(8,128)(2,1)S(1)}, u32[]{:S(2)}, u32[]{:S(2)}) %collective-permute-start.7) | collective-permute-done | bytes 262176 | tf_op jit(solution)/shard_map/ppermute | solution.py:79
  113.6 10.0 %shard_map.274 = (bf16[1024,2048]{1,0:T(8,128)(2,1)}, bf16[2048,768]{1,0:T(8,128)(2,1)}, f32[1024,768]{1,0:T(8,128)}) custom-call(s32[32]{0:T(128)} %stack.733.order, f32[1,2048]{1,0:T(1,128)} %bitcast.397, bf16[128,2048]{1,0:T(8,128)(2,1)} %refs_0_, bf16[128,2048]{1,0:T(8,128)(2,1)} %copy-done.71, bf16[128,2048]{1,0:T(8,128)(2,1)} %copy-done.70, ...), custom_call_target="tpu_custom_call" | custom-call | flops 11274289152 | bytes 17825792 | tf_op jit(solution)/shard_map/pallas_call | solution.py:386
  123.6 8.7 %shard_map.275 = (bf16[1024,768]{1,0:T(8,128)(2,1)}, bf16[1024,256]{1,0:T(8,128)(2,1)}) custom-call(s32[10]{0:T(128)} %pad_add_fusion.here, f32[1024,768]{1,0:T(8,128)} %get-tuple-element.534.raw, f32[1,768]{1,0:T(1,128)} %broadcast_in_dim.112.bias, f32[128,128]{1,0:T(8,128)} %get-tuple-element.977.cosine, f32[128,128]{1,0:T(8,128)} %get-tuple-element.976.signed_sine), custom_call_target="tpu_custom_call" | custom-call | flops 10066329600 | bytes 5242880 | tf_op jit(solution)/shard_map/pallas_call | solution.py:233
  170.3 9.0 %collective-permute-done.34 = bf16[128,2048]{1,0:T(8,128)(2,1)S(1)} collective-permute-done((bf16[128,2048]{1,0:T(8,128)(2,1)S(1)}, bf16[128,2048]{1,0:T(8,128)(2,1)S(1)}, u32[]{:S(2)}, u32[]{:S(2)}) %collective-permute-start.34) | collective-permute-done | bytes 524320 | tf_op jit(solution)/shard_map/ppermute | solution.py:79
  186.5 9.9 %collective-permute-done.30 = bf16[128,2048]{1,0:T(8,128)(2,1)S(1)} collective-permute-done((bf16[128,2048]{1,0:T(8,128)(2,1)S(1)}, bf16[128,2048]{1,0:T(8,128)(2,1)S(1)}, u32[]{:S(2)}, u32[]{:S(2)}) %collective-permute-start.30) | collective-permute-done | bytes 524320 | tf_op jit(solution)/shard_map/ppermute | solution.py:79
  199.4 27.1 %shard_map.277 = (bf16[512,1152]{1,0:T(8,128)(2,1)}, bf16[512,1152]{1,0:T(8,128)(2,1)}, bf16[512,1152]{1,0:T(8,128)(2,1)}, bf16[256,2048]{1,0:T(8,128)(2,1)}, bf...) custom-call(s32[2]{0:T(128)} %pad_add_fusion.1.expert, ...), custom_call_target="tpu_custom_call" | custom-call | flops 28991029248 | bytes 22544384 | tf_op jit(solution)/shard_map/pallas_call | solution.py:564
  237.7 26.7 %shard_map.278 = (bf16[512,1152]{1,0:T(8,128)(2,1)}, bf16[512,1152]{1,0:T(8,128)(2,1)}, bf16[512,1152]{1,0:T(8,128)(2,1)}, bf16[256,2048]{1,0:T(8,128)(2,1)}, bf...) custom-call(s32[2]{0:T(128)} %pad_add_fusion.1.expert, ...), custom_call_target="tpu_custom_call" | custom-call | flops 28991029248 | bytes 22544384 | tf_op jit(solution)/shard_map/pallas_call | solution.py:564
  275.8 26.8 %shard_map.279 = (bf16[512,1152]{1,0:T(8,128)(2,1)}, bf16[512,1152]{1,0:T(8,128)(2,1)}, bf16[512,1152]{1,0:T(8,128)(2,1)}, bf16[256,2048]{1,0:T(8,128)(2,1)}, bf...) custom-call(s32[2]{0:T(128)} %pad_add_fusion.1.expert, ...), custom_call_target="tpu_custom_call" | custom-call | flops 28991029248 | bytes 22544384 | tf_op jit(solution)/shard_map/pallas_call | solution.py:564
  314.7 26.8 %shard_map.280 = (bf16[512,1152]{1,0:T(8,128)(2,1)}, bf16[512,1152]{1,0:T(8,128)(2,1)}, bf16[512,1152]{1,0:T(8,128)(2,1)}, bf16[256,2048]{1,0:T(8,128)(2,1)}, bf...) custom-call(s32[2]{0:T(128)} %pad_add_fusion.1.expert, ...), custom_call_target="tpu_custom_call" | custom-call | flops 28991029248 | bytes 22544384 | tf_op jit(solution)/shard_map/pallas_call | solution.py:564
  352.0 13.8 %shard_map.281 = (f32[704,2048]{1,0:T(8,128)}, bf16[352,2048]{1,0:T(8,128)(2,1)}) custom-call(bf16[512,1152]{1,0:T(8,128)(2,1)} %get-tuple-element.664.refs_0_, bf16[512,1152]{1,0:T(8,128)(2,1)} %get-tuple-element.665.refs_1_, bf16[512,1152]{1,0:T(8,128)(2,1)} %get-tuple-element.666.refs_2_, bf16[512,1152]{1,0:T(8,128)(2,1)} %get-tuple-element.667.refs_3_, ...), custom_call_target="tpu_custom_call" | custom-call | flops 17716740096 | bytes 21757952 | tf_op jit(solution)/shard_map/pallas_call | solution.py:641
  365.8 10.0 %collective-permute-done.59 = bf16[256,2048]{1,0:T(8,128)(2,1)S(1)} collective-permute-done((bf16[256,2048]{1,0:T(8,128)(2,1)S(1)}, bf16[256,2048]{1,0:T(8,128)(2,1)S(1)}, u32[]{:S(2)}, u32[]{:S(2)}) %collective-permute-start.59) | collective-permute-done | bytes 1048608 | tf_op jit(solution)/shard_map/ppermute | solution.py:79
  382.5 13.8 %shard_map.282 = (f32[704,2048]{1,0:T(8,128)}, bf16[352,2048]{1,0:T(8,128)(2,1)}) custom-call(bf16[512,1152]{1,0:T(8,128)(2,1)} %get-tuple-element.730.refs_0_, bf16[512,1152]{1,0:T(8,128)(2,1)} %get-tuple-element.731.refs_1_, bf16[512,1152]{1,0:T(8,128)(2,1)} %get-tuple-element.732.refs_2_, bf16[512,1152]{1,0:T(8,128)(2,1)} %get-tuple-element.733.refs_3_, ...), custom_call_target="tpu_custom_call" | custom-call | flops 17716740096 | bytes 21757952 | tf_op jit(solution)/shard_map/pallas_call | solution.py:641
  397.9 13.8 %shard_map.283 = (f32[704,2048]{1,0:T(8,128)}, bf16[352,2048]{1,0:T(8,128)(2,1)}) custom-call(bf16[512,1152]{1,0:T(8,128)(2,1)} %get-tuple-element.718.refs_0_, bf16[512,1152]{1,0:T(8,128)(2,1)} %get-tuple-element.719.refs_1_, bf16[512,1152]{1,0:T(8,128)(2,1)} %get-tuple-element.720.refs_2_, bf16[512,1152]{1,0:T(8,128)(2,1)} %get-tuple-element.721.refs_3_, ...), custom_call_target="tpu_custom_call" | custom-call | flops 17716740096 | bytes 21757952 | tf_op jit(solution)/shard_map/pallas_call | solution.py:641
  411.7 10.4 %collective-permute-done.63 = bf16[256,2048]{1,0:T(8,128)(2,1)S(1)} collective-permute-done((bf16[256,2048]{1,0:T(8,128)(2,1)S(1)}, bf16[256,2048]{1,0:T(8,128)(2,1)S(1)}, u32[]{:S(2)}, u32[]{:S(2)}) %collective-permute-start.63) | collective-permute-done | bytes 1048608 | tf_op jit(solution)/shard_map/ppermute | solution.py:79
  434.7 14.0 %shard_map.284 = (bf16[512,1152]{1,0:T(8,128)(2,1)}, bf16[512,1152]{1,0:T(8,128)(2,1)}, bf16[512,1152]{1,0:T(8,128)(2,1)}, bf16[256,2048]{1,0:T(8,128)(2,1)}, bf...) custom-call(s32[2]{0:T(128)} %pad_add_fusion.2.expert, ...), custom_call_target="tpu_custom_call" | custom-call | flops 14495514624 | bytes 22544384 | tf_op jit(solution)/shard_map/pallas_call | solution.py:564
  454.7 10.8 %shard_map.285 = (bf16[1024,768]{1,0:T(8,128)(2,1)}, f32[1,768]{1,0:T(1,128)}) custom-call(s32[10]{0:T(128)} %pad_add_fusion.here, bf16[1024,768]{1,0:T(8,128)(2,1)} %get-tuple-element.775.low, bf16[1024,256]{1,0:T(8,128)(2,1)} %bitcast.390, f32[128,128]{1,0:T(8,128)} %get-tuple-element.977.cosine, f32[128,128]{1,0:T(8,128)} %get-tuple-element.975.sine, ...), custom_call_target="tpu_custom_call" | custom-call | flops 12415139840 | bytes 3670016 | tf_op jit(solution)/shard_map/pallas_call | solution.py:264
  503.2 14.2 %shard_map.286 = (bf16[512,1152]{1,0:T(8,128)(2,1)}, bf16[512,1152]{1,0:T(8,128)(2,1)}, bf16[512,1152]{1,0:T(8,128)(2,1)}, bf16[256,2048]{1,0:T(8,128)(2,1)}, bf...) custom-call(s32[2]{0:T(128)} %pad_add_fusion.2.expert, ...), custom_call_target="tpu_custom_call" | custom-call | flops 14495514624 | bytes 22544384 | tf_op jit(solution)/shard_map/pallas_call | solution.py:564
  539.9 14.3 %shard_map.287 = (bf16[512,1152]{1,0:T(8,128)(2,1)}, bf16[512,1152]{1,0:T(8,128)(2,1)}, bf16[512,1152]{1,0:T(8,128)(2,1)}, bf16[256,2048]{1,0:T(8,128)(2,1)}, bf...) custom-call(s32[2]{0:T(128)} %pad_add_fusion.2.expert, ...), custom_call_target="tpu_custom_call" | custom-call | flops 14495514624 | bytes 22544384 | tf_op jit(solution)/shard_map/pallas_call | solution.py:564
  575.7 14.2 %shard_map.288 = (bf16[512,1152]{1,0:T(8,128)(2,1)}, bf16[512,1152]{1,0:T(8,128)(2,1)}, bf16[512,1152]{1,0:T(8,128)(2,1)}, bf16[256,2048]{1,0:T(8,128)(2,1)}, bf...) custom-call(s32[2]{0:T(128)} %pad_add_fusion.2.expert, ...), custom_call_target="tpu_custom_call" | custom-call | flops 14495514624 | bytes 22544384 | tf_op jit(solution)/shard_map/pallas_call | solution.py:564
  609.3 12.9 %shard_map.289 = f32[704,2048]{1,0:T(8,128)} custom-call(bf16[512,1152]{1,0:T(8,128)(2,1)} %get-tuple-element.878.refs_0_, bf16[512,1152]{1,0:T(8,128)(2,1)} %get-tuple-element.885.refs_1_, bf16[512,1152]{1,0:T(8,128)(2,1)} %get-tuple-element.892.refs_2_, bf16[512,1152]{1,0:T(8,128)(2,1)} %get-tuple-element.899.refs_3_, ...), custom_call_target="tpu_custom_call", output_to_operand_aliasing={{}: (12, {})} | custom-call | flops 11811160064 | bytes 23068672 | tf_op jit(solution)/shard_map/pallas_call | solution.py:641
  633.1 12.8 %shard_map.290 = f32[704,2048]{1,0:T(8,128)} custom-call(bf16[512,1152]{1,0:T(8,128)(2,1)} %get-tuple-element.919.refs_0_, bf16[512,1152]{1,0:T(8,128)(2,1)} %get-tuple-element.920.refs_1_, bf16[512,1152]{1,0:T(8,128)(2,1)} %get-tuple-element.921.refs_2_, bf16[512,1152]{1,0:T(8,128)(2,1)} %get-tuple-element.922.refs_3_, ...), custom_call_target="tpu_custom_call", output_to_operand_aliasing={{}: (12, {})} | custom-call | flops 11811160064 | bytes 23068672 | tf_op jit(solution)/shard_map/pallas_call | solution.py:641
  646.0 13.4 %shard_map.291 = f32[704,2048]{1,0:T(8,128)} custom-call(bf16[512,1152]{1,0:T(8,128)(2,1)} %get-tuple-element.932.refs_0_, bf16[512,1152]{1,0:T(8,128)(2,1)} %get-tuple-element.933.refs_1_, bf16[512,1152]{1,0:T(8,128)(2,1)} %get-tuple-element.934.refs_2_, bf16[512,1152]{1,0:T(8,128)(2,1)} %get-tuple-element.935.refs_3_, ...), custom_call_target="tpu_custom_call", output_to_operand_aliasing={{}: (12, {})} | custom-call | flops 11811160064 | bytes 23068672 | tf_op jit(solution)/shard_map/pallas_call | solution.py:641
  (502 shorter events, 328.4 us)
Async XLA Ops:
  23.5 39.7 %all-to-all-start = ((bf16[8,80,768]{2,1,0:T(8,128)(2,1)}), bf16[8,80,768]{2,1,0:T(8,128)(2,1)}, u32[]{:S(2)}, u32[]{:S(2)}) async-start(bf16[8,80,768]{2,1,0:T(8,128)(2,1)} %pad_maximum_fusion.5), calls=%async_computation | async-start | bytes 1966080 | tf_op jit(solution)/shard_map/all_to_all | solution.py:101
  184.7 41.8 %collective-permute-start.38 = (bf16[256,2048]{1,0:T(8,128)(2,1)}, bf16[256,2048]{1,0:T(8,128)(2,1)S(1)}, u32[]{:S(2)}, u32[]{:S(2)}) collective-permute-start(bf16[256,2048]{1,0:T(8,128)(2,1)} %constant_dynamic-update-slice_fusion.refs_2_.refs_4_), channel_id=1, source_target_pairs={{0,16},{16,0},{1,17},{17,1},{2,18},{18,2},{3,19},{19,3},{4,20},{20... | collective-permute-start | bytes 3145736 | tf_op jit(solution)/shard_map/ppermute | solution.py:83
  197.5 35.1 %collective-permute-start.35 = (bf16[256,2048]{1,0:T(8,128)(2,1)S(1)}, bf16[256,2048]{1,0:T(8,128)(2,1)}, u32[]{:S(2)}, u32[]{:S(2)}) collective-permute-start(bf16[256,2048]{1,0:T(8,128)(2,1)S(1)} %pad_maximum_fusion.3.refs_0_.refs_4_), channel_id=1, source_target_pairs={{0,4},{1,5},{2,6},{3,7},{4,8},{5,9},{6,10},{7,11},{8,12},{9,13},{1... | collective-permute-start | bytes 3145736 | tf_op jit(solution)/shard_map/ppermute | solution.py:79
  197.6 35.0 %collective-permute-start.39 = (bf16[256,2048]{1,0:T(8,128)(2,1)S(1)}, bf16[256,2048]{1,0:T(8,128)(2,1)S(1)}, u32[]{:S(2)}, u32[]{:S(2)}) collective-permute-start(bf16[256,2048]{1,0:T(8,128)(2,1)S(1)} %pad_maximum_fusion.3.refs_0_.refs_4_), channel_id=1, source_target_pairs={{0,16},{16,0},{1,17},{17,1},{2,18},{18,2},{3,19},{19,3},{4,20},{20... | collective-permute-start | bytes 3145736 | tf_op jit(solution)/shard_map/ppermute | solution.py:83
  233.1 32.6 %collective-permute-start.41 = (bf16[256,2048]{1,0:T(8,128)(2,1)}, bf16[256,2048]{1,0:T(8,128)(2,1)}, u32[]{:S(2)}, u32[]{:S(2)}) collective-permute-start(bf16[256,2048]{1,0:T(8,128)(2,1)} %collective-permute-done.35.refs_0_.refs_6_), channel_id=1, source_target_pairs={{0,4},{1,5},{2,6},{3,7},{4,8},{5,9},{6,10},{7,11},{8,12},{9,13},{1... | collective-permute-start | bytes 3145736 | tf_op jit(solution)/shard_map/ppermute | solution.py:79
  267.2 38.3 %collective-permute-start.45 = (bf16[256,2048]{1,0:T(8,128)(2,1)}, bf16[256,2048]{1,0:T(8,128)(2,1)}, u32[]{:S(2)}, u32[]{:S(2)}) collective-permute-start(bf16[256,2048]{1,0:T(8,128)(2,1)} %collective-permute-done.41.refs_0_.refs_8_), channel_id=1, source_target_pairs={{0,4},{1,5},{2,6},{3,7},{4,8},{5,9},{6,10},{7,11},{8,12},{9,13},{1... | collective-permute-start | bytes 3145736 | tf_op jit(solution)/shard_map/ppermute | solution.py:79
  268.0 37.5 %collective-permute-start.48 = (bf16[256,2048]{1,0:T(8,128)(2,1)}, bf16[256,2048]{1,0:T(8,128)(2,1)}, u32[]{:S(2)}, u32[]{:S(2)}) collective-permute-start(bf16[256,2048]{1,0:T(8,128)(2,1)} %collective-permute-done.35.refs_0_.refs_6_), channel_id=1, source_target_pairs={{0,16},{16,0},{1,17},{17,1},{2,18},{18,2},{3,19},{19,3},{4,20},{20... | collective-permute-start | bytes 3145736 | tf_op jit(solution)/shard_map/ppermute | solution.py:83
  306.1 35.9 %collective-permute-start.53 = (bf16[256,2048]{1,0:T(8,128)(2,1)}, bf16[256,2048]{1,0:T(8,128)(2,1)}, u32[]{:S(2)}, u32[]{:S(2)}) collective-permute-start(bf16[256,2048]{1,0:T(8,128)(2,1)} %pad_maximum_fusion.1.refs_2_.refs_8_), channel_id=1, source_target_pairs={{0,16},{16,0},{1,17},{17,1},{2,18},{18,2},{3,19},{19,3},{4,20},{20... | collective-permute-start | bytes 3145736 | tf_op jit(solution)/shard_map/ppermute | solution.py:83
  308.0 34.0 %collective-permute-start.56 = (bf16[256,2048]{1,0:T(8,128)(2,1)}, bf16[256,2048]{1,0:T(8,128)(2,1)}, u32[]{:S(2)}, u32[]{:S(2)}) collective-permute-start(bf16[256,2048]{1,0:T(8,128)(2,1)} %convert_add_fusion.10), channel_id=1, source_target_pairs={{0,4},{1,5},{2,6},{3,7},{4,8},{5,9},{6,10},{7,11},{8,12},{9,13},{1... | collective-permute-start | bytes 3145736 | tf_op jit(solution)/shard_map/ppermute | solution.py:79
  344.1 90.5 %collective-permute-start.66 = (bf16[256,2048]{1,0:T(8,128)(2,1)}, bf16[256,2048]{1,0:T(8,128)(2,1)}, u32[]{:S(2)}, u32[]{:S(2)}) collective-permute-start(bf16[256,2048]{1,0:T(8,128)(2,1)} %copy-done.63), channel_id=1, source_target_pairs={{0,1},{1,0},{2,3},{3,2},{4,5},{5,4},{6,7},{7,6},{8,9},{9,8},{10,11... | collective-permute-start | bytes 3145736 | tf_op jit(solution)/shard_map/ppermute | solution.py:79
  344.4 90.2 %collective-permute-start.67 = (bf16[256,2048]{1,0:T(8,128)(2,1)}, bf16[256,2048]{1,0:T(8,128)(2,1)}, u32[]{:S(2)}, u32[]{:S(2)}) collective-permute-start(bf16[256,2048]{1,0:T(8,128)(2,1)} %copy-done.62), channel_id=1, source_target_pairs={{0,1},{1,0},{2,3},{3,2},{4,5},{5,4},{6,7},{7,6},{8,9},{9,8},{10,11... | collective-permute-start | bytes 3145736 | tf_op jit(solution)/shard_map/ppermute | solution.py:79
  344.6 33.0 %collective-permute-start.57 = (bf16[256,2048]{1,0:T(8,128)(2,1)}, bf16[256,2048]{1,0:T(8,128)(2,1)}, u32[]{:S(2)}, u32[]{:S(2)}) collective-permute-start(bf16[256,2048]{1,0:T(8,128)(2,1)} %collective-permute-done.41.refs_0_.refs_8_), channel_id=1, source_target_pairs={{0,16},{16,0},{1,17},{17,1},{2,18},{18,2},{3,19},{19,3},{4,20},{20... | collective-permute-start | bytes 3145736 | tf_op jit(solution)/shard_map/ppermute | solution.py:83
  377.6 45.1 %collective-permute-start.61 = (bf16[256,2048]{1,0:T(8,128)(2,1)S(1)}, bf16[256,2048]{1,0:T(8,128)(2,1)}, u32[]{:S(2)}, u32[]{:S(2)}) collective-permute-start(bf16[256,2048]{1,0:T(8,128)(2,1)S(1)} %copy-done.35), channel_id=1, source_target_pairs={{0,16},{16,0},{1,17},{17,1},{2,18},{18,2},{3,19},{19,3},{4,20},{20... | collective-permute-start | bytes 3145736 | tf_op jit(solution)/shard_map/ppermute | solution.py:83
  380.3 43.0 %collective-permute-start.64 = (bf16[256,2048]{1,0:T(8,128)(2,1)}, bf16[256,2048]{1,0:T(8,128)(2,1)S(1)}, u32[]{:S(2)}, u32[]{:S(2)}) collective-permute-start(bf16[256,2048]{1,0:T(8,128)(2,1)} %add_convert_fusion.3), channel_id=1, source_target_pairs={{0,4},{1,5},{2,6},{3,7},{4,8},{5,9},{6,10},{7,11},{8,12},{9,13},{1... | collective-permute-start | bytes 3145736 | tf_op jit(solution)/shard_map/ppermute | solution.py:79
  422.1 81.1 %collective-permute-start.72 = (bf16[256,2048]{1,0:T(8,128)(2,1)}, bf16[256,2048]{1,0:T(8,128)(2,1)}, u32[]{:S(2)}, u32[]{:S(2)}) collective-permute-start(bf16[256,2048]{1,0:T(8,128)(2,1)} %collective-permute-done.44.refs_2_.refs_6_), channel_id=1, source_target_pairs={{0,1},{1,0},{2,3},{3,2},{4,5},{5,4},{6,7},{7,6},{8,9},{9,8},{10,11... | collective-permute-start | bytes 3145736 | tf_op jit(solution)/shard_map/ppermute | solution.py:79
  422.7 80.5 %collective-permute-start.71 = (bf16[256,2048]{1,0:T(8,128)(2,1)}, bf16[256,2048]{1,0:T(8,128)(2,1)}, u32[]{:S(2)}, u32[]{:S(2)}) collective-permute-start(bf16[256,2048]{1,0:T(8,128)(2,1)} %collective-permute-done.48.refs_0_.refs_6_), channel_id=1, source_target_pairs={{0,1},{1,0},{2,3},{3,2},{4,5},{5,4},{6,7},{7,6},{8,9},{9,8},{10,11... | collective-permute-start | bytes 3145736 | tf_op jit(solution)/shard_map/ppermute | solution.py:79
  454.2 33.8 %collective-permute-start.70 = (bf16[352,2048]{1,0:T(8,128)(2,1)}, bf16[352,2048]{1,0:T(8,128)(2,1)}, u32[]{:S(2)}, u32[]{:S(2)}) collective-permute-start(bf16[352,2048]{1,0:T(8,128)(2,1)} %get-tuple-element.945), channel_id=1, source_target_pairs={{0,16},{16,0},{1,17},{17,1},{2,18},{18,2},{3,19},{19,3},{4,20},{20... | collective-permute-start | bytes 4325384 | tf_op jit(solution)/shard_map/ppermute | solution.py:83
  499.2 33.2 %collective-permute-start.73 = (bf16[256,2048]{1,0:T(8,128)(2,1)}, bf16[256,2048]{1,0:T(8,128)(2,1)}, u32[]{:S(2)}, u32[]{:S(2)}) collective-permute-start(bf16[256,2048]{1,0:T(8,128)(2,1)} %slice.165), channel_id=1, source_target_pairs={{0,16},{16,0},{1,17},{17,1},{2,18},{18,2},{3,19},{19,3},{4,20},{20... | collective-permute-start | bytes 3145736 | tf_op jit(solution)/shard_map/ppermute | solution.py:83
  530.8 44.4 %collective-permute-start.81 = (bf16[256,2048]{1,0:T(8,128)(2,1)}, bf16[256,2048]{1,0:T(8,128)(2,1)}, u32[]{:S(2)}, u32[]{:S(2)}) collective-permute-start(bf16[256,2048]{1,0:T(8,128)(2,1)} %collective-permute-done.61.refs_2_.refs_10_), channel_id=1, source_target_pairs={{0,1},{1,0},{2,3},{3,2},{4,5},{5,4},{6,7},{7,6},{8,9},{9,8},{10,11... | collective-permute-start | bytes 3145736 | tf_op jit(solution)/shard_map/ppermute | solution.py:79
  532.3 43.4 %collective-permute-start.80 = (bf16[256,2048]{1,0:T(8,128)(2,1)}, bf16[256,2048]{1,0:T(8,128)(2,1)}, u32[]{:S(2)}, u32[]{:S(2)}) collective-permute-start(bf16[256,2048]{1,0:T(8,128)(2,1)} %collective-permute-done.65.refs_0_.refs_10_), channel_id=1, source_target_pairs={{0,1},{1,0},{2,3},{3,2},{4,5},{5,4},{6,7},{7,6},{8,9},{9,8},{10,11... | collective-permute-start | bytes 3145736 | tf_op jit(solution)/shard_map/ppermute | solution.py:79
  568.1 33.0 %collective-permute-start.82 = (bf16[256,2048]{1,0:T(8,128)(2,1)}, bf16[256,2048]{1,0:T(8,128)(2,1)}, u32[]{:S(2)}, u32[]{:S(2)}) collective-permute-start(bf16[256,2048]{1,0:T(8,128)(2,1)} %fusion.3), channel_id=1, source_target_pairs={{0,4},{1,5},{2,6},{3,7},{4,8},{5,9},{6,10},{7,11},{8,12},{9,13},{1... | collective-permute-start | bytes 3145736 | tf_op jit(solution)/shard_map/ppermute | solution.py:79
  575.2 52.8 %collective-permute-start.86 = (bf16[352,2048]{1,0:T(8,128)(2,1)}, bf16[352,2048]{1,0:T(8,128)(2,1)}, u32[]{:S(2)}, u32[]{:S(2)}) collective-permute-start(bf16[352,2048]{1,0:T(8,128)(2,1)} %get-tuple-element.947), channel_id=1, source_target_pairs={{0,16},{16,0},{1,17},{17,1},{2,18},{18,2},{3,19},{19,3},{4,20},{20... | collective-permute-start | bytes 4325384 | tf_op jit(solution)/shard_map/ppermute | solution.py:83
  628.4 50.0 %collective-permute-start.93 = (bf16[64,2048]{1,0:T(8,128)(2,1)S(1)}, bf16[64,2048]{1,0:T(8,128)(2,1)S(1)}, u32[]{:S(2)}, u32[]{:S(2)}) collective-permute-start(bf16[64,2048]{1,0:T(8,128)(2,1)S(1)} %get-tuple-element.958), channel_id=1, source_target_pairs={{0,4},{1,5},{2,6},{3,7},{4,8},{5,9},{6,10},{7,11},{8,12},{9,13},{1... | collective-permute-start | bytes 786440 | tf_op jit(solution)/shard_map/ppermute | solution.py:79
  628.7 50.6 %collective-permute-start.96 = (bf16[352,2048]{1,0:T(8,128)(2,1)}, bf16[352,2048]{1,0:T(8,128)(2,1)}, u32[]{:S(2)}, u32[]{:S(2)}) collective-permute-start(bf16[352,2048]{1,0:T(8,128)(2,1)} %get-tuple-element.949), channel_id=1, source_target_pairs={{0,16},{16,0},{1,17},{17,1},{2,18},{18,2},{3,19},{19,3},{4,20},{20... | collective-permute-start | bytes 4325384 | tf_op jit(solution)/shard_map/ppermute | solution.py:83
  (154 other events, 2166.3 us)
